TPU v7x, 32 devices: a whole 2x2x4 slice. The times are simulated.
32 devices in a mesh: seq: 8 (over z, y), head: 4 (over x, core).
Axes of the slice: x: 2, y: 2, z: 4, core: 2. Of those that a mesh axis runs over, the one named last changes fastest.
Arguments:
- tokens: bfloat16 [16384, 1024], P('seq', 'head'), may hold values from -6 to 6
- row_starts: int32 [4], replicated, may hold values from 0 to 16320, as said below
- attn_gain: bfloat16 [1, 1024], replicated, may hold values from 0.5 to 1.5
- query_weight: bfloat16 [1, 1024, 512], P(None, None, 'head'), may hold values from -0.1875 to 0.1875
- key_weight: bfloat16 [1, 1024, 512], P(None, None, 'head'), may hold values from -0.1875 to 0.1875
- value_weight: bfloat16 [1, 1024, 1024], P(None, None, 'head'), may hold values from -0.1875 to 0.1875
- gate_weight: bfloat16 [1, 1024, 1024], P(None, None, 'head'), may hold values from -0.1875 to 0.1875
- rank_down: bfloat16 [1, 1024, 16], replicated, may hold values from -0.1875 to 0.1875
- rank_up: bfloat16 [1, 16, 512], P(None, None, 'head'), may hold values from -1.5 to 1.5
- rank_bias: bfloat16 [1, 512], P(None, 'head'), may hold values from -1 to 11
- group_gain: bfloat16 [1, 256], replicated, may hold values from 0.5 to 1.5
- out_weight: bfloat16 [1, 1024, 1024], P(None, 'head'), may hold values from -0.1875 to 0.1875
- feed_gain: bfloat16 [1, 1024], replicated, may hold values from 0.5 to 1.5
- feed_gate: bfloat16 [1, 1024, 2816], P(None, None, 'head'), may hold values from -0.1875 to 0.1875
- feed_up: bfloat16 [1, 1024, 2816], P(None, None, 'head'), may hold values from -0.1875 to 0.1875
- feed_down: bfloat16 [1, 2816, 1024], P(None, 'head'), may hold values from -0.109375 to 0.109375
- cotangent: bfloat16 [16384, 1024], P('seq', 'head'), may hold values from -6 to 6
Outputs:
- layer_out: bfloat16 [16384, 1024], P('seq', 'head')
- grad_tokens: float32 [16384, 1024], P('seq', 'head')
- grad_attn_gain: float32 [1, 1024], P(None, 'head')
- grad_query: float32 [1, 1024, 512], P(None, None, 'head')
- grad_key: float32 [1, 1024, 512], P(None, None, 'head')
- grad_value: float32 [1, 1024, 1024], P(None, None, 'head')
- grad_gate: float32 [1, 1024, 1024], P(None, None, 'head')
- grad_rank_down: float32 [1, 1024, 16], replicated
- grad_rank_up: float32 [1, 16, 512], P(None, None, 'head')
- grad_rank_bias: float32 [1, 512], P(None, 'head')
- grad_group_gain: float32 [1, 256], replicated
- grad_out: float32 [1, 1024, 1024], P(None, 'head')
- grad_feed_gain: float32 [1, 1024], P(None, 'head')
- grad_feed_gate: float32 [1, 1024, 2816], P(None, None, 'head')
- grad_feed_up: float32 [1, 1024, 2816], P(None, None, 'head')
- grad_feed_down: float32 [1, 2816, 1024], P(None, 'head')
Inputs may be any that keep to these rules, and one draw needn't show every extreme that they name: `row_starts`: increasing multiples of 64; the first is 0, the second lies within the first 2048 tokens and the third within the last 2048.
All inputs are finite; a program needn't handle non-finite values.
Results may differ from a plain program's by a relative error of at most 0.03.
Values may be sent and summed in bfloat16 or wider, within the bound.
A program may use at most 192 MiB of HBM per device.

v0:
```python
import jax
import jax.numpy as jnp
from jax import lax
from jax.sharding import PartitionSpec as P

MODEL_WIDTH = 1024
HK = 128
HV = 256
SPAN = 64


EPS = 1e-06
GATE_NORM = 16.0
EXACT_MATH = lax.Precision.HIGHEST


def carried_in(x, axis, join, neutral, backward):
    count = lax.axis_size(axis)
    place = lax.axis_index(axis)
    ahead = count - 1 - place if backward else place
    gathered = jax.tree.map(
        lambda a, kind: lax.all_gather(a.astype(kind), axis), x, (jnp.bfloat16, jnp.bfloat16)
    )
    state = jax.tree.map(lambda a, e: jnp.zeros_like(a) + jnp.asarray(e, a.dtype), x, neutral)

    def one(step, state):
        source = count - 1 - step if backward else step
        return join(
            state,
            jax.tree.map(
                lambda a, own: lax.dynamic_index_in_dim(a, source, 0, False).astype(own.dtype),
                gathered,
                x,
            ),
        )

    return lax.fori_loop(0, ahead, one, state)


def as_sent(x):
    return jax.tree.map(lambda a: a.astype(jnp.bfloat16) if a.dtype == jnp.float32 else a, x)


def matmul(left, right):
    return jnp.dot(left, right, preferred_element_type=jnp.float32)


def rows_product(left, right):
    return lax.dot_general(
        left, right, (((0,), (0,)), ((), ())), preferred_element_type=jnp.float32
    )


def cols_product(left, right):
    return lax.dot_general(
        left, right, (((1,), (1,)), ((), ())), preferred_element_type=jnp.float32
    )


def exact_rows(left, right):
    return jnp.einsum(
        "tk,tj->kj", left, right, precision=EXACT_MATH, preferred_element_type=jnp.float32
    )


def exact_cols(left, right):
    return jnp.einsum(
        "tk,jk->tj", left, right, precision=EXACT_MATH, preferred_element_type=jnp.float32
    )


def chain_state(earlier, later):
    return (earlier[0] * later[0], later[1] + later[0][..., None] * earlier[1])


def gather_features(slice_value):
    return lax.all_gather(slice_value.astype(jnp.bfloat16), "head", axis=1, tiled=True)


def reduce_partial(partial_value):
    return lax.psum_scatter(
        partial_value.astype(jnp.bfloat16), "head", scatter_dimension=1, tiled=True
    ).astype(jnp.float32)


def gather_grads(slice_grad):
    return lax.all_gather(slice_grad.astype(jnp.bfloat16), "head", axis=1, tiled=True)


def normalize(collected_rows, gain):
    values = collected_rows.astype(jnp.float32)
    inverse_norm = lax.rsqrt(jnp.mean(values * values, axis=1, keepdims=True) + EPS)
    return ((values * inverse_norm * gain).astype(jnp.bfloat16), inverse_norm)


def norm_stat(grad_normed, collected_rows, inverse_norm, gain):
    return jnp.sum(
        grad_normed * gain * (collected_rows.astype(jnp.float32) * inverse_norm),
        axis=1,
        keepdims=True,
    )


def norm_back(gradient_portion, statistic_sum, collected_rows, inverse_norm, gain, feature_width):
    column_slot = lax.axis_index("head") * feature_width
    normalized_portion = (
        lax.dynamic_slice_in_dim(collected_rows, column_slot, feature_width, 1).astype(jnp.float32)
        * inverse_norm
    )
    gain_portion = lax.dynamic_slice_in_dim(gain, column_slot, feature_width, 0)
    gain_gradient = jnp.sum(gradient_portion * normalized_portion, axis=0)
    input_gradient = inverse_norm * (
        gain_portion * gradient_portion - normalized_portion * statistic_sum / MODEL_WIDTH
    )
    return (input_gradient, gain_gradient)


def core_forward(query_raw, key_raw, reduced_value, log_decay, resets, keep_before, causal):
    query_scale = HK ** (-0.5)
    cumul = jnp.cumsum(log_decay, axis=1)
    ending = cumul[:, -1]
    decayed_query = (query_raw * query_scale * jnp.exp(cumul - ending[:, None])).astype(
        jnp.bfloat16
    )
    decayed_key = (key_raw * jnp.exp(ending[:, None] - cumul)).astype(jnp.bfloat16)
    scores = jnp.einsum(
        "cthk,cshk->chts", decayed_query, decayed_key, preferred_element_type=jnp.float32
    )
    attn_weights = jnp.where(causal, scores, 0.0).astype(jnp.bfloat16)
    intra_out = jnp.einsum(
        "chts,cshv->cthv", attn_weights, reduced_value, preferred_element_type=jnp.float32
    )
    state_update = jnp.einsum(
        "cshk,cshv->chkv", decayed_key, reduced_value, preferred_element_type=jnp.float32
    )
    decay_end = jnp.exp(ending)

    def forward_step(carried, pieces):
        reset_now, decay_now, update_now = pieces
        state_in = (1.0 - reset_now) * carried
        return (decay_now[..., None] * state_in + update_now, state_in)

    final_local, states_local = lax.scan(
        forward_step,
        jnp.zeros(state_update.shape[1:], jnp.float32),
        (resets, decay_end, state_update),
    )
    device_decay = keep_before[-1] * jnp.exp(jnp.sum(ending, axis=0))
    incoming = carried_in(
        (device_decay, final_local),
        "seq",
        chain_state,
        (jnp.ones_like(device_decay), jnp.zeros_like(final_local)),
        False,
    )[1]
    prior_decay = keep_before[:, None, None] * jnp.exp(jnp.cumsum(ending, axis=0) - ending)
    states_in = states_local + prior_decay[..., None] * incoming[None]
    scaled_rows = decay_end[..., None] * states_in
    state_low = scaled_rows.astype(jnp.bfloat16)
    across_output = jnp.einsum(
        "cthk,chkv->cthv", decayed_query, state_low, preferred_element_type=jnp.float32
    )
    kept_core = (
        query_raw,
        key_raw,
        cumul,
        ending,
        decayed_query,
        decayed_key,
        attn_weights,
        reduced_value,
        decay_end,
        scaled_rows,
        state_low,
        device_decay,
    )
    return (intra_out + across_output, kept_core)


def core_backward(grad_core, kept_core, resets, keep_after, causal):
    (
        query_raw,
        key_raw,
        cumul,
        ending,
        decayed_query,
        decayed_key,
        attn_weights,
        reduced_value,
        decay_end,
        scaled_rows,
        state_low,
        device_decay,
    ) = kept_core
    query_scale = HK ** (-0.5)
    grad_attn = jnp.einsum(
        "cthv,cshv->chts", grad_core, reduced_value, preferred_element_type=jnp.float32
    )
    grad_scores = jnp.where(causal, grad_attn, 0.0).astype(jnp.bfloat16)
    grad_value = jnp.einsum(
        "chts,cthv->cshv", attn_weights, grad_core, preferred_element_type=jnp.float32
    )
    grad_state_low = jnp.einsum(
        "cthk,cthv->chkv", decayed_query, grad_core, preferred_element_type=jnp.float32
    )
    grad_query_dec = jnp.einsum(
        "chts,cshk->cthk", grad_scores, decayed_key, preferred_element_type=jnp.float32
    )
    grad_query_dec = grad_query_dec + jnp.einsum(
        "cthv,chkv->cthk", grad_core, state_low, preferred_element_type=jnp.float32
    )
    grad_key_dec = jnp.einsum(
        "chts,cthk->cshk", grad_scores, decayed_query, preferred_element_type=jnp.float32
    )

    def backward_step(carried, pieces):
        reset_now, decay_now, grad_now = pieces
        grad_state_in = decay_now[..., None] * (grad_now + carried)
        return ((1.0 - reset_now) * grad_state_in, carried)

    first_local, grad_out_local = lax.scan(
        backward_step,
        jnp.zeros(grad_state_low.shape[1:], jnp.float32),
        (resets, decay_end, grad_state_low),
        reverse=True,
    )
    outgoing = carried_in(
        (device_decay, first_local),
        "seq",
        chain_state,
        (jnp.ones_like(device_decay), jnp.zeros_like(first_local)),
        True,
    )[1]
    following = keep_after[:, None, None] * jnp.exp(
        jnp.sum(ending, axis=0) - jnp.cumsum(ending, axis=0)
    )
    grad_state_out = grad_out_local + following[..., None] * outgoing[None]
    grad_scaled = grad_state_low + grad_state_out
    grad_update = grad_state_out.astype(jnp.bfloat16)
    grad_key_dec = grad_key_dec + jnp.einsum(
        "chkv,cshv->cshk", grad_update, reduced_value, preferred_element_type=jnp.float32
    )
    grad_value = grad_value + jnp.einsum(
        "cshk,chkv->cshv", decayed_key, grad_update, preferred_element_type=jnp.float32
    )
    query_factor = jnp.exp(cumul - ending[:, None])
    key_factor = jnp.exp(ending[:, None] - cumul)
    query_term = grad_query_dec * (query_raw * query_scale * query_factor)
    key_term = grad_key_dec * (key_raw * key_factor)
    extra_term = jnp.sum(key_term - query_term, axis=1) + jnp.sum(grad_scaled * scaled_rows, axis=3)
    local_term = query_term - key_term
    grad_log_decay = jnp.flip(jnp.cumsum(jnp.flip(local_term, 1), axis=1), 1) + extra_term[:, None]
    grad_query = grad_query_dec * query_scale * query_factor
    grad_key = grad_key_dec * key_factor
    return (grad_query, grad_key, grad_value, grad_log_decay)


def shards(
    tokens,
    row_starts,
    attn_gain,
    query_weight,
    key_weight,
    value_weight,
    gate_weight,
    rank_down,
    rank_up,
    rank_bias,
    group_gain,
    out_weight,
    feed_gain,
    feed_gate,
    feed_up,
    feed_down,
    cotangent,
):
    rows_local = tokens.shape[0]
    slice_width = tokens.shape[1]
    heads_local = query_weight.shape[2] // HK
    head_count = lax.axis_size("head")
    spans = rows_local // SPAN
    span_ids = lax.axis_index("seq") * spans + jnp.arange(spans, dtype=jnp.int32)
    resets = jnp.any((row_starts // SPAN)[None, :] == span_ids[:, None], axis=1).astype(jnp.float32)
    keep_before = jnp.cumprod(1.0 - resets)
    keep_after = jnp.concatenate(
        [jnp.cumprod((1.0 - resets)[::-1])[::-1][1:], jnp.ones((1,), jnp.float32)]
    )
    causal = jnp.arange(SPAN)[:, None] >= jnp.arange(SPAN)[None, :]
    key_shape = (spans, SPAN, heads_local, HK)
    value_shape = (spans, SPAN, heads_local, HV)
    residual = tokens.astype(jnp.float32)
    layer_number = 0
    gathered_attn = gather_features(residual)
    normed_attn, inverse_attn = normalize(
        gathered_attn, attn_gain[layer_number].astype(jnp.float32)
    )
    query_raw = matmul(normed_attn, query_weight[layer_number])
    key_raw = matmul(normed_attn, key_weight[layer_number])
    reduced_value = matmul(normed_attn, value_weight[layer_number]).astype(jnp.bfloat16)
    gate_raw = matmul(normed_attn, gate_weight[layer_number])
    low_rank = matmul(normed_attn, rank_down[layer_number]).astype(jnp.bfloat16)
    gate_logit = matmul(low_rank, rank_up[layer_number]) + rank_bias[layer_number].astype(
        jnp.float32
    )
    log_decay = jax.nn.log_sigmoid(gate_logit) / GATE_NORM
    core_output, kept_core = core_forward(
        query_raw.reshape(key_shape),
        key_raw.reshape(key_shape),
        reduced_value.reshape(value_shape),
        log_decay.reshape(key_shape),
        resets,
        keep_before,
        causal,
    )
    core_output = core_output.reshape(rows_local, heads_local, HV)
    group_inverse_norm = lax.rsqrt(jnp.mean(core_output * core_output, axis=2, keepdims=True) + EPS)
    group_normalized = core_output * group_inverse_norm
    gate_activations = gate_raw.reshape(rows_local, heads_local, HV)
    common_gain = group_gain[layer_number].astype(jnp.float32)
    gated_low = (
        (group_normalized * common_gain * jax.nn.silu(gate_activations))
        .astype(jnp.bfloat16)
        .reshape(rows_local, heads_local * HV)
    )
    middle = residual + reduce_partial(matmul(gated_low, out_weight[layer_number]))
    gathered_feed = gather_features(middle)
    normed_feed, inverse_feed = normalize(
        gathered_feed, feed_gain[layer_number].astype(jnp.float32)
    )
    gate_feed = matmul(normed_feed, feed_gate[layer_number])
    up_feed = matmul(normed_feed, feed_up[layer_number])
    hidden_feed = (jax.nn.silu(gate_feed) * up_feed).astype(jnp.bfloat16)
    residual = middle + reduce_partial(matmul(hidden_feed, feed_down[layer_number]))
    memory = [
        (
            gathered_attn,
            normed_attn,
            inverse_attn,
            low_rank,
            gate_logit,
            kept_core,
            group_inverse_norm,
            group_normalized,
            gate_activations,
            gated_low,
            gathered_feed,
            normed_feed,
            inverse_feed,
            gate_feed,
            up_feed,
            hidden_feed,
        )
    ]
    layer_out = residual.astype(jnp.bfloat16)
    grad_stream = cotangent.astype(jnp.float32)
    layer_grads = []
    layer_number = 0
    (
        gathered_attn,
        normed_attn,
        inverse_attn,
        low_rank,
        gate_logit,
        kept_core,
        group_inverse_norm,
        group_normalized,
        gate_activations,
        gated_low,
        gathered_feed,
        normed_feed,
        inverse_feed,
        gate_feed,
        up_feed,
        hidden_feed,
    ) = memory[layer_number]
    grad_full = gather_grads(grad_stream)
    grad_feed_down = rows_product(hidden_feed, grad_full)
    grad_hidden = cols_product(grad_full, feed_down[layer_number])
    sigma_feed = jax.nn.sigmoid(gate_feed)
    grad_up_feed = (grad_hidden * gate_feed * sigma_feed).astype(jnp.bfloat16)
    grad_gate_feed = (
        grad_hidden * up_feed * sigma_feed * (1.0 + gate_feed * (1.0 - sigma_feed))
    ).astype(jnp.bfloat16)
    grad_feed_gate = rows_product(normed_feed, grad_gate_feed)
    grad_feed_up = rows_product(normed_feed, grad_up_feed)
    grad_normed_feed = cols_product(grad_gate_feed, feed_gate[layer_number]) + cols_product(
        grad_up_feed, feed_up[layer_number]
    )
    gain_feed = feed_gain[layer_number].astype(jnp.float32)
    stat_feed = norm_stat(grad_normed_feed, gathered_feed, inverse_feed, gain_feed)
    slice_feed = lax.psum_scatter(
        grad_normed_feed.astype(jnp.bfloat16), "head", scatter_dimension=1, tiled=True
    ).astype(jnp.float32)
    total_feed = lax.psum_scatter(
        jnp.tile(stat_feed, (1, head_count)).astype(jnp.bfloat16),
        "head",
        scatter_dimension=1,
        tiled=True,
    ).astype(jnp.float32)
    grad_middle_norm, grad_feed_gain = norm_back(
        slice_feed, total_feed, gathered_feed, inverse_feed, gain_feed, slice_width
    )
    grad_middle = grad_stream + grad_middle_norm
    feed_grads = (grad_feed_gain, grad_feed_gate, grad_feed_up, grad_feed_down)
    grad_mid_full = gather_grads(grad_middle)
    grad_out = rows_product(gated_low, grad_mid_full)
    grad_gated = cols_product(grad_mid_full, out_weight[layer_number]).reshape(
        rows_local, heads_local, HV
    )
    common_gain = group_gain[layer_number].astype(jnp.float32)
    sigma_gate = jax.nn.sigmoid(gate_activations)
    normed_core_gradient = grad_gated * gate_activations * sigma_gate
    grad_gate_values = (
        (
            grad_gated
            * group_normalized
            * common_gain
            * sigma_gate
            * (1.0 + gate_activations * (1.0 - sigma_gate))
        )
        .astype(jnp.bfloat16)
        .reshape(rows_local, heads_local * HV)
    )
    shared_gradient = jnp.sum(normed_core_gradient * group_normalized, axis=(0, 1))
    inside_term = normed_core_gradient * common_gain
    grad_core = group_inverse_norm * (
        inside_term
        - group_normalized * jnp.mean(inside_term * group_normalized, axis=2, keepdims=True)
    )
    grad_query_raw, grad_key_raw, grad_value_raw, grad_log_decay = core_backward(
        grad_core.astype(jnp.bfloat16).reshape(value_shape), kept_core, resets, keep_after, causal
    )
    grad_query_low = grad_query_raw.reshape(rows_local, heads_local * HK).astype(jnp.bfloat16)
    grad_key_low = grad_key_raw.reshape(rows_local, heads_local * HK).astype(jnp.bfloat16)
    grad_value_low = grad_value_raw.reshape(rows_local, heads_local * HV).astype(jnp.bfloat16)
    grad_logit = (
        grad_log_decay.reshape(rows_local, heads_local * HK)
        / GATE_NORM
        * jax.nn.sigmoid(-gate_logit)
    )
    grad_rank_up = exact_rows(low_rank, grad_logit)
    grad_rank_bias = jnp.sum(grad_logit, axis=0)
    grad_low = exact_cols(grad_logit, rank_up[layer_number])
    grad_query = rows_product(normed_attn, grad_query_low)
    grad_key = rows_product(normed_attn, grad_key_low)
    grad_value = rows_product(normed_attn, grad_value_low)
    grad_gate = rows_product(normed_attn, grad_gate_values)
    grad_normed_attn = cols_product(grad_query_low, query_weight[layer_number]) + cols_product(
        grad_key_low, key_weight[layer_number]
    )
    grad_normed_attn = (
        grad_normed_attn
        + cols_product(grad_value_low, value_weight[layer_number])
        + cols_product(grad_gate_values, gate_weight[layer_number])
    )
    grad_normed_attn = grad_normed_attn + exact_cols(grad_low, rank_down[layer_number])
    gain_attn = attn_gain[layer_number].astype(jnp.float32)
    stat_attn = norm_stat(grad_normed_attn, gathered_attn, inverse_attn, gain_attn)
    slice_attn = lax.psum_scatter(
        grad_normed_attn.astype(jnp.bfloat16), "head", scatter_dimension=1, tiled=True
    ).astype(jnp.float32)
    total_attn = lax.psum_scatter(
        jnp.tile(stat_attn, (1, head_count)).astype(jnp.bfloat16),
        "head",
        scatter_dimension=1,
        tiled=True,
    ).astype(jnp.float32)
    low_total = lax.psum_scatter(
        jnp.tile(grad_low, (1, head_count)).astype(jnp.bfloat16),
        "head",
        scatter_dimension=1,
        tiled=True,
    ).astype(jnp.float32)
    shared_total = lax.psum_scatter(
        jnp.tile(shared_gradient[None, :], (1, head_count)).astype(jnp.bfloat16),
        "head",
        scatter_dimension=1,
        tiled=True,
    ).astype(jnp.float32)
    grad_rank_down = exact_rows(normed_attn, low_total)
    grad_input_norm, grad_attn_gain = norm_back(
        slice_attn, total_attn, gathered_attn, inverse_attn, gain_attn, slice_width
    )
    grad_stream = grad_middle + grad_input_norm
    attn_grads = (
        grad_attn_gain,
        grad_query,
        grad_key,
        grad_value,
        grad_gate,
        grad_rank_down,
        grad_rank_up,
        grad_rank_bias,
        shared_total[0],
        grad_out,
    )
    layer_grads.insert(0, tuple(attn_grads) + tuple(feed_grads))
    stacked = tuple((jnp.stack([layer_grads[0][member]]) for member in range(14)))
    stacked = jax.tree.map(lambda part: part.astype(jnp.float32), lax.psum(as_sent(stacked), "seq"))
    return (layer_out, grad_stream) + tuple(stacked)


def solution(mesh):
    placed = (
        P("seq", "head"),
        P(),
        P(),
        P(None, None, "head"),
        P(None, None, "head"),
        P(None, None, "head"),
        P(None, None, "head"),
        P(),
        P(None, None, "head"),
        P(None, "head"),
        P(),
        P(None, "head", None),
        P(),
        P(None, None, "head"),
        P(None, None, "head"),
        P(None, "head", None),
        P("seq", "head"),
    )
    return jax.shard_map(
        shards,
        mesh=mesh,
        in_specs=placed,
        out_specs=(
            P("seq", "head"),
            P("seq", "head"),
            P(None, "head"),
            P(None, None, "head"),
            P(None, None, "head"),
            P(None, None, "head"),
            P(None, None, "head"),
            P(),
            P(None, None, "head"),
            P(None, "head"),
            P(),
            P(None, "head", None),
            P(None, "head"),
            P(None, None, "head"),
            P(None, None, "head"),
            P(None, "head", None),
        ),
        check_vma=False,
    )
```

profile of v0, /device:TPU:0, one launch (start us, length us, event | category | flops | bytes accessed | tf_op | source)
XLA Modules:
  0.0 1145.5 jit_solution(17989597503372898996)
XLA Ops:
  14.3 33.0 %all-gather.9.cloned.1.call-done = bf16[2048,1024]{1,0:T(8,128)(2,1)} async-done(((bf16[2048,256]{1,0:T(8,128)(2,1)}), bf16[2048,1024]{1,0:T(8,128)(2,1)}) %all-gather.9.cloned.1.call-update) | async-done | bytes 4194320 | tf_op jit(solution)/shard_map/all_gather | solution.py:77
  58.9 21.1 %all-gather.3 = bf16[8,1,128]{2,1,0:T(2,128)(2,1)} all-gather(bf16[1,1,128]{2,1,0:T(2,128)(2,1)S(1)} %convert_bitcast_fusion.1), channel_id=3, replica_groups=mesh['seq'=8,'head'=4] {'seq'}, dimensions={0}, use_global_device_ids=true | all-gather | bytes 2304 | tf_op jit(solution)/shard_map/all_gather | solution.py:22
  93.8 184.6 %while.58 = (s32[]{:T(128)}, f32[1,128,256]{2,1,0:T(8,128)}, f32[32,1,128,256]{3,2,1,0:T(8,128)}, f32[32,1,128]{2,1,0:T(1,128)}, f32[32]{0:T(128)}, /*index=5*/f...) while((s32[]{:T(128)}, f32[1,128,256]{2,1,0:T(8,128)}, ...), condition=%wide.region_4.5_spmd.clone, body=%wide.region_3.4_spmd.clone.sunk | while | flops 196612 | bytes 657560 | solution.py:143
  279.2 33.4 %all-gather = bf16[8,128,256]{2,1,0:T(8,128)(2,1)} all-gather(bf16[1,128,256]{2,1,0:T(8,128)(2,1)S(1)} %convert_element_type.447), channel_id=2, replica_groups=mesh['seq'=8,'head'=4] {'seq'}, dimensions={0}, use_global_device_ids=true | all-gather | bytes 589824 | tf_op jit(solution)/shard_map/all_gather | solution.py:22
  334.3 56.7 %reduce-scatter.9.cloned.1.call-done = bf16[2048,256]{1,0:T(8,128)(2,1)} async-done(((bf16[2048,1024]{1,0:T(8,128)(2,1)}), bf16[2048,256]{1,0:T(8,128)(2,1)}) %reduce-scatter.9.cloned.1.call-update) | async-done | bytes 1048592 | tf_op jit(solution)/shard_map/reduce_scatter | solution.py:81
  395.7 33.3 %all-gather.11.cloned.1.call-done = bf16[2048,1024]{1,0:T(8,128)(2,1)} async-done(((bf16[2048,256]{1,0:T(8,128)(2,1)}), bf16[2048,1024]{1,0:T(8,128)(2,1)}) %all-gather.11.cloned.1.call-update) | async-done | bytes 4194320 | tf_op jit(solution)/shard_map/all_gather | solution.py:77
  432.4 6.7 fusion.38
  444.3 21.2 %all-gather.13.cloned.1.call-done = bf16[2048,1024]{1,0:T(8,128)(2,1)} async-done(((bf16[2048,256]{1,0:T(8,128)(2,1)}), bf16[2048,1024]{1,0:T(8,128)(2,1)}) %all-gather.13.cloned.1.call-update) | async-done | bytes 4194320 | tf_op jit(solution)/shard_map/all_gather | solution.py:87
  465.5 10.5 multiply_convert_fusion
  480.7 7.1 fusion.100
  491.7 11.6 %all-reduce = bf16[2048,4]{0,1:T(4,128)(2,1)} all-reduce(bf16[2048,4]{0,1:T(4,128)(2,1)} %tile.8), channel_id=8, replica_groups=mesh['seq'=8,'head'=4] {'head'}, use_global_device_ids=true, to_apply=%region_16.17.clone | all-reduce | flops 8192 | bytes 32768
  505.3 27.2 %reduce-scatter.13.cloned.1.call-done = bf16[2048,256]{1,0:T(8,128)(2,1)} async-done(((bf16[2048,1024]{1,0:T(8,128)(2,1)}), bf16[2048,256]{1,0:T(8,128)(2,1)}) %reduce-scatter.13.cloned.1.call-update) | async-done | bytes 1048592 | tf_op jit(solution)/shard_map/reduce_scatter | solution.py:391
  535.7 7.0 convolution_convert_fusion
  542.8 8.1 fusion.31
  559.8 11.0 all-gather.15.cloned.1.call-done
  584.2 114.0 %while.59 = (s32[]{:T(128)}, f32[1,128,256]{2,1,0:T(8,128)S(1)}, f32[32,1,128,256]{3,2,1,0:T(8,128)}, f32[32]{0:T(128)S(1)}, f32[32,1,128]{2,1,0:T(1,128)}, /*in...) while((s32[]{:T(128)}, f32[1,128,256]{2,1,0:T(8,128)S(1)}, ...), condition=%wide.region_19.20_spmd.clone, body=%wide.region_18.19_spmd.clone.sunk | while | flops 163845 | bytes 657068 | solution.py:221
  704.8 33.2 %all-gather.2 = bf16[8,128,256]{2,1,0:T(8,128)(2,1)} all-gather(bf16[1,128,256]{2,1,0:T(8,128)(2,1)S(1)} %convert_element_type.477), channel_id=4, replica_groups=mesh['seq'=8,'head'=4] {'seq'}, dimensions={0}, use_global_device_ids=true | all-gather | bytes 589824 | tf_op jit(solution)/shard_map/all_gather | solution.py:22
  738.1 11.4 while.57
  749.5 6.9 multiply_convert_fusion.6
  807.9 14.3 %fusion.11 = (bf16[2048]{0:T(1024)(128)(2,1)S(1)}, bf16[2048,1024]{1,0:T(8,128)(2,1)}) fusion(bf16[2048,1024]{1,0:T(8,128)(2,1)} %all-gather.9.cloned.1.call-done, f32[1024]{0:T(1024)S(1)} %bitcast.396, f32[2048]{0:T(1024)S(1)} %copy-done.61, f32[2048,16]{0,1:T(8,128)S(1)} %get-tuple-element.535, bf16[1,1024,16]{1,2,0:T(8,128)(2,1)S(1)} %copy-done.59, ...), kind=kOutput, calls=%fused_computation.26 | convolution fusion | flops 423622656 | bytes 42123264 | tf_op jit(solution)/shard_map/tk,jk->tj/dot_general | solution.py:67
  826.3 10.7 all-reduce.1
  844.3 201.9 %all-reduce.6.cloned.1.call-done = (bf16[1,1024,128]{2,1,0:T(8,128)(2,1)}, bf16[1,1024,128]{2,1,0:T(8,128)(2,1)}, bf16[1,1024,256]{2,1,0:T(8,128)(2,1)}, bf16[1,...) async-done(((bf16[1,1024,128]{2,1,0:T(8,128)(2,1)}, ...) | async-done | bytes 6422544 | tf_op jit(solution)/shard_map/psum | solution.py:499
  1061.3 30.7 %reduce-scatter.15.cloned.1.call-done = bf16[2048,256]{1,0:T(8,128)(2,1)} async-done(((bf16[2048,1024]{1,0:T(8,128)(2,1)}), bf16[2048,256]{1,0:T(8,128)(2,1)}) %reduce-scatter.15.cloned.1.call-update) | async-done | bytes 1048592 | tf_op jit(solution)/shard_map/reduce_scatter | solution.py:459
  1097.3 38.1 %all-reduce.2 = (bf16[1,256]{1,0:T(2,128)(2,1)S(1)}, bf16[1,1024,16]{1,2,0:T(8,128)(2,1)S(1)}, bf16[1,16,128]{2,1,0:T(8,128)(2,1)S(1)}, bf16[1,128]{1,0:T(2,128)...) all-reduce(bf16[1,256]{1,0:T(2,128)(2,1)S(1)} %convert_element_type, ...), channel_id=1, replica_groups=mesh['seq'=8,'head'=4] {'seq'}, use_global_device_ids=true, to_apply=%region_30.31 | all-reduce | flops 19328 | bytes 77312 | tf_op jit(solution)/shard_map/psum | solution.py:499
  (588 shorter events, 464.4 us)
Async XLA Ops:
  7.2 458.3 %copy-start = (bf16[1,704,1024]{2,1,0:T(8,128)(2,1)S(1)}, bf16[1,704,1024]{2,1,0:T(8,128)(2,1)}, u32[]{:S(2)}) copy-start(bf16[1,704,1024]{2,1,0:T(8,128)(2,1)} %param.40) | copy-start | bytes 4325380
  7.2 40.1 %all-gather.9.cloned.1.call-start = ((), (), s32[]{:S(2)}) async-start(), calls=%async_computation.6 | async-start | bytes 5242880 | tf_op jit(solution)/shard_map/all_gather | solution.py:77
  7.9 383.0 %reduce-scatter.9.cloned.1.call-start = ((), (), s32[]{:S(2)}) async-start(), calls=%async_computation.7 | async-start | bytes 5242880 | tf_op jit(solution)/shard_map/reduce_scatter | solution.py:81
  10.8 41.1 %copy-start.68 = (f32[1,1024]{1,0:T(1,128)}, f32[1,1024]{1,0:T(1,128)S(1)}, u32[]{:S(2)}) copy-start(f32[1,1024]{1,0:T(1,128)S(1)} %mul.605) | copy-start | bytes 12292
  334.2 94.7 %all-gather.11.cloned.1.call-start = ((), (), s32[]{:S(2)}) async-start(), calls=%async_computation.8 | async-start | bytes 5242880 | tf_op jit(solution)/shard_map/all_gather | solution.py:77
  393.8 71.7 %all-gather.13.cloned.1.call-start = ((), (), s32[]{:S(2)}) async-start(), calls=%async_computation.10 | async-start | bytes 5242880 | tf_op jit(solution)/shard_map/all_gather | solution.py:87
  394.4 138.1 %reduce-scatter.13.cloned.1.call-start = ((), (), s32[]{:S(2)}) async-start(), calls=%async_computation.11 | async-start | bytes 5242880 | tf_op jit(solution)/shard_map/reduce_scatter | solution.py:391
  487.9 83.0 %all-gather.15.cloned.1.call-start = ((), (), s32[]{:S(2)}) async-start(), calls=%async_computation.12 | async-start | bytes 5242880 | tf_op jit(solution)/shard_map/all_gather | solution.py:87
  535.6 287.2 %reduce-scatter.11.cloned.1.call-start = ((), (), s32[]{:S(2)}) async-start(), calls=%async_computation.9 | async-start | bytes 5242880 | tf_op jit(solution)/shard_map/reduce_scatter | solution.py:81
  542.7 296.6 %reduce-scatter.19.cloned.1.call-start = ((), (), s32[]{:S(2)}) async-start(), calls=%async_computation.15 | async-start | bytes 327680
  555.4 15.5 %copy-start.70 = (f32[2048]{0:T(1024)S(1)}, f32[2048]{0:T(1024)}, u32[]{:S(2)}) copy-start(f32[2048]{0:T(1024)} %rsqrt.29) | copy-start | bytes 24580
  555.4 15.5 %copy-start.76 = (f32[1,256]{1,0:T(1,128)S(1)}, f32[1,256]{1,0:T(1,128)}, u32[]{:S(2)}) copy-start(f32[1,256]{1,0:T(1,128)} %convert_element_type.538) | copy-start | bytes 3076
  581.6 117.5 %copy-start.66 = (pred[64,64]{1,0:T(8,128)(4,1)S(1)}, pred[64,64]{1,0:T(8,128)(4,1)}, u32[]{:S(2)}) copy-start(pred[64,64]{1,0:T(8,128)(4,1)} %iota_compare_fusion) | copy-start | bytes 12292
  584.2 118.0 %copy-start.14 = (f32[1,128,256]{2,1,0:T(8,128)S(1)}, f32[1,128,256]{2,1,0:T(8,128)}, u32[]{:S(2)}) copy-start(f32[1,128,256]{2,1,0:T(8,128)} %get-tuple-element.302) | copy-start | bytes 393220
  584.2 118.0 %copy-start.55 = (f32[32,128]{1,0:T(8,128)S(1)}, f32[32,128]{1,0:T(8,128)}, u32[]{:S(2)}) copy-start(f32[32,128]{1,0:T(8,128)} %copy-done.54) | copy-start | bytes 49156
  584.2 118.0 %copy-start.57 = (f32[32,128]{1,0:T(8,128)S(1)}, f32[32,128]{1,0:T(8,128)}, u32[]{:S(2)}) copy-start(f32[32,128]{1,0:T(8,128)} %copy-done.56) | copy-start | bytes 49156
  703.6 45.9 %copy-start.52 = (f32[32,128]{1,0:T(8,128)S(1)}, f32[32,128]{1,0:T(8,128)}, u32[]{:S(2)}) copy-start(f32[32,128]{1,0:T(8,128)} %get-tuple-element.521) | copy-start | bytes 49156
  777.2 63.6 %reduce-scatter.17.cloned.1.call-start = ((), (), s32[]{:S(2)}) async-start(), calls=%async_computation.14 | async-start | bytes 327680 | tf_op jit(solution)/shard_map/reduce_scatter | solution.py:468
  782.0 264.2 %all-reduce.6.cloned.1.call-start = ((), (), s32[]{:S(2)}) async-start(), calls=%async_computation.16 | async-start | bytes 12845056 | tf_op jit(solution)/shard_map/psum | solution.py:499
  791.8 300.2 %reduce-scatter.15.cloned.1.call-start = ((), (), s32[]{:S(2)}) async-start(), calls=%async_computation.13 | async-start | bytes 5242880 | tf_op jit(solution)/shard_map/reduce_scatter | solution.py:459
  1057.4 34.6 %copy-start.19 = (bf16[2048,256]{1,0:T(8,128)(2,1)S(1)}, bf16[2048,256]{1,0:T(8,128)(2,1)}, u32[]{:S(2)}) copy-start(bf16[2048,256]{1,0:T(8,128)(2,1)} %param.41) | copy-start | bytes 3145732
  1057.4 34.6 %copy-start.29 = (bf16[2048,256]{1,0:T(8,128)(2,1)S(1)}, bf16[2048,256]{1,0:T(8,128)(2,1)}, u32[]{:S(2)}) copy-start(bf16[2048,256]{1,0:T(8,128)(2,1)} %reduce-scatter.13.cloned.1.call-done) | copy-start | bytes 3145732
  1057.4 34.6 %copy-start.65 = (f32[2048]{0:T(1024)S(1)}, f32[2048]{0:T(1024)}, u32[]{:S(2)}) copy-start(f32[2048]{0:T(1024)} %copy-done.62) | copy-start | bytes 24580
  1059.3 79.5 %copy-start.1 = (bf16[1,704,1024]{2,1,0:T(8,128)(2,1)S(1)}, bf16[1,704,1024]{2,1,0:T(8,128)(2,1)}, u32[]{:S(2)}) copy-start(bf16[1,704,1024]{2,1,0:T(8,128)(2,1)} %param.40) | copy-start | bytes 4325380
  (74 other events, 341.8 us)
Sparse Core Ops, SparseCore 0:
  9.6 37.7 all-gather.8
  334.4 56.5 reduce-scatter.8
  393.9 35.0 all-gather.10
  430.4 35.0 all-gather.12
  488.0 44.4 reduce-scatter.12
  535.8 35.0 all-gather.14
  573.3 44.4 reduce-scatter.10
  777.3 16.4 reduce-scatter.18
  796.9 20.0 reduce-scatter.16
  824.3 221.8 all-reduce.5
  1048.7 43.2 reduce-scatter.14
where the time goes:
time: 1160 us; the launch traced here: 1150 us
  waiting for transfers between devices  416 us (36%)
  other arithmetic  235 us (20%)
  matrix products  160 us (14%)
  blocking collectives  148 us (13%)
  local copies, waits for them, and re-layouts  128 us (11%)
  loops' own time  42.9 us (4%)
  between operations  14.9 us (1%)
    psum x1, waiting for transfers between devices, shards(): lax.psum(as_sent(stacked), 'seq')  202 us
    all_gather x3, blocking collectives, carried_in(): lax.all_gather(a.astype(kind), axis)  87.8 us
    dynamic_update_slice x64, other arithmetic, core_forward(): lax.scan(forward_step, jnp.zeros(state_update.shape[1:], jnp.float32), (r...  70.6 us
    all_gather x2, waiting for transfers between devices, gather_features(): lax.all_gather(slice_value.astype(jnp.bfloat16), 'head', axis=1, tiled=True)  66.3 us
    dynamic_slice x64, local copies, waits for them, and re-layouts, core_forward(): lax.scan(forward_step, jnp.zeros(state_update.shape[1:], jnp.float32), (r...  58.4 us
    reduce_scatter x2, waiting for transfers between devices, reduce_partial(): lax.psum_scatter(partial_value.astype(jnp.bfloat16), 'head', scatter_dime...  56.7 us
    add x32, other arithmetic, forward_step(): return (decay_now[..., None] * state_in + update_now, state_in)  54.6 us
    dot_general x8, matrix products, cols_product(): lax.dot_general(left, right, (((1,), (1,)), ((), ())), preferred_element_...  41.6 us
  transfers between devices with their start and end apart: 11, of which 8 were waited for; matrix products, arithmetic and copies ran while one was open for 23% of the time, Pallas kernels for 0%

commit v1 on v0

--- a/solution.py
+++ b/solution.py
@@ -1,16 +1,318 @@
+import functools
+
 import jax
 import jax.numpy as jnp
 from jax import lax
+from jax.experimental import pallas as pl
+from jax.experimental.pallas import tpu as pltpu
 from jax.sharding import PartitionSpec as P
 
 MODEL_WIDTH = 1024
 HK = 128
 HV = 256
 SPAN = 64
-
-
+RANK = 16
 EPS = 1e-06
 GATE_NORM = 16.0
+TILE = 256
+PER = TILE // SPAN
+BLOCK = 256
+AHEAD = 3
+F32 = jnp.float32
+BF16 = jnp.bfloat16
+MESH = pl.DeviceIdType.MESH
+VMEM_LIMIT = 60 * 1024 * 1024
+
+
+def dot_nn(a, b):
+    return jnp.dot(a, b, preferred_element_type=F32)
+
+
+def dot_nt(a, b):
+    return lax.dot_general(a, b, (((1,), (1,)), ((), ())), preferred_element_type=F32)
+
+
+def dot_tn(a, b):
+    return lax.dot_general(a, b, (((0,), (0,)), ((), ())), preferred_element_type=F32)
+
+
+def peers():
+    me = lax.axis_index("head")
+    mate = me + 1 - 2 * lax.rem(me, 2)
+    cross = lax.rem(me + 2, 4)
+    far = cross + 1 - 2 * lax.rem(cross, 2)
+    return me, mate, cross, far
+
+
+def greet_head():
+    _, mate, cross, far = peers()
+    barrier = pltpu.get_barrier_semaphore()
+    for other in (mate, cross, far):
+        pl.semaphore_signal(barrier, inc=1, device_id={"head": other}, device_id_type=MESH)
+
+
+def greet_seq(count):
+    place = lax.axis_index("seq")
+    barrier = pltpu.get_barrier_semaphore()
+
+    def one(step, carry):
+        other = lax.rem(place + step, count)
+        pl.semaphore_signal(barrier, inc=1, device_id={"seq": other}, device_id_type=MESH)
+        return carry
+
+    lax.fori_loop(1, count, one, 0)
+
+
+def to_head(src, dst, send, recv, other):
+    return pltpu.make_async_remote_copy(
+        src_ref=src, dst_ref=dst, send_sem=send, recv_sem=recv,
+        device_id={"head": other}, device_id_type=MESH,
+    )
+
+
+def to_seq(src, dst, send, recv, other):
+    return pltpu.make_async_remote_copy(
+        src_ref=src, dst_ref=dst, send_sem=send, recv_sem=recv,
+        device_id={"seq": other}, device_id_type=MESH,
+    )
+
+
+def span_masks(rows, cols):
+    r = lax.broadcasted_iota(jnp.int32, (rows, cols), 0)
+    c = lax.broadcasted_iota(jnp.int32, (rows, cols), 1)
+    same = (r >> 6) == (c >> 6)
+    return same & (r >= c), same
+
+
+def three(x):
+    a = x.astype(BF16)
+    rest = x - a.astype(F32)
+    b = rest.astype(BF16)
+    c = (rest - b.astype(F32)).astype(BF16)
+    return jnp.concatenate([a, b, c], axis=1)
+
+
+def fold(x):
+    w = x.shape[1] // 3
+    return x[:, :w] + x[:, w : 2 * w] + x[:, 2 * w :]
+
+
+def front_kernel(
+    tiles, count,
+    x_ref, c_ref, keep_ref, gain_ref, wq, wk, wv, wg, wr, rup, bias_ref,
+    na_o, cg_o, inv_o, f_o, b_o, o_o, u_o, e_o, in_o, d_o,
+    grid_buf, wcat, tri, state, decay, sbuf, rbuf, sems, esend, erecv,
+):
+    i = pl.program_id(0)
+    me, mate, cross, far = peers()
+    place = lax.axis_index("seq")
+    total = 2 * tiles
+
+    def own_mate(m):
+        return to_head(grid_buf.at[m, me], grid_buf.at[m, me], sems.at[0, m], sems.at[1, m], mate)
+
+    def own_cross(m):
+        return to_head(grid_buf.at[m, me], grid_buf.at[m, me], sems.at[2, m], sems.at[3, m], cross)
+
+    def onward(m):
+        return to_head(grid_buf.at[m, cross], grid_buf.at[m, cross], sems.at[4, m], sems.at[5, m], mate)
+
+    @pl.when(i == 0)
+    def _():
+        greet_head()
+        greet_seq(count)
+
+        def own(m, carry):
+            rows = pl.ds(pl.multiple_of(m * TILE, TILE), TILE)
+            grid_buf[m, me] = x_ref[rows, :]
+            grid_buf[m + tiles, me] = c_ref[rows, :]
+            return carry
+
+        lax.fori_loop(0, tiles, own, 0)
+        pl.semaphore_wait(pltpu.get_barrier_semaphore(), 3 + count - 1)
+        for m in range(AHEAD):
+            own_cross(m).start()
+            own_mate(m).start()
+        wcat[:, 0:128] = wq[...]
+        wcat[:, 128:256] = wk[...]
+        wcat[:, 256:512] = wv[...]
+        wcat[:, 512:768] = wg[...]
+        wcat[:, 768:896] = wr[...]
+        causal, same = span_masks(TILE, TILE)
+        tri[0:TILE, :] = jnp.where(causal, 1.0, 0.0).astype(BF16)
+        tri[TILE : 2 * TILE, :] = jnp.where(same, 1.0, 0.0).astype(BF16)
+        state[...] = jnp.zeros_like(state)
+        decay[...] = jnp.ones_like(decay)
+
+    @pl.when(i < total)
+    def _():
+        own_cross(i).wait_recv()
+        onward(i).start()
+
+    @pl.when(i + AHEAD < total)
+    def _():
+        own_cross(i + AHEAD).start()
+        own_mate(i + AHEAD).start()
+
+    @pl.when(i >= 1)
+    def _():
+        own_mate(i - 1).wait_recv()
+        onward(i - 1).wait_recv()
+
+    @pl.when((i >= 1) & (i <= tiles))
+    def _():
+        m = i - 1
+        squares = jnp.zeros((TILE, 1), F32)
+        for j in range(4):
+            xj = grid_buf[m, j].astype(F32)
+            squares = squares + jnp.sum(xj * xj, axis=1, keepdims=True)
+        inv = lax.rsqrt(squares / MODEL_WIDTH + EPS)
+        inv_o[...] = jnp.broadcast_to(inv, (TILE, 128))
+        for j in range(4):
+            cols = slice(j * BLOCK, (j + 1) * BLOCK)
+            xj = grid_buf[m, j].astype(F32)
+            na_o[:, cols] = (xj * inv * gain_ref[:, cols]).astype(BF16)
+        proj = dot_nn(na_o[...], wcat[...])
+        q = proj[:, 0:128]
+        k = proj[:, 128:256]
+        v = proj[:, 256:512].astype(BF16)
+        o_o[:, 0:256] = proj[:, 512:768]
+        lr = proj[:, 768:896].astype(BF16)
+        z = dot_nn(lr, rup[...]) + bias_ref[...]
+        g = (jnp.minimum(z, 0.0) - jnp.log1p(jnp.exp(-jnp.abs(z)))) / GATE_NORM
+        sums = fold(dot_nn(tri[...], three(g)))
+        b = sums[0:TILE]
+        e = sums[TILE : 2 * TILE]
+        fq = (HK ** (-0.5)) * jnp.exp(b - e)
+        fk = jnp.exp(e - b)
+        qf = q * fq
+        kf = k * fk
+        f_o[:, 0:128] = qf
+        f_o[:, 128:256] = kf
+        f_o[:, 256:384] = fq
+        f_o[:, 384:512] = fk
+        f_o[:, 512:640] = jax.nn.sigmoid(-z) / GATE_NORM
+        qd = qf.astype(BF16)
+        kd = kf.astype(BF16)
+        causal, _ = span_masks(TILE, TILE)
+        scores = jnp.where(causal, dot_nt(qd, kd), 0.0).astype(BF16)
+        b_o[:, 0:256] = v
+        b_o[:, 256:512] = scores
+        b_o[:, 512:640] = lr
+        o_o[:, 256:512] = dot_nn(scores, v)
+        for c in range(PER):
+            rows = slice(c * SPAN, (c + 1) * SPAN)
+            update = dot_tn(v[rows], kd[rows])
+            u_o[c] = update
+            ee = jnp.exp(e[c * SPAN : c * SPAN + 1])
+            e_o[0, c : c + 1, :] = ee
+            through = keep_ref[m, c : c + 1, :] * ee
+            state[...] = through * state[...] + update
+            decay[...] = through * decay[...]
+
+    @pl.when(i == tiles)
+    def _():
+        d_o[...] = decay[...]
+        sbuf[0:HV, :] = state[...].astype(BF16)
+        d = decay[...]
+        hi = d.astype(BF16).astype(F32)
+        first = lax.broadcasted_iota(jnp.int32, (16, 128), 0) < 8
+        both = jnp.where(first, jnp.concatenate([hi, hi], axis=0), jnp.concatenate([d - hi, d - hi], axis=0))
+        sbuf[HV : HV + 16, :] = both.astype(BF16)
+
+        def send(p, carry):
+            to_seq(sbuf, rbuf.at[place], esend.at[p], erecv.at[place], p).start()
+            return carry
+
+        lax.fori_loop(place + 1, count, send, 0)
+
+    @pl.when(i > tiles)
+    def _():
+        m = i - 1
+        for j in range(4):
+            cg_o[:, j * BLOCK : (j + 1) * BLOCK] = grid_buf[m, j]
+
+    @pl.when(i == total)
+    def _():
+        in_o[...] = jnp.zeros_like(in_o)
+
+        def join(p, carry):
+            to_seq(sbuf, rbuf.at[p], esend.at[p], erecv.at[p], place).wait_recv()
+            got = rbuf[p].astype(F32)
+            d = got[HV : HV + 1] + got[HV + 8 : HV + 9]
+            in_o[...] = got[0:HV] + d * in_o[...]
+            return carry
+
+        lax.fori_loop(0, place, join, 0)
+
+        def sent(p, carry):
+            to_seq(sbuf, rbuf.at[place], esend.at[p], erecv.at[place], p).wait_send()
+            return carry
+
+        lax.fori_loop(place + 1, count, sent, 0)
+
+        def out(m, carry):
+            own_cross(m).wait_send()
+            own_mate(m).wait_send()
+            onward(m).wait_send()
+            return carry
+
+        lax.fori_loop(0, total, out, 0)
+
+
+def whole(shape):
+    zeros = (0,) * len(shape)
+    return pl.BlockSpec(shape, lambda i: zeros, pipeline_mode=pl.Buffered(1))
+
+
+def front(x, cot, keep, gain, wq, wk, wv, wg, wr, rup, bias):
+    rows = x.shape[0]
+    tiles = rows // TILE
+    count = lax.axis_size("seq")
+
+    def tile(shape, lag, axis0=True):
+        rest = (0,) * (len(shape) - 1)
+        return pl.BlockSpec(shape, lambda i: (jnp.clip(i - lag, 0, tiles - 1),) + rest)
+
+    ins = (x, cot, keep, gain, wq, wk, wv, wg, wr, rup, bias)
+    outs = [
+        ((rows, MODEL_WIDTH), BF16, tile((TILE, MODEL_WIDTH), 1)),
+        ((rows, MODEL_WIDTH), BF16, tile((TILE, MODEL_WIDTH), 1 + tiles)),
+        ((rows, 128), F32, tile((TILE, 128), 1)),
+        ((rows, 640), F32, tile((TILE, 640), 1)),
+        ((rows, 640), BF16, tile((TILE, 640), 1)),
+        ((rows, 512), F32, tile((TILE, 512), 1)),
+        ((rows // SPAN, HV, HK), F32, tile((PER, HV, HK), 1)),
+        ((tiles, 8, 128), F32, tile((1, 8, 128), 1)),
+        ((HV, HK), F32, whole((HV, HK))),
+        ((8, 128), F32, whole((8, 128))),
+    ]
+    return pl.pallas_call(
+        functools.partial(front_kernel, tiles, count),
+        grid=(2 * tiles + 1,),
+        out_shape=[jax.ShapeDtypeStruct(s, d) for s, d, _ in outs],
+        in_specs=[whole(a.shape) for a in ins],
+        out_specs=[s for _, _, s in outs],
+        scratch_shapes=[
+            pltpu.VMEM((2 * tiles, 4, TILE, BLOCK), BF16),
+            pltpu.VMEM((MODEL_WIDTH, 896), BF16),
+            pltpu.VMEM((2 * TILE, TILE), BF16),
+            pltpu.VMEM((HV, HK), F32),
+            pltpu.VMEM((8, 128), F32),
+            pltpu.VMEM((HV + 16, HK), BF16),
+            pltpu.VMEM((count, HV + 16, HK), BF16),
+            pltpu.SemaphoreType.DMA((6, 2 * tiles)),
+            pltpu.SemaphoreType.DMA((count,)),
+            pltpu.SemaphoreType.DMA((count,)),
+        ],
+        compiler_params=pltpu.CompilerParams(
+            collective_id=1, has_side_effects=True, vmem_limit_bytes=VMEM_LIMIT,
+            dimension_semantics=("arbitrary",),
+        ),
+        name="front",
+    )(*ins)
+
+
 EXACT_MATH = lax.Precision.HIGHEST
 
 
@@ -115,74 +417,42 @@
     return (input_gradient, gain_gradient)
 
 
-def core_forward(query_raw, key_raw, reduced_value, log_decay, resets, keep_before, causal):
-    query_scale = HK ** (-0.5)
-    cumul = jnp.cumsum(log_decay, axis=1)
-    ending = cumul[:, -1]
-    decayed_query = (query_raw * query_scale * jnp.exp(cumul - ending[:, None])).astype(
-        jnp.bfloat16
-    )
-    decayed_key = (key_raw * jnp.exp(ending[:, None] - cumul)).astype(jnp.bfloat16)
-    scores = jnp.einsum(
-        "cthk,cshk->chts", decayed_query, decayed_key, preferred_element_type=jnp.float32
-    )
-    attn_weights = jnp.where(causal, scores, 0.0).astype(jnp.bfloat16)
-    intra_out = jnp.einsum(
-        "chts,cshv->cthv", attn_weights, reduced_value, preferred_element_type=jnp.float32
-    )
-    state_update = jnp.einsum(
-        "cshk,cshv->chkv", decayed_key, reduced_value, preferred_element_type=jnp.float32
-    )
-    decay_end = jnp.exp(ending)
+def core_forward(f, bb, o, u, ee, inc, decay, reduced_value, resets, keep_before, causal):
+    spans = u.shape[0]
+    shape = (spans, SPAN, 1, HK)
+    qf = f[:, 0:128].reshape(shape)
+    kf = f[:, 128:256].reshape(shape)
+    fq = f[:, 256:384].reshape(shape)
+    fk = f[:, 384:512].reshape(shape)
+    blocks = bb[:, 256:512].reshape(spans // PER, PER, SPAN, PER, SPAN)
+    attn_weights = jnp.stack([blocks[:, c, :, c, :] for c in range(PER)], axis=1).reshape(spans, 1, SPAN, SPAN)
+    state_update = jnp.swapaxes(u, 1, 2)[:, None]
+    decay_end = ee[:, 0:PER].reshape(spans, 1, HK)
 
     def forward_step(carried, pieces):
         reset_now, decay_now, update_now = pieces
         state_in = (1.0 - reset_now) * carried
         return (decay_now[..., None] * state_in + update_now, state_in)
 
-    final_local, states_local = lax.scan(
-        forward_step,
-        jnp.zeros(state_update.shape[1:], jnp.float32),
-        (resets, decay_end, state_update),
-    )
-    device_decay = keep_before[-1] * jnp.exp(jnp.sum(ending, axis=0))
-    incoming = carried_in(
-        (device_decay, final_local),
-        "seq",
-        chain_state,
-        (jnp.ones_like(device_decay), jnp.zeros_like(final_local)),
-        False,
-    )[1]
-    prior_decay = keep_before[:, None, None] * jnp.exp(jnp.cumsum(ending, axis=0) - ending)
-    states_in = states_local + prior_decay[..., None] * incoming[None]
+    _, states_in = lax.scan(forward_step, inc.T[None], (resets, decay_end, state_update))
     scaled_rows = decay_end[..., None] * states_in
     state_low = scaled_rows.astype(jnp.bfloat16)
+    decayed_query = qf.astype(jnp.bfloat16)
+    decayed_key = kf.astype(jnp.bfloat16)
     across_output = jnp.einsum(
         "cthk,chkv->cthv", decayed_query, state_low, preferred_element_type=jnp.float32
     )
-    kept_core = (
-        query_raw,
-        key_raw,
-        cumul,
-        ending,
-        decayed_query,
-        decayed_key,
-        attn_weights,
-        reduced_value,
-        decay_end,
-        scaled_rows,
-        state_low,
-        device_decay,
-    )
-    return (intra_out + across_output, kept_core)
+    intra_out = o[:, 256:512].reshape(spans, SPAN, 1, HV)
+    kept = (qf, kf, fq, fk, decayed_query, decayed_key, attn_weights, reduced_value, decay_end, scaled_rows, state_low, decay)
+    return (intra_out + across_output, kept)
 
 
 def core_backward(grad_core, kept_core, resets, keep_after, causal):
     (
-        query_raw,
-        key_raw,
-        cumul,
-        ending,
+        qf,
+        kf,
+        fq,
+        fk,
         decayed_query,
         decayed_key,
         attn_weights,
@@ -192,7 +462,7 @@
         state_low,
         device_decay,
     ) = kept_core
-    query_scale = HK ** (-0.5)
+    ending = jnp.log(decay_end)
     grad_attn = jnp.einsum(
         "cthv,cshv->chts", grad_core, reduced_value, preferred_element_type=jnp.float32
     )
@@ -243,15 +513,13 @@
     grad_value = grad_value + jnp.einsum(
         "cshk,chkv->cshv", decayed_key, grad_update, preferred_element_type=jnp.float32
     )
-    query_factor = jnp.exp(cumul - ending[:, None])
-    key_factor = jnp.exp(ending[:, None] - cumul)
-    query_term = grad_query_dec * (query_raw * query_scale * query_factor)
-    key_term = grad_key_dec * (key_raw * key_factor)
+    query_term = grad_query_dec * qf
+    key_term = grad_key_dec * kf
     extra_term = jnp.sum(key_term - query_term, axis=1) + jnp.sum(grad_scaled * scaled_rows, axis=3)
     local_term = query_term - key_term
     grad_log_decay = jnp.flip(jnp.cumsum(jnp.flip(local_term, 1), axis=1), 1) + extra_term[:, None]
-    grad_query = grad_query_dec * query_scale * query_factor
-    grad_key = grad_key_dec * key_factor
+    grad_query = grad_query_dec * fq
+    grad_key = grad_key_dec * fk
     return (grad_query, grad_key, grad_value, grad_log_decay)
 
 
@@ -290,28 +558,25 @@
     value_shape = (spans, SPAN, heads_local, HV)
     residual = tokens.astype(jnp.float32)
     layer_number = 0
+    tiles = rows_local // TILE
+    keep_tiles = jnp.zeros((tiles, 8, 128), jnp.float32).at[:, 0:PER].set(
+        jnp.broadcast_to((1.0 - resets).reshape(tiles, PER, 1), (tiles, PER, 128))
+    )
+    rank_wide = jnp.pad(rank_down[0], ((0, 0), (0, 128 - RANK)))
+    rank_tall = jnp.pad(rank_up[0], ((0, 128 - RANK), (0, 0)))
+    normed_attn, grad_full, inverse_wide, f, bb, o, u, ee, inc, dec = front(
+        tokens, cotangent, keep_tiles, attn_gain.astype(jnp.float32), query_weight[0], key_weight[0],
+        value_weight[0], gate_weight[0], rank_wide, rank_tall, rank_bias.astype(jnp.float32),
+    )
+    inverse_attn = inverse_wide[:, 0:1]
+    low_rank = bb[:, 512:512 + RANK]
+    reduced_value = bb[:, 0:256]
+    gate_raw = o[:, 0:256]
     gathered_attn = gather_features(residual)
-    normed_attn, inverse_attn = normalize(
-        gathered_attn, attn_gain[layer_number].astype(jnp.float32)
-    )
-    query_raw = matmul(normed_attn, query_weight[layer_number])
-    key_raw = matmul(normed_attn, key_weight[layer_number])
-    reduced_value = matmul(normed_attn, value_weight[layer_number]).astype(jnp.bfloat16)
-    gate_raw = matmul(normed_attn, gate_weight[layer_number])
-    low_rank = matmul(normed_attn, rank_down[layer_number]).astype(jnp.bfloat16)
-    gate_logit = matmul(low_rank, rank_up[layer_number]) + rank_bias[layer_number].astype(
-        jnp.float32
-    )
-    log_decay = jax.nn.log_sigmoid(gate_logit) / GATE_NORM
     core_output, kept_core = core_forward(
-        query_raw.reshape(key_shape),
-        key_raw.reshape(key_shape),
-        reduced_value.reshape(value_shape),
-        log_decay.reshape(key_shape),
-        resets,
-        keep_before,
-        causal,
-    )
+        f, bb, o, u, ee, inc, dec[0:1], reduced_value.reshape(value_shape), resets, keep_before, causal
+    )
+    gate_logit = None
     core_output = core_output.reshape(rows_local, heads_local, HV)
     group_inverse_norm = lax.rsqrt(jnp.mean(core_output * core_output, axis=2, keepdims=True) + EPS)
     group_normalized = core_output * group_inverse_norm
@@ -373,7 +638,6 @@
         up_feed,
         hidden_feed,
     ) = memory[layer_number]
-    grad_full = gather_grads(grad_stream)
     grad_feed_down = rows_product(hidden_feed, grad_full)
     grad_hidden = cols_product(grad_full, feed_down[layer_number])
     sigma_feed = jax.nn.sigmoid(gate_feed)
@@ -434,9 +698,7 @@
     grad_key_low = grad_key_raw.reshape(rows_local, heads_local * HK).astype(jnp.bfloat16)
     grad_value_low = grad_value_raw.reshape(rows_local, heads_local * HV).astype(jnp.bfloat16)
     grad_logit = (
-        grad_log_decay.reshape(rows_local, heads_local * HK)
-        / GATE_NORM
-        * jax.nn.sigmoid(-gate_logit)
+        grad_log_decay.reshape(rows_local, heads_local * HK) * f[:, 512:640]
     )
     grad_rank_up = exact_rows(low_rank, grad_logit)
     grad_rank_bias = jnp.sum(grad_logit, axis=0)

time: 1160 us -> 997 us (0.86)
  waiting for transfers between devices: 416 us -> 332 us
  other arithmetic: 235 us -> 158 us
  Pallas kernels: 0 us -> 58.7 us
  blocking collectives: 148 us -> 116 us
  matrix products: 160 us -> 134 us
    pallas_call x0 -> x1, Pallas kernels: none -> 58.7 us  [front(): pl.pallas_call(functools.partial(front_kernel, tiles, count), grid=(2 * t...]
    add x32, other arithmetic: 54.6 us -> 2.93 us  [forward_step(): return (decay_now[..., None] * state_in + update_now, state_in)]
    all_gather x3 -> x2, blocking collectives: 87.8 us -> 54.7 us  [carried_in(): lax.all_gather(a.astype(kind), axis)]
    all_gather x2, waiting for transfers between devices: 66.3 us -> 33.6 us  [gather_features(): lax.all_gather(slice_value.astype(jnp.bfloat16), 'head', axis=1, tiled=True)]
    all_gather x2 -> x1, waiting for transfers between devices: 32.2 us -> 0.01 us  [gather_grads(): lax.all_gather(slice_grad.astype(jnp.bfloat16), 'head', axis=1, tiled=True)]
    dynamic_update_slice x64, other arithmetic: 70.6 us -> 42.5 us  [core_forward(): lax.scan(forward_step, inc.T[None], (resets, decay_end, state_update))]
    dot_general x10 -> x4, matrix products: 40.3 us -> 16.5 us  [matmul(): return jnp.dot(left, right, preferred_element_type=jnp.float32)]
    mul x32, local copies, waits for them, and re-layouts: 20.6 us -> 0.3 us  [backward_step(): grad_state_in = decay_now[..., None] * (grad_now + carried)]
  transfers between devices with their start and end apart: 11 -> 10, of which waited for: 8 -> 5; matrix products, arithmetic and copies ran while one was open for 23% -> 27% of each run, Pallas kernels for 0% -> 0%
where the time goes in v1:
time: 997 us; the launch traced here: 988 us
  waiting for transfers between devices  332 us (33%)
  other arithmetic  158 us (16%)
  matrix products  134 us (13%)
  local copies, waits for them, and re-layouts  129 us (13%)
  blocking collectives  116 us (12%)
  Pallas kernels  58.7 us (6%)
  loops' own time  44.3 us (4%)
  between operations  15.4 us (2%)
    psum x1, waiting for transfers between devices, shards(): lax.psum(as_sent(stacked), 'seq')  197 us
    dynamic_slice x128, local copies, waits for them, and re-layouts, core_forward(): lax.scan(forward_step, inc.T[None], (resets, decay_end, state_update))  70 us
    pallas_call x1, Pallas kernels, front(): pl.pallas_call(functools.partial(front_kernel, tiles, count), grid=(2 * t...  58.7 us
    all_gather x2, blocking collectives, carried_in(): lax.all_gather(a.astype(kind), axis)  54.7 us
    dot_general x8, matrix products, cols_product(): lax.dot_general(left, right, (((1,), (1,)), ((), ())), preferred_element_...  44.4 us
    reduce_scatter x2, waiting for transfers between devices, reduce_partial(): lax.psum_scatter(partial_value.astype(jnp.bfloat16), 'head', scatter_dime...  42.8 us
    dynamic_update_slice x64, other arithmetic, core_forward(): lax.scan(forward_step, inc.T[None], (resets, decay_end, state_update))  42.5 us
    psum x1, blocking collectives, shards(): lax.psum(as_sent(stacked), 'seq')  38.1 us
  transfers between devices with their start and end apart: 10, of which 5 were waited for; matrix products, arithmetic and copies ran while one was open for 27% of the time, Pallas kernels for 0%

profile of v1, /device:TPU:0, one launch (start us, length us, event | category | flops | bytes accessed | tf_op | source)
XLA Modules:
  0.0 988.0 jit_solution(1991468128077597668)
XLA Ops:
  15.6 58.7 %front.1 = (bf16[2048,1024]{1,0:T(8,128)(2,1)}, bf16[2048,1024]{1,0:T(8,128)(2,1)}, f32[2048,128]{1,0:T(8,128)}, f32[2048,640]{1,0:T(8,128)}, bf16[2048,640]{1,0...) custom-call(bf16[2048,256]{1,0:T(8,128)(2,1)} %x_ref.1, ...), custom_call_target="tpu_custom_call" | custom-call | tf_op jit(solution)/shard_map/front/pallas_call | solution.py:290
  79.2 97.9 %while.44 = (s32[]{:T(128)}, f32[1,128,256]{2,1,0:T(8,128)S(1)}, f32[32,1,128,256]{3,2,1,0:T(8,128)}, f32[32,1,128]{2,1,0:T(1,128)S(1)}, f32[32]{0:T(128)S(1)}, ...) while((s32[]{:T(128)}, f32[1,128,256]{2,1,0:T(8,128)S(1)}, f32[32,1,128,256]{3,2,1,0:T(8,128)}, ...), condition=%wide.region_2.3_spmd, body=%wide.region_1.2_spmd.sunk | while | flops 131075 | bytes 1181829 | solution.py:437
  192.4 42.8 %reduce-scatter.9.cloned.1.call-done = bf16[2048,256]{1,0:T(8,128)(2,1)} async-done(((bf16[2048,1024]{1,0:T(8,128)(2,1)}), bf16[2048,256]{1,0:T(8,128)(2,1)}) %reduce-scatter.9.cloned.1.call-update) | async-done | bytes 1048592 | tf_op jit(solution)/shard_map/reduce_scatter | solution.py:383
  239.5 33.6 %all-gather.7.cloned.1.call-done = bf16[2048,1024]{1,0:T(8,128)(2,1)} async-done(((bf16[2048,256]{1,0:T(8,128)(2,1)}), bf16[2048,1024]{1,0:T(8,128)(2,1)}) %all-gather.7.cloned.1.call-update) | async-done | bytes 4194320 | tf_op jit(solution)/shard_map/all_gather | solution.py:379
  284.8 7.9 multiply_convert_fusion
  292.7 5.5 fusion.33
  298.3 7.2 fusion.76
  309.3 11.5 %all-reduce.3 = bf16[2048,4]{0,1:T(4,128)(2,1)} all-reduce(bf16[2048,4]{0,1:T(4,128)(2,1)} %tile.8), channel_id=7, replica_groups=mesh['seq'=8,'head'=4] {'head'}, use_global_device_ids=true, to_apply=%region_9.10.clone | all-reduce | flops 8192 | bytes 32768
  322.8 27.4 %reduce-scatter.13.cloned.1.call-done = bf16[2048,256]{1,0:T(8,128)(2,1)} async-done(((bf16[2048,1024]{1,0:T(8,128)(2,1)}), bf16[2048,256]{1,0:T(8,128)(2,1)}) %reduce-scatter.13.cloned.1.call-update) | async-done | bytes 1048592 | tf_op jit(solution)/shard_map/reduce_scatter | solution.py:655
  379.5 21.3 %all-gather.2 = bf16[8,1,128]{2,1,0:T(2,128)(2,1)} all-gather(bf16[1,1,128]{2,1,0:T(2,128)(2,1)S(1)} %slice_bitcast_fusion), channel_id=3, replica_groups=mesh['seq'=8,'head'=4] {'seq'}, dimensions={0}, use_global_device_ids=true | all-gather | bytes 2304 | tf_op jit(solution)/shard_map/all_gather | solution.py:324
  411.5 7.6 fusion.24
  419.8 7.6 fusion.26
  432.0 5.6 multiply_reduce_fusion.1
  445.4 94.0 %while.46 = (s32[]{:T(128)}, f32[1,128,256]{2,1,0:T(8,128)S(1)}, f32[32,1,128,256]{3,2,1,0:T(8,128)}, f32[32]{0:T(128)S(1)}, f32[32,1,128]{2,1,0:T(1,128)S(1)}, ...) while((s32[]{:T(128)}, f32[1,128,256]{2,1,0:T(8,128)S(1)}, ...), condition=%wide.region_12.13_spmd.clone, body=%wide.region_11.12_spmd.clone.sunk | while | flops 163845 | bytes 657068 | solution.py:491
  543.6 33.4 %all-gather = bf16[8,128,256]{2,1,0:T(8,128)(2,1)} all-gather(bf16[1,128,256]{2,1,0:T(8,128)(2,1)S(1)} %convert_element_type.426), channel_id=2, replica_groups=mesh['seq'=8,'head'=4] {'seq'}, dimensions={0}, use_global_device_ids=true | all-gather | bytes 589824 | tf_op jit(solution)/shard_map/all_gather | solution.py:324
  577.1 11.2 %while.45 = (s32[]{:T(128)}, f32[1,128,256]{2,1,0:T(8,128)S(1)}, s32[]{:T(128)}, bf16[8,1,128,256]{3,2,1,0:T(8,128)(2,1)}, bf16[8,1,128]{2,1,0:T(2,128)(2,1)}, /*index=5*/s32[]{:T(128)}, s32[]{:T(128)}, s32[]{:T(128)}, s32[]{:T(128)}) while((s32[]{:T(128)}, f32[1,128,256]{2,1,0:T(8,128)S(1)}, s32[]{:T(128)}, ...), condition=%wide.region_17.18_spmd, body=%wide.region_16.17_spmd.sunk | while | flops 98438 | bytes 329115 | solution.py:339
  588.2 6.7 subtract_reduce_fusion
  596.4 5.6 fusion.10
  649.9 17.1 %multiply_reduce_fusion = (bf16[2048]{0:T(1024)(128)(2,1)S(1)}, bf16[2048,1024]{1,0:T(8,128)(2,1)}) fusion(bf16[2048,1024]{1,0:T(8,128)(2,1)} %all-gather.11.cloned.1.call-done, f32[2048]{0:T(1024)S(1)} %slice_reduce_fusion, f32[1024]{0:T(1024)S(1)} %bitcast.344, f32[2048,16]{0,1:T(8,128)S(1)} %get-tuple-element.466, ...), kind=kOutput, calls=%fused_computation.20 | convolution fusion | flops 423622656 | bytes 42123264 | tf_op jit(solution)/shard_map/tk,jk->tj/dot_general | solution.py:369
  671.1 11.2 %all-reduce.4 = bf16[2048,4]{0,1:T(4,128)(2,1)S(1)} all-reduce(bf16[2048,4]{0,1:T(4,128)(2,1)S(1)} %tile.9), channel_id=9, replica_groups=mesh['seq'=8,'head'=4] {'head'}, use_global_device_ids=true, to_apply=%region_23.24.clone | all-reduce | flops 8192 | bytes 32768
  690.9 197.1 %all-reduce.9.cloned.1.call-done = (bf16[1,1024,128]{2,1,0:T(8,128)(2,1)}, bf16[1,1024,128]{2,1,0:T(8,128)(2,1)}, bf16[1,1024,256]{2,1,0:T(8,128)(2,1)}, bf16[1,...) async-done(((bf16[1,1024,128]{2,1,0:T(8,128)(2,1)}, ...) | async-done | bytes 6422544 | tf_op jit(solution)/shard_map/psum | solution.py:761
  903.2 30.6 %reduce-scatter.15.cloned.1.call-done = bf16[2048,256]{1,0:T(8,128)(2,1)} async-done(((bf16[2048,1024]{1,0:T(8,128)(2,1)}), bf16[2048,256]{1,0:T(8,128)(2,1)}) %reduce-scatter.15.cloned.1.call-update) | async-done | bytes 1048592 | tf_op jit(solution)/shard_map/reduce_scatter | solution.py:721
  933.7 5.3 fusion.16
  939.1 38.1 %all-reduce.5 = (bf16[1,256]{1,0:T(2,128)(2,1)S(1)}, bf16[1,1024,16]{1,2,0:T(8,128)(2,1)S(1)}, bf16[1,16,128]{2,1,0:T(8,128)(2,1)S(1)}, bf16[1,128]{1,0:T(2,128)...) all-reduce(bf16[1,256]{1,0:T(2,128)(2,1)S(1)} %convert_element_type, ...), channel_id=1, replica_groups=mesh['seq'=8,'head'=4] {'seq'}, use_global_device_ids=true, to_apply=%region_25.26 | all-reduce | flops 19328 | bytes 77312 | tf_op jit(solution)/shard_map/psum | solution.py:761
  (607 shorter events, 346.3 us)
Async XLA Ops:
  7.2 277.6 %copy-start = (bf16[1,704,1024]{2,1,0:T(8,128)(2,1)S(1)}, bf16[1,704,1024]{2,1,0:T(8,128)(2,1)}, u32[]{:S(2)}) copy-start(bf16[1,704,1024]{2,1,0:T(8,128)(2,1)} %param.40) | copy-start | bytes 4325380
  7.2 228.0 %reduce-scatter.9.cloned.1.call-start = ((), (), s32[]{:S(2)}) async-start(), calls=%async_computation.6 | async-start | bytes 5242880 | tf_op jit(solution)/shard_map/reduce_scatter | solution.py:383
  192.3 80.8 %all-gather.7.cloned.1.call-start = ((), (), s32[]{:S(2)}) async-start(), calls=%async_computation.7 | async-start | bytes 5242880 | tf_op jit(solution)/shard_map/all_gather | solution.py:379
  237.9 112.3 %reduce-scatter.13.cloned.1.call-start = ((), (), s32[]{:S(2)}) async-start(), calls=%async_computation.9 | async-start | bytes 5242880 | tf_op jit(solution)/shard_map/reduce_scatter | solution.py:655
  276.4 21.9 %copy-start.44 = (f32[2048]{0:T(1024)}, f32[2048]{0:T(1024)S(1)}, u32[]{:S(2)}) copy-start(f32[2048]{0:T(1024)S(1)} %add_rsqrt_fusion.1) | copy-start | bytes 24580
  305.6 126.4 %all-gather.9.cloned.1.call-start = ((), (), s32[]{:S(2)}) async-start(), calls=%async_computation.10 | async-start | bytes 5242880 | tf_op jit(solution)/shard_map/all_gather | solution.py:389
  353.3 296.5 %all-gather.11.cloned.1.call-start = ((), (), s32[]{:S(2)}) async-start(), calls=%async_computation.12 | async-start | bytes 5242880 | tf_op jit(solution)/shard_map/all_gather | solution.py:379
  353.9 313.7 %reduce-scatter.11.cloned.1.call-start = ((), (), s32[]{:S(2)}) async-start(), calls=%async_computation.8 | async-start | bytes 5242880 | tf_op jit(solution)/shard_map/reduce_scatter | solution.py:383
  378.6 27.8 %copy-start.63 = (bf16[2048,704]{0,1:T(8,128)(2,1)S(1)}, bf16[2048,704]{0,1:T(8,128)(2,1)}, u32[]{:S(2)}) copy-start(bf16[2048,704]{0,1:T(8,128)(2,1)} %get-tuple-element.434) | copy-start | bytes 8650756
  419.1 266.8 %reduce-scatter.19.cloned.1.call-start = ((), (), s32[]{:S(2)}) async-start(), calls=%async_computation.14 | async-start | bytes 327680
  443.0 96.7 %copy-start.11 = (bf16[2048,256]{1,0:T(8,128)(2,1)S(1)}, bf16[2048,256]{1,0:T(8,128)(2,1)}, u32[]{:S(2)}) copy-start(bf16[2048,256]{1,0:T(8,128)(2,1)} %get-tuple-element.450) | copy-start | bytes 3145732
  443.0 96.7 %copy-start.52 = (pred[64,64]{1,0:T(8,128)(4,1)S(1)}, pred[64,64]{1,0:T(8,128)(4,1)}, u32[]{:S(2)}) copy-start(pred[64,64]{1,0:T(8,128)(4,1)} %iota_compare_fusion) | copy-start | bytes 12292
  445.4 94.7 %copy-start.15 = (bf16[2048,128]{1,0:T(8,128)(2,1)S(1)}, bf16[2048,128]{1,0:T(8,128)(2,1)}, u32[]{:S(2)}) copy-start(bf16[2048,128]{1,0:T(8,128)(2,1)} %copy-done.13) | copy-start | bytes 1572868
  619.5 67.9 %reduce-scatter.17.cloned.1.call-start = ((), (), s32[]{:S(2)}) async-start(), calls=%async_computation.13 | async-start | bytes 327680 | tf_op jit(solution)/shard_map/reduce_scatter | solution.py:730
  620.9 267.1 %all-reduce.9.cloned.1.call-start = ((), (), s32[]{:S(2)}) async-start(), calls=%async_computation.15 | async-start | bytes 12845056 | tf_op jit(solution)/shard_map/psum | solution.py:761
  629.8 303.9 %reduce-scatter.15.cloned.1.call-start = ((), (), s32[]{:S(2)}) async-start(), calls=%async_computation.11 | async-start | bytes 5242880 | tf_op jit(solution)/shard_map/reduce_scatter | solution.py:721
  631.7 18.2 %copy-start.49 = (f32[2048]{0:T(1024)}, f32[2048]{0:T(1024)S(1)}, u32[]{:S(2)}) copy-start(f32[2048]{0:T(1024)S(1)} %slice_reduce_fusion) | copy-start | bytes 24580
  888.1 8.1 copy-start.41
  888.1 9.2 copy-start.36
  899.2 34.5 %copy-start.8 = (bf16[2048,256]{1,0:T(8,128)(2,1)S(1)}, bf16[2048,256]{1,0:T(8,128)(2,1)}, u32[]{:S(2)}) copy-start(bf16[2048,256]{1,0:T(8,128)(2,1)} %c_ref.1) | copy-start | bytes 3145732
  899.2 34.5 %copy-start.25 = (bf16[2048,256]{1,0:T(8,128)(2,1)S(1)}, bf16[2048,256]{1,0:T(8,128)(2,1)}, u32[]{:S(2)}) copy-start(bf16[2048,256]{1,0:T(8,128)(2,1)} %reduce-scatter.13.cloned.1.call-done) | copy-start | bytes 3145732
  899.3 34.5 %copy-start.46 = (f32[2048]{0:T(1024)S(1)}, f32[2048]{0:T(1024)}, u32[]{:S(2)}) copy-start(f32[2048]{0:T(1024)} %copy-done.44) | copy-start | bytes 24580
  899.3 34.5 %copy-start.47 = (f32[2048,1]{0,1:T(1,128)S(1)}, f32[2048,1]{0,1:T(1,128)}, u32[]{:S(2)}) copy-start(f32[2048,1]{0,1:T(1,128)} %dynamic-slice_convert_fusion.1) | copy-start | bytes 24580
  901.2 79.4 %copy-start.1 = (bf16[1,704,1024]{2,1,0:T(8,128)(2,1)S(1)}, bf16[1,704,1024]{2,1,0:T(8,128)(2,1)}, u32[]{:S(2)}) copy-start(bf16[1,704,1024]{2,1,0:T(8,128)(2,1)} %param.40) | copy-start | bytes 4325380
  (51 other events, 194.5 us)
Sparse Core Ops, SparseCore 0:
  192.4 42.6 reduce-scatter.8
  238.1 35.0 all-gather.6
  305.7 44.4 reduce-scatter.12
  353.5 35.0 all-gather.8
  389.9 35.0 all-gather.10
  427.4 44.4 reduce-scatter.10
  619.7 16.4 reduce-scatter.18
  638.6 20.0 reduce-scatter.16
  666.1 221.8 all-reduce.8
  890.4 43.2 reduce-scatter.14

commit v2 on v1

v2 whole, which is shorter than its diff:
```python
import functools

import jax
import jax.numpy as jnp
from jax import lax
from jax.experimental import pallas as pl
from jax.experimental.pallas import tpu as pltpu
from jax.sharding import PartitionSpec as P

MODEL_WIDTH = 1024
HK = 128
HV = 256
SPAN = 64
RANK = 16
EPS = 1e-06
GATE_NORM = 16.0
TILE = 256
PER = TILE // SPAN
BLOCK = 256
AHEAD = 3
F32 = jnp.float32
BF16 = jnp.bfloat16
MESH = pl.DeviceIdType.MESH
VMEM_LIMIT = 60 * 1024 * 1024


def dot_nn(a, b):
    return jnp.dot(a, b, preferred_element_type=F32)


def dot_nt(a, b):
    return lax.dot_general(a, b, (((1,), (1,)), ((), ())), preferred_element_type=F32)


def dot_tn(a, b):
    return lax.dot_general(a, b, (((0,), (0,)), ((), ())), preferred_element_type=F32)


def peers():
    me = lax.axis_index("head")
    mate = me + 1 - 2 * lax.rem(me, 2)
    cross = lax.rem(me + 2, 4)
    far = cross + 1 - 2 * lax.rem(cross, 2)
    return me, mate, cross, far


def greet_head():
    _, mate, cross, far = peers()
    barrier = pltpu.get_barrier_semaphore()
    for other in (mate, cross, far):
        pl.semaphore_signal(barrier, inc=1, device_id={"head": other}, device_id_type=MESH)


def greet_seq(count):
    place = lax.axis_index("seq")
    barrier = pltpu.get_barrier_semaphore()

    def one(step, carry):
        other = lax.rem(place + step, count)
        pl.semaphore_signal(barrier, inc=1, device_id={"seq": other}, device_id_type=MESH)
        return carry

    lax.fori_loop(1, count, one, 0)


def to_head(src, dst, send, recv, other):
    return pltpu.make_async_remote_copy(
        src_ref=src, dst_ref=dst, send_sem=send, recv_sem=recv,
        device_id={"head": other}, device_id_type=MESH,
    )


def to_seq(src, dst, send, recv, other):
    return pltpu.make_async_remote_copy(
        src_ref=src, dst_ref=dst, send_sem=send, recv_sem=recv,
        device_id={"seq": other}, device_id_type=MESH,
    )


def span_masks(rows, cols):
    r = lax.broadcasted_iota(jnp.int32, (rows, cols), 0)
    c = lax.broadcasted_iota(jnp.int32, (rows, cols), 1)
    same = (r >> 6) == (c >> 6)
    return same & (r >= c), same


def three(x):
    a = x.astype(BF16)
    rest = x - a.astype(F32)
    b = rest.astype(BF16)
    c = (rest - b.astype(F32)).astype(BF16)
    return jnp.concatenate([a, b, c], axis=1)


def fold(x):
    w = x.shape[1] // 3
    return x[:, :w] + x[:, w : 2 * w] + x[:, 2 * w :]


def front_kernel(
    tiles, count,
    x_ref, c_ref, keep_ref, gain_ref, wq, wk, wv, wg, wr, rup, bias_ref,
    na_o, cg_o, inv_o, f_o, b_o, o_o, u_o, e_o, in_o, d_o,
    grid_buf, wcat, tri, state, decay, sbuf, rbuf, sems, esend, erecv,
):
    i = pl.program_id(0)
    me, mate, cross, far = peers()
    place = lax.axis_index("seq")
    total = 2 * tiles

    def own_mate(m):
        return to_head(grid_buf.at[m, me], grid_buf.at[m, me], sems.at[0, m], sems.at[1, m], mate)

    def own_cross(m):
        return to_head(grid_buf.at[m, me], grid_buf.at[m, me], sems.at[2, m], sems.at[3, m], cross)

    def onward(m):
        return to_head(grid_buf.at[m, cross], grid_buf.at[m, cross], sems.at[4, m], sems.at[5, m], mate)

    @pl.when(i == 0)
    def _():
        greet_head()
        greet_seq(count)

        def own(m, carry):
            rows = pl.ds(pl.multiple_of(m * TILE, TILE), TILE)
            grid_buf[m, me] = x_ref[rows, :]
            grid_buf[m + tiles, me] = c_ref[rows, :]
            return carry

        lax.fori_loop(0, tiles, own, 0)
        pl.semaphore_wait(pltpu.get_barrier_semaphore(), 3 + count - 1)
        for m in range(AHEAD):
            own_cross(m).start()
            own_mate(m).start()
        wcat[:, 0:128] = wq[...]
        wcat[:, 128:256] = wk[...]
        wcat[:, 256:512] = wv[...]
        wcat[:, 512:768] = wg[...]
        wcat[:, 768:896] = wr[...]
        causal, same = span_masks(TILE, TILE)
        tri[0:TILE, :] = jnp.where(causal, 1.0, 0.0).astype(BF16)
        tri[TILE : 2 * TILE, :] = jnp.where(same, 1.0, 0.0).astype(BF16)
        state[...] = jnp.zeros_like(state)
        decay[...] = jnp.ones_like(decay)

    @pl.when(i < total)
    def _():
        own_cross(i).wait_recv()
        onward(i).start()

    @pl.when(i + AHEAD < total)
    def _():
        own_cross(i + AHEAD).start()
        own_mate(i + AHEAD).start()

    @pl.when(i >= 1)
    def _():
        own_mate(i - 1).wait_recv()
        onward(i - 1).wait_recv()

    @pl.when((i >= 1) & (i <= tiles))
    def _():
        m = i - 1
        squares = jnp.zeros((TILE, 1), F32)
        for j in range(4):
            xj = grid_buf[m, j].astype(F32)
            squares = squares + jnp.sum(xj * xj, axis=1, keepdims=True)
        inv = lax.rsqrt(squares / MODEL_WIDTH + EPS)
        inv_o[...] = jnp.broadcast_to(inv, (TILE, 128))
        for j in range(4):
            cols = slice(j * BLOCK, (j + 1) * BLOCK)
            xj = grid_buf[m, j].astype(F32)
            na_o[:, cols] = (xj * inv * gain_ref[:, cols]).astype(BF16)
        proj = dot_nn(na_o[...], wcat[...])
        q = proj[:, 0:128]
        k = proj[:, 128:256]
        v = proj[:, 256:512].astype(BF16)
        o_o[:, 0:256] = proj[:, 512:768]
        lr = proj[:, 768:896].astype(BF16)
        z = dot_nn(lr, rup[...]) + bias_ref[...]
        g = (jnp.minimum(z, 0.0) - jnp.log1p(jnp.exp(-jnp.abs(z)))) / GATE_NORM
        sums = fold(dot_nn(tri[...], three(g)))
        b = sums[0:TILE]
        e = sums[TILE : 2 * TILE]
        fq = (HK ** (-0.5)) * jnp.exp(b - e)
        fk = jnp.exp(e - b)
        qf = q * fq
        kf = k * fk
        f_o[:, 0:128] = qf
        f_o[:, 128:256] = kf
        f_o[:, 256:384] = fq
        f_o[:, 384:512] = fk
        f_o[:, 512:640] = jax.nn.sigmoid(-z) / GATE_NORM
        qd = qf.astype(BF16)
        kd = kf.astype(BF16)
        causal, _ = span_masks(TILE, TILE)
        scores = jnp.where(causal, dot_nt(qd, kd), 0.0).astype(BF16)
        b_o[:, 0:256] = v
        b_o[:, 256:512] = scores
        b_o[:, 512:640] = lr
        o_o[:, 256:512] = dot_nn(scores, v)
        for c in range(PER):
            rows = slice(c * SPAN, (c + 1) * SPAN)
            update = dot_tn(v[rows], kd[rows])
            u_o[c] = update
            ee = jnp.exp(e[c * SPAN : c * SPAN + 1])
            e_o[0, c : c + 1, :] = ee
            through = keep_ref[m, c : c + 1, :] * ee
            state[...] = through * state[...] + update
            decay[...] = through * decay[...]

    @pl.when(i == tiles)
    def _():
        d_o[...] = decay[...]
        sbuf[0:HV, :] = state[...].astype(BF16)
        d = decay[...]
        hi = d.astype(BF16).astype(F32)
        first = lax.broadcasted_iota(jnp.int32, (16, 128), 0) < 8
        both = jnp.where(first, jnp.concatenate([hi, hi], axis=0), jnp.concatenate([d - hi, d - hi], axis=0))
        sbuf[HV : HV + 16, :] = both.astype(BF16)

        def send(p, carry):
            to_seq(sbuf, rbuf.at[place], esend.at[p], erecv.at[place], p).start()
            return carry

        lax.fori_loop(place + 1, count, send, 0)

    @pl.when(i > tiles)
    def _():
        m = i - 1
        for j in range(4):
            cg_o[:, j * BLOCK : (j + 1) * BLOCK] = grid_buf[m, j]

    @pl.when(i == total)
    def _():
        in_o[...] = jnp.zeros_like(in_o)

        def join(p, carry):
            to_seq(sbuf, rbuf.at[p], esend.at[p], erecv.at[p], place).wait_recv()
            got = rbuf[p].astype(F32)
            d = got[HV : HV + 1] + got[HV + 8 : HV + 9]
            in_o[...] = got[0:HV] + d * in_o[...]
            return carry

        lax.fori_loop(0, place, join, 0)

        def sent(p, carry):
            to_seq(sbuf, rbuf.at[place], esend.at[p], erecv.at[place], p).wait_send()
            return carry

        lax.fori_loop(place + 1, count, sent, 0)

        def out(m, carry):
            own_cross(m).wait_send()
            own_mate(m).wait_send()
            onward(m).wait_send()
            return carry

        lax.fori_loop(0, total, out, 0)


def whole(shape):
    zeros = (0,) * len(shape)
    return pl.BlockSpec(shape, lambda i: zeros, pipeline_mode=pl.Buffered(1))


def front(x, cot, keep, gain, wq, wk, wv, wg, wr, rup, bias):
    rows = x.shape[0]
    tiles = rows // TILE
    count = lax.axis_size("seq")

    def tile(shape, lag, axis0=True):
        rest = (0,) * (len(shape) - 1)
        return pl.BlockSpec(shape, lambda i: (jnp.clip(i - lag, 0, tiles - 1),) + rest)

    ins = (x, cot, keep, gain, wq, wk, wv, wg, wr, rup, bias)
    outs = [
        ((rows, MODEL_WIDTH), BF16, tile((TILE, MODEL_WIDTH), 1)),
        ((rows, MODEL_WIDTH), BF16, tile((TILE, MODEL_WIDTH), 1 + tiles)),
        ((rows, 128), F32, tile((TILE, 128), 1)),
        ((rows, 640), F32, tile((TILE, 640), 1)),
        ((rows, 640), BF16, tile((TILE, 640), 1)),
        ((rows, 512), F32, tile((TILE, 512), 1)),
        ((rows // SPAN, HV, HK), F32, tile((PER, HV, HK), 1)),
        ((tiles, 8, 128), F32, tile((1, 8, 128), 1)),
        ((HV, HK), F32, whole((HV, HK))),
        ((8, 128), F32, whole((8, 128))),
    ]
    return pl.pallas_call(
        functools.partial(front_kernel, tiles, count),
        grid=(2 * tiles + 1,),
        out_shape=[jax.ShapeDtypeStruct(s, d) for s, d, _ in outs],
        in_specs=[whole(a.shape) for a in ins],
        out_specs=[s for _, _, s in outs],
        scratch_shapes=[
            pltpu.VMEM((2 * tiles, 4, TILE, BLOCK), BF16),
            pltpu.VMEM((MODEL_WIDTH, 896), BF16),
            pltpu.VMEM((2 * TILE, TILE), BF16),
            pltpu.VMEM((HV, HK), F32),
            pltpu.VMEM((8, 128), F32),
            pltpu.VMEM((HV + 16, HK), BF16),
            pltpu.VMEM((count, HV + 16, HK), BF16),
            pltpu.SemaphoreType.DMA((6, 2 * tiles)),
            pltpu.SemaphoreType.DMA((count,)),
            pltpu.SemaphoreType.DMA((count,)),
        ],
        compiler_params=pltpu.CompilerParams(
            collective_id=1, has_side_effects=True, vmem_limit_bytes=VMEM_LIMIT,
            dimension_semantics=("arbitrary",),
        ),
        name="front",
    )(*ins)


def tile_spec(tiles, shape, lag, back=False, col=0):
    rest = (0,) * (len(shape) - 2) + (col,)

    def index(i):
        t = jnp.clip(i - lag, 0, tiles - 1)
        return ((tiles - 1 - t) if back else t,) + rest

    return pl.BlockSpec(shape, index)


def ffn_kernel(
    tiles,
    x_ref, keep_ref, in_ref, gg_ref, gain_ref, wout, wfg, wfu, wfd,
    f_ref, o_ref, u_ref, e_ref, cg_ref,
    gated_o, oo_o, ws_o, h_o, inv_o, gsend_o, gown_o, psend_o, pown_o, stat_o, dg_o, du_o, dd_o,
    state, pa, pp, pg, ma, mp, mg, sc, rc, own, hg, nf_s, ag, au, ad, st_s, st_r,
    asem, psem, gsem, csem, hsem, tsem,
):
    i = pl.program_id(0)
    me, mate, cross, far = peers()
    last = tiles - 1

    def pair(buf, got, sem, t, which):
        block = mate if which == 0 else far
        return to_head(buf.at[t, block], got.at[t, which], sem.at[2 * which, t], sem.at[2 * which + 1, t], mate)

    def over(t):
        return to_head(sc.at[t], rc.at[t], csem.at[0, t], csem.at[1, t], cross)

    def own_mate(t):
        return to_head(hg.at[t, me], hg.at[t, me], hsem.at[0, t], hsem.at[1, t], mate)

    def own_cross(t):
        return to_head(hg.at[t, me], hg.at[t, me], hsem.at[2, t], hsem.at[3, t], cross)

    def onward(t):
        return to_head(hg.at[t, cross], hg.at[t, cross], hsem.at[4, t], hsem.at[5, t], mate)

    def stats(n, other):
        return to_head(st_s, st_r.at[n], tsem.at[0, n], tsem.at[1, n], other)

    @pl.when(i == 0)
    def _():
        greet_head()
        state[...] = in_ref[...]
        ag[...] = jnp.zeros_like(ag)
        au[...] = jnp.zeros_like(au)
        ad[...] = jnp.zeros_like(ad)
        st_s[...] = jnp.zeros_like(st_s)
        pl.semaphore_wait(pltpu.get_barrier_semaphore(), 3)

    @pl.when((i >= 5) & (i - 5 <= last))
    def _():
        t = i - 5
        own_cross(t).wait_recv()
        onward(t).start()

    @pl.when((i >= 3) & (i - 3 <= last))
    def _():
        t = i - 3
        over(t).wait_recv()
        rows = pl.ds(pl.multiple_of(t * TILE, TILE), TILE)
        h = x_ref[rows, :].astype(F32) + (own[lax.rem(t, 4)] + rc[t].astype(F32))
        h_o[...] = h
        hg[t, me] = h.astype(BF16)
        own_cross(t).start()
        own_mate(t).start()

    @pl.when((i >= 1) & (i - 1 <= last))
    def _():
        t = i - 1
        pair(pa, ma, asem, t, 0).wait_recv()
        pair(pa, ma, asem, t, 1).wait_recv()
        sc[t] = (pa[t, cross].astype(F32) + ma[t, 1].astype(F32)).astype(BF16)
        over(t).start()
        own[lax.rem(t, 4)] = pa[t, me].astype(F32) + ma[t, 0].astype(F32)

    @pl.when(i <= last)
    def _():
        t = i
        for c in range(PER):
            rows = slice(c * SPAN, (c + 1) * SPAN)
            scaled = (keep_ref[t, c : c + 1, :] * e_ref[0, c : c + 1, :]) * state[...]
            low = scaled.astype(BF16)
            ws_o[c] = low
            state[...] = scaled + u_ref[c]
            oo_o[rows, :] = o_ref[rows, 256:512] + dot_nt(f_ref[rows, :].astype(BF16), low)
        o = oo_o[...]
        gz = o_ref[:, 0:256]
        inv = lax.rsqrt(jnp.mean(o * o, axis=1, keepdims=True) + EPS)
        gated = (o * inv * gg_ref[...] * (gz * jax.nn.sigmoid(gz))).astype(BF16)
        gated_o[...] = gated
        for j in range(4):
            pa[t, j] = dot_nn(gated, wout[:, j * BLOCK : (j + 1) * BLOCK]).astype(BF16)
        pair(pa, ma, asem, t, 1).start()
        pair(pa, ma, asem, t, 0).start()

    @pl.when((i >= 7) & (i - 7 <= last))
    def _():
        t = i - 7
        for which in range(2):
            pair(pp, mp, psem, t, which).wait_recv()
            pair(pg, mg, gsem, t, which).wait_recv()
        psend_o[...] = (pp[t, cross].astype(F32) + mp[t, 1].astype(F32)).astype(BF16)
        pown_o[...] = pp[t, me].astype(F32) + mp[t, 0].astype(F32)
        gsend_o[...] = (pg[t, cross].astype(F32) + mg[t, 1].astype(F32)).astype(BF16)
        gown_o[...] = pg[t, me].astype(F32) + mg[t, 0].astype(F32)

    @pl.when((i >= 6) & (i - 6 <= last))
    def _():
        t = i - 6
        own_mate(t).wait_recv()
        onward(t).wait_recv()
        squares = jnp.zeros((TILE, 1), F32)
        for j in range(4):
            hj = hg[t, j].astype(F32)
            squares = squares + jnp.sum(hj * hj, axis=1, keepdims=True)
        inv = lax.rsqrt(squares / MODEL_WIDTH + EPS)
        inv_o[...] = jnp.broadcast_to(inv, (TILE, 128))
        for j in range(4):
            cols = slice(j * BLOCK, (j + 1) * BLOCK)
            nf_s[:, cols] = (hg[t, j].astype(F32) * inv * gain_ref[:, cols]).astype(BF16)
        nf = nf_s[...]
        fg = dot_nn(nf, wfg[...])
        fu = dot_nn(nf, wfu[...])
        sig = jax.nn.sigmoid(fg)
        silu = fg * sig
        act = (silu * fu).astype(BF16)
        cg = cg_ref[...]
        for j in range(4):
            pp[t, j] = dot_nn(act, wfd[:, j * BLOCK : (j + 1) * BLOCK]).astype(BF16)
        for which in range(2):
            pair(pp, mp, psem, t, which).start()
        gact = dot_nt(cg, wfd[...])
        gfg = (gact * fu * (sig * (1.0 + fg * (1.0 - sig)))).astype(BF16)
        gfu = (gact * silu).astype(BF16)
        stat = jnp.zeros((TILE, 1), F32)
        for j in range(4):
            rows = slice(j * BLOCK, (j + 1) * BLOCK)
            gj = dot_nt(gfg, wfg[rows, :]) + dot_nt(gfu, wfu[rows, :])
            stat = stat + jnp.sum(gj * nf_s[:, rows].astype(F32), axis=1, keepdims=True)
            pg[t, j] = gj.astype(BF16)
        for which in range(2):
            pair(pg, mg, gsem, t, which).start()
        st_s[pl.ds(t, 1), :] = jnp.broadcast_to(stat, (TILE, 128)).T[0:1, :]
        ad[...] += dot_tn(act, cg)
        ag[...] += dot_tn(nf, gfg)
        au[...] += dot_tn(nf, gfu)

    @pl.when(i == last + 6)
    def _():
        for n, other in enumerate((mate, cross, far)):
            stats(n, other).start()

    @pl.when(i == last + 7)
    def _():
        dg_o[...] = ag[...].astype(BF16)
        du_o[...] = au[...].astype(BF16)
        dd_o[...] = ad[...].astype(BF16)
        for n, other in enumerate((mate, cross, far)):
            stats(n, other).wait()
        stat_o[...] = (st_s[...] + st_r[0]) + (st_r[1] + st_r[2])

        def out(t, carry):
            for which in range(2):
                pair(pa, ma, asem, t, which).wait_send()
                pair(pp, mp, psem, t, which).wait_send()
                pair(pg, mg, gsem, t, which).wait_send()
            over(t).wait_send()
            own_cross(t).wait_send()
            own_mate(t).wait_send()
            onward(t).wait_send()
            return carry

        lax.fori_loop(0, tiles, out, 0)


def ffn(x, keep, inc, gg, gain, wout, wfg, wfu, wfd, f, o, u, e, cg):
    rows = x.shape[0]
    tiles = rows // TILE
    hidden = wfg.shape[1]
    width = wfg.shape[0]
    assert tiles <= 8
    ts = functools.partial(tile_spec, tiles)
    ins = (x, keep, inc, gg, gain, wout, wfg, wfu, wfd)
    outs = [
        ((rows, BLOCK), BF16, ts((TILE, BLOCK), 0)),
        ((rows, HV), F32, ts((TILE, HV), 0)),
        ((rows // SPAN, HV, HK), BF16, ts((PER, HV, HK), 0)),
        ((rows, BLOCK), F32, ts((TILE, BLOCK), 3)),
        ((rows, 128), F32, ts((TILE, 128), 6)),
        ((rows, BLOCK), BF16, ts((TILE, BLOCK), 7)),
        ((rows, BLOCK), F32, ts((TILE, BLOCK), 7)),
        ((rows, BLOCK), BF16, ts((TILE, BLOCK), 7)),
        ((rows, BLOCK), F32, ts((TILE, BLOCK), 7)),
        ((8, TILE), F32, whole((8, TILE))),
        ((width, hidden), BF16, whole((width, hidden))),
        ((width, hidden), BF16, whole((width, hidden))),
        ((hidden, width), BF16, whole((hidden, width))),
    ]
    tiled = lambda n: pltpu.VMEM((tiles, n, TILE, BLOCK), BF16)
    return pl.pallas_call(
        functools.partial(ffn_kernel, tiles),
        grid=(tiles + 7,),
        out_shape=[jax.ShapeDtypeStruct(s, d) for s, d, _ in outs],
        in_specs=[whole(a.shape) for a in ins]
        + [
            ts((TILE, 128), 0), ts((TILE, 512), 0), ts((PER, HV, HK), 0), ts((1, 8, 128), 0),
            ts((TILE, MODEL_WIDTH), 6),
        ],
        out_specs=[s for _, _, s in outs],
        scratch_shapes=[
            pltpu.VMEM((HV, HK), F32),
            tiled(4), tiled(4), tiled(4), tiled(2), tiled(2), tiled(2),
            pltpu.VMEM((tiles, TILE, BLOCK), BF16),
            pltpu.VMEM((tiles, TILE, BLOCK), BF16),
            pltpu.VMEM((4, TILE, BLOCK), F32),
            tiled(4),
            pltpu.VMEM((TILE, MODEL_WIDTH), BF16),
            pltpu.VMEM((width, hidden), F32),
            pltpu.VMEM((width, hidden), F32),
            pltpu.VMEM((hidden, width), F32),
            pltpu.VMEM((8, TILE), F32),
            pltpu.VMEM((3, 8, TILE), F32),
            pltpu.SemaphoreType.DMA((4, tiles)),
            pltpu.SemaphoreType.DMA((4, tiles)),
            pltpu.SemaphoreType.DMA((4, tiles)),
            pltpu.SemaphoreType.DMA((2, tiles)),
            pltpu.SemaphoreType.DMA((6, tiles)),
            pltpu.SemaphoreType.DMA((2, 3)),
        ],
        compiler_params=pltpu.CompilerParams(
            collective_id=2, has_side_effects=True, vmem_limit_bytes=VMEM_LIMIT,
            dimension_semantics=("arbitrary",),
        ),
        name="ffn",
    )(*ins, f, o, u, e, cg)


def back_kernel(
    tiles, count,
    gsend, psend, x_ref, c_ref, keep_ref, d_ref, stat_ref, gg_ref, again, fgain, wout, wq, wk, wv, wg, wr, rup,
    gown, h1, invf, f1, gz_ref, oo_ref, gated, ws1, b1, e1,
    f2, b2, ws2, e2, na, h2, pown, inva,
    gt_o, lo_o, dq_o, dk_o, dv_o, dg_o, dr_o, dwo_o, dag_o, dfg_o, dgg_o, db_o, dup_o,
    wcat, tri, rg, rp, gh, gb, gat, gzs, gw, gqd, gkd, gv, state, sbuf, rbuf,
    gcat, pn, mn, sc, rc, own, st_s, st_r, dwa, dwo,
    gsem, psem, hsem, nsem, csem, tsem, esend, erecv,
):
    i = pl.program_id(0)
    me, mate, cross, far = peers()
    place = lax.axis_index("seq")
    last = tiles - 1
    second = tiles + 3

    def rows_of(t):
        return pl.ds(pl.multiple_of(t * TILE, TILE), TILE)

    def grads(t):
        return to_head(gsend.at[rows_of(t)], rg.at[t], gsem.at[0, t], gsem.at[1, t], cross)

    def feeds(t):
        return to_head(psend.at[rows_of(t)], rp.at[t], psem.at[0, t], psem.at[1, t], cross)

    def own_mate(t):
        return to_head(gb.at[t, me], gb.at[t, me], hsem.at[0, t], hsem.at[1, t], mate)

    def own_cross(t):
        return to_head(gb.at[t, me], gb.at[t, me], hsem.at[2, t], hsem.at[3, t], cross)

    def onward(t):
        return to_head(gb.at[t, cross], gb.at[t, cross], hsem.at[4, t], hsem.at[5, t], mate)

    def pair(t, which):
        block = mate if which == 0 else far
        return to_head(pn.at[t, block], mn.at[t, which], nsem.at[2 * which, t], nsem.at[2 * which + 1, t], mate)

    def over(t):
        return to_head(sc.at[t], rc.at[t], csem.at[0, t], csem.at[1, t], cross)

    def stats(t, n, other):
        return to_head(st_s.at[t], st_r.at[t, n], tsem.at[0, n, t], tsem.at[1, n, t], other)

    @pl.when(i == 0)
    def _():
        greet_head()
        greet_seq(count)
        pl.semaphore_wait(pltpu.get_barrier_semaphore(), 3 + count - 1)
        for n in range(AHEAD):
            grads(last - n).start()
        wcat[:, 0:128] = wq[...]
        wcat[:, 128:256] = wk[...]
        wcat[:, 256:512] = wv[...]
        wcat[:, 512:768] = wg[...]
        wcat[:, 768:896] = wr[...]
        r = lax.broadcasted_iota(jnp.int32, (TILE, TILE), 0)
        c = lax.broadcasted_iota(jnp.int32, (TILE, TILE), 1)
        tri[...] = jnp.where(((r >> 6) == (c >> 6)) & (r > c), 1.0, 0.0).astype(BF16)
        state[...] = jnp.zeros_like(state)
        dwa[...] = jnp.zeros_like(dwa)
        dwo[...] = jnp.zeros_like(dwo)
        dag_o[...] = jnp.zeros_like(dag_o)
        dfg_o[...] = jnp.zeros_like(dfg_o)
        dgg_o[...] = jnp.zeros_like(dgg_o)
        db_o[...] = jnp.zeros_like(db_o)
        dup_o[...] = jnp.zeros_like(dup_o)

    @pl.when(i + AHEAD <= last)
    def _():
        grads(last - i - AHEAD).start()

    @pl.when((i >= 2) & (i - 2 <= last))
    def _():
        t = last - (i - 2)
        own_cross(t).wait_recv()
        onward(t).start()

    @pl.when(i <= last)
    def _():
        t = last - i
        grads(t).wait_recv()
        gnf = gown[...] + rg[t].astype(F32)
        inv = invf[...][:, 0:1]
        hn = h1[...].astype(BF16).astype(F32) * inv
        row = stat_ref[pl.ds(t, 1), :]
        stat = jnp.broadcast_to(row, (128, TILE)).T[:, 0:1]
        grad = c_ref[rows_of(t), :].astype(F32) + inv * (fgain[me] * gnf - hn * (stat / MODEL_WIDTH))
        dfg_o[...] += jnp.sum(gnf * hn, axis=0, keepdims=True)
        gh[t] = grad
        gb[t, me] = grad.astype(BF16)
        own_cross(t).start()
        own_mate(t).start()

    @pl.when((i >= last) & (i - last <= (tiles - 1) // 2))
    def _():
        n = 2 * (i - last)
        feeds(last - n).start()

        @pl.when(n + 1 <= last)
        def _():
            feeds(last - n - 1).start()

    @pl.when((i >= 3) & (i - 3 <= last))
    def _():
        t = last - (i - 3)
        own_mate(t).wait_recv()
        onward(t).wait_recv()
        for j in range(4):
            gat[:, j * BLOCK : (j + 1) * BLOCK] = gb[t, j]
        g = gat[...]
        gt = dot_nt(g, wout[...])
        dwo[...] += dot_tn(gated[...], g)
        o = oo_ref[...]
        gz = gz_ref[...]
        inv = lax.rsqrt(jnp.mean(o * o, axis=1, keepdims=True) + EPS)
        on = o * inv
        sig = jax.nn.sigmoid(gz)
        gn = gt * (gz * sig)
        dgg_o[...] += jnp.sum(gn * on, axis=0, keepdims=True)
        gzs[t] = (gt * on * gg_ref[...] * (sig * (1.0 + gz * (1.0 - sig)))).astype(BF16)
        p = gn * gg_ref[...]
        go = (inv * (p - on * jnp.mean(p * on, axis=1, keepdims=True))).astype(BF16)
        qd = f1[:, 0:128].astype(BF16)
        kd = f1[:, 128:256].astype(BF16)
        v = b1[:, 0:256]
        causal, _ = span_masks(TILE, TILE)
        ga = jnp.where(causal, dot_nt(go, v), 0.0).astype(BF16)
        gqd[t] = dot_nn(ga, kd)
        gkd[t] = dot_tn(ga, qd)
        gv[t] = dot_tn(b1[:, 256:512], go)
        for c in range(PER - 1, -1, -1):
            rows = slice(c * SPAN, (c + 1) * SPAN)
            gqd[t, rows, :] += dot_nn(go[rows], ws1[c])
            fresh = dot_tn(go[rows], qd[rows])
            gw[t * PER + c] = fresh
            through = keep_ref[t, c : c + 1, :] * e1[0, c : c + 1, :]
            state[...] = through * (fresh + state[...])

    @pl.when(i == last + 3)
    def _():
        sbuf[...] = jnp.zeros_like(sbuf)
        sbuf[0:HV, :] = state[...].astype(BF16)
        d = d_ref[...]
        hi = d.astype(BF16).astype(F32)
        first = lax.broadcasted_iota(jnp.int32, (16, 128), 0) < 8
        both = jnp.where(first, jnp.concatenate([hi, hi], axis=0), jnp.concatenate([d - hi, d - hi], axis=0))
        sbuf[HV : HV + 16, :] = both.astype(BF16)

        def send(p, carry):
            to_seq(sbuf, rbuf.at[place], esend.at[p], erecv.at[place], p).start()
            return carry

        lax.fori_loop(0, place, send, 0)

    @pl.when(i == second)
    def _():
        state[...] = jnp.zeros_like(state)

        def join(n, carry):
            p = count - 1 - n
            to_seq(sbuf, rbuf.at[p], esend.at[p], erecv.at[p], place).wait_recv()
            got = rbuf[p].astype(F32)
            d = got[HV : HV + 1] + got[HV + 8 : HV + 9]
            state[...] = got[0:HV] + d * state[...]
            return carry

        lax.fori_loop(0, count - 1 - place, join, 0)

    @pl.when((i >= second + 3) & (i - second - 3 <= last))
    def _():
        t = last - (i - second - 3)
        over(t).wait_recv()
        for n, other in enumerate((mate, cross, far)):
            stats(t, n, other).wait_recv()
        gna = own[lax.rem(t, 4)] + rc[t].astype(F32)
        inv = inva[...][:, 0:1]
        xn = x_ref[rows_of(t), :].astype(F32) * inv
        row = (st_s[t] + st_r[t, 0]) + (st_r[t, 1] + st_r[t, 2])
        stat = jnp.broadcast_to(row[0:1], (128, TILE)).T[:, 0:1]
        gt_o[...] = gh[t] + inv * (again[me] * gna - xn * (stat / MODEL_WIDTH))
        dag_o[...] += jnp.sum(gna * xn, axis=0, keepdims=True)

    @pl.when((i >= second + 1) & (i - second - 1 <= last))
    def _():
        t = last - (i - second - 1)
        pair(t, 0).wait_recv()
        pair(t, 1).wait_recv()
        sc[t] = (pn[t, cross].astype(F32) + mn[t, 1].astype(F32)).astype(BF16)
        over(t).start()
        own[lax.rem(t, 4)] = pn[t, me].astype(F32) + mn[t, 0].astype(F32)

    @pl.when((i >= second) & (i - second <= last))
    def _():
        t = last - (i - second)
        qf = f2[:, 0:128]
        kf = f2[:, 128:256]
        kd = kf.astype(BF16)
        pieces = [None] * PER
        for c in range(PER - 1, -1, -1):
            rows = slice(c * SPAN, (c + 1) * SPAN)
            low = state[...].astype(BF16)
            gkd[t, rows, :] += dot_nn(b2[rows, 0:256], low)
            gv[t, rows, :] += dot_nt(kd[rows], low)
            ge = gw[t * PER + c] + state[...]
            pieces[c] = jnp.broadcast_to(jnp.sum(ge * ws2[c].astype(F32), axis=0, keepdims=True), (SPAN, HK))
            state[...] = (keep_ref[t, c : c + 1, :] * e2[0, c : c + 1, :]) * ge
        gq = gqd[t]
        gk = gkd[t]
        diff = gq * qf - gk * kf
        gg = jnp.concatenate(pieces, axis=0) - fold(dot_nn(tri[...], three(diff)))
        glogit = gg * f2[:, 512:640]
        db_o[...] += jnp.sum(glogit, axis=0, keepdims=True)
        hi = glogit.astype(BF16)
        lo = (glogit - hi.astype(F32)).astype(BF16)
        glr = dot_nt(hi, rup[...]) + dot_nt(lo, rup[...])
        lr = b2[:, 512:640]
        dup_o[...] += dot_tn(lr, hi) + dot_tn(lr, lo)
        gcat[:, 0:128] = (gq * f2[:, 256:384]).astype(BF16)
        gcat[:, 128:256] = (gk * f2[:, 384:512]).astype(BF16)
        gcat[:, 256:512] = gv[t].astype(BF16)
        gcat[:, 512:768] = gzs[t]
        gcat[:, 768:896] = glr.astype(BF16)
        g = gcat[...]
        stat = jnp.zeros((TILE, 1), F32)
        for j in range(4):
            cols = slice(j * BLOCK, (j + 1) * BLOCK)
            gj = dot_nt(g, wcat[cols, :])
            stat = stat + jnp.sum(gj * na[:, cols].astype(F32), axis=1, keepdims=True)
            pn[t, j] = gj.astype(BF16)
        pair(t, 1).start()
        pair(t, 0).start()
        st_s[t] = jnp.broadcast_to(stat, (TILE, 128)).T[0:8, :]
        for n, other in enumerate((mate, cross, far)):
            stats(t, n, other).start()
        dwa[...] += dot_tn(na[...], g)

    @pl.when((i >= second) & (i - second <= last))
    def _():
        t = last - (i - second)
        feeds(t).wait_recv()
        lo_o[...] = (h2[...] + (pown[...] + rp[t].astype(F32))).astype(BF16)

    @pl.when(i == second + last + 3)
    def _():
        dq_o[...] = dwa[:, 0:128].astype(BF16)
        dk_o[...] = dwa[:, 128:256].astype(BF16)
        dv_o[...] = dwa[:, 256:512].astype(BF16)
        dg_o[...] = dwa[:, 512:768].astype(BF16)
        dr_o[...] = dwa[:, 768:896]
        dwo_o[...] = dwo[...].astype(BF16)

        def sent(p, carry):
            to_seq(sbuf, rbuf.at[place], esend.at[p], erecv.at[place], p).wait_send()
            return carry

        lax.fori_loop(0, place, sent, 0)

        def out(t, carry):
            grads(t).wait_send()
            feeds(t).wait_send()
            own_cross(t).wait_send()
            own_mate(t).wait_send()
            onward(t).wait_send()
            pair(t, 0).wait_send()
            pair(t, 1).wait_send()
            over(t).wait_send()
            for n, other in enumerate((mate, cross, far)):
                stats(t, n, other).wait_send()
            return carry

        lax.fori_loop(0, tiles, out, 0)


def back(fixed, gown, h, invf, f, o, oo, gated, ws, b, e, na, pown, inva):
    rows = h.shape[0]
    tiles = rows // TILE
    count = lax.axis_size("seq")
    second = tiles + 3
    width = MODEL_WIDTH
    ts = functools.partial(tile_spec, tiles, back=True)
    outs = [
        ((rows, BLOCK), F32, ts((TILE, BLOCK), second + 3)),
        ((rows, BLOCK), BF16, ts((TILE, BLOCK), second)),
        ((width, 128), BF16, whole((width, 128))),
        ((width, 128), BF16, whole((width, 128))),
        ((width, 256), BF16, whole((width, 256))),
        ((width, 256), BF16, whole((width, 256))),
        ((width, 128), F32, whole((width, 128))),
        ((256, width), BF16, whole((256, width))),
        ((1, 256), F32, whole((1, 256))),
        ((1, 256), F32, whole((1, 256))),
        ((1, 256), F32, whole((1, 256))),
        ((1, 128), F32, whole((1, 128))),
        ((128, 128), F32, whole((128, 128))),
    ]
    tiled = lambda n: pltpu.VMEM((tiles, n, TILE, BLOCK), BF16)
    flat = lambda n, d: pltpu.VMEM((tiles, TILE, n), d)
    return pl.pallas_call(
        functools.partial(back_kernel, tiles, count),
        grid=(second + tiles + 3,),
        out_shape=[jax.ShapeDtypeStruct(s, d) for s, d, _ in outs],
        in_specs=[whole(a.shape) for a in fixed]
        + [
            ts((TILE, BLOCK), 0), ts((TILE, BLOCK), 0), ts((TILE, 128), 0),
            ts((TILE, 256), 3), ts((TILE, 256), 3), ts((TILE, 256), 3), ts((TILE, 256), 3),
            ts((PER, HV, HK), 3), ts((TILE, 640), 3), ts((1, 8, 128), 3),
            ts((TILE, 640), second), ts((TILE, 640), second), ts((PER, HV, HK), second), ts((1, 8, 128), second),
            ts((TILE, width), second), ts((TILE, BLOCK), second), ts((TILE, BLOCK), second),
            ts((TILE, 128), second + 3),
        ],
        out_specs=[s for _, _, s in outs],
        scratch_shapes=[
            pltpu.VMEM((width, 896), BF16),
            pltpu.VMEM((TILE, TILE), BF16),
            flat(BLOCK, BF16), flat(BLOCK, BF16), flat(BLOCK, F32),
            tiled(4),
            pltpu.VMEM((TILE, width), BF16),
            flat(BLOCK, BF16),
            pltpu.VMEM((rows // SPAN, HV, HK), F32),
            flat(HK, F32), flat(HK, F32), flat(HV, F32),
            pltpu.VMEM((HV, HK), F32),
            pltpu.VMEM((HV + 16, HK), BF16),
            pltpu.VMEM((count, HV + 16, HK), BF16),
            pltpu.VMEM((TILE, 896), BF16),
            tiled(4), tiled(2), flat(BLOCK, BF16), flat(BLOCK, BF16),
            pltpu.VMEM((4, TILE, BLOCK), F32),
            pltpu.VMEM((tiles, 8, TILE), F32),
            pltpu.VMEM((tiles, 3, 8, TILE), F32),
            pltpu.VMEM((width, 896), F32),
            pltpu.VMEM((256, width), F32),
            pltpu.SemaphoreType.DMA((2, tiles)),
            pltpu.SemaphoreType.DMA((2, tiles)),
            pltpu.SemaphoreType.DMA((6, tiles)),
            pltpu.SemaphoreType.DMA((4, tiles)),
            pltpu.SemaphoreType.DMA((2, tiles)),
            pltpu.SemaphoreType.DMA((2, 3, tiles)),
            pltpu.SemaphoreType.DMA((count,)),
            pltpu.SemaphoreType.DMA((count,)),
        ],
        compiler_params=pltpu.CompilerParams(
            collective_id=3, has_side_effects=True, vmem_limit_bytes=VMEM_LIMIT,
            dimension_semantics=("arbitrary",),
        ),
        name="back",
    )(*fixed, gown, h, invf, f, o, oo, gated, ws, b, e, f, b, ws, e, na, h, pown, inva)


def shards(
    tokens,
    row_starts,
    attn_gain,
    query_weight,
    key_weight,
    value_weight,
    gate_weight,
    rank_down,
    rank_up,
    rank_bias,
    group_gain,
    out_weight,
    feed_gain,
    feed_gate,
    feed_up,
    feed_down,
    cotangent,
):
    rows = tokens.shape[0]
    tiles = rows // TILE
    spans = rows // SPAN
    span_ids = lax.axis_index("seq") * spans + jnp.arange(spans, dtype=jnp.int32)
    resets = jnp.any((row_starts // SPAN)[None, :] == span_ids[:, None], axis=1).astype(F32)
    keep = jnp.pad((1.0 - resets).reshape(tiles, PER, 1), ((0, 0), (0, 8 - PER), (0, 0)))
    keep = jnp.broadcast_to(keep, (tiles, 8, 128))
    wide = jnp.pad(rank_down[0], ((0, 0), (0, 128 - RANK)))
    tall = jnp.pad(rank_up[0], ((0, 128 - RANK), (0, 0)))
    weights = (query_weight[0], key_weight[0], value_weight[0], gate_weight[0], wide, tall)
    again = attn_gain.astype(F32)
    fgain = feed_gain.astype(F32)
    ggain = group_gain.astype(F32)
    na, cg, inva, f, b, o, u, e, inc, dec = front(
        tokens, cotangent, keep, again, *weights, rank_bias.astype(F32)
    )
    gated, oo, ws, h, invf, gsend, gown, psend, pown, stat, dfg, dfu, dfd = ffn(
        tokens, keep, inc, ggain, fgain, out_weight[0], feed_gate[0], feed_up[0], feed_down[0], f, o, u, e, cg
    )
    dfg, dfu, dfd = lax.psum((dfg, dfu, dfd), "seq")
    fixed = (
        gsend, psend, tokens, cotangent, keep, dec, stat, ggain, again.reshape(4, 1, BLOCK), fgain.reshape(4, 1, BLOCK),
        out_weight[0],
    ) + weights
    grad_tokens, layer_out, dq, dk, dv, dg, dr, dwo, dag, dffg, dgg, db, dup = back(
        fixed, gown, h, invf, f, o, oo, gated, ws, b, e, na, pown, inva
    )
    dq, dk, dv, dg, dwo, dfg, dfu, dfd = lax.optimization_barrier((dq, dk, dv, dg, dwo, dfg, dfu, dfd))
    dr = dr[:, 0:RANK].T.reshape(128, 128)
    dr, dgg = lax.psum((dr.astype(BF16), dgg.astype(BF16)), "head")
    dq, dk, dv, dg, dwo, dr, dgg, dag, dffg, db, dup = lax.psum(
        (dq, dk, dv, dg, dwo, dr, dgg, dag.astype(BF16), dffg.astype(BF16), db.astype(BF16), dup[0:RANK].astype(BF16)),
        "seq",
    )
    dr = dr.reshape(RANK, MODEL_WIDTH).T
    grads = (dag, dq[None], dk[None], dv[None], dg[None], dr[None], dup[None], db, dgg, dwo[None], dffg, dfg[None], dfu[None], dfd[None])
    return (layer_out, grad_tokens) + tuple(g.astype(F32) for g in grads)


def solution(mesh):
    placed = (
        P("seq", "head"),
        P(),
        P(),
        P(None, None, "head"),
        P(None, None, "head"),
        P(None, None, "head"),
        P(None, None, "head"),
        P(),
        P(None, None, "head"),
        P(None, "head"),
        P(),
        P(None, "head", None),
        P(),
        P(None, None, "head"),
        P(None, None, "head"),
        P(None, "head", None),
        P("seq", "head"),
    )
    return jax.shard_map(
        shards,
        mesh=mesh,
        in_specs=placed,
        out_specs=(
            P("seq", "head"),
            P("seq", "head"),
            P(None, "head"),
            P(None, None, "head"),
            P(None, None, "head"),
            P(None, None, "head"),
            P(None, None, "head"),
            P(),
            P(None, None, "head"),
            P(None, "head"),
            P(),
            P(None, "head", None),
            P(None, "head"),
            P(None, None, "head"),
            P(None, None, "head"),
            P(None, "head", None),
        ),
        check_vma=False,
    )
```

time: 997 us -> 449 us (0.45)
  waiting for transfers between devices: 332 us -> 105 us
  Pallas kernels: 58.7 us -> 239 us
  matrix products: 134 us -> 0 us
  other arithmetic: 158 us -> 24.7 us
  local copies, waits for them, and re-layouts: 129 us -> 16.8 us
  blocking collectives: 116 us -> 48.7 us
  loops' own time: 44.3 us -> 0 us
    pallas_call x0 -> x2, Pallas kernels: none -> 180 us  [the longest x1 105 us: back(): pl.pallas_call(functools.partial(back_kernel, tiles, count), grid=(second...]
    dot_general x33 -> x0, matrix products: 134 us -> none  [the longest x8 44.4 us: cols_product(): lax.dot_general(left, right, (((1,), (1,)), ((), ())), preferred_element_...]
    reduce_scatter x5 -> x0, waiting for transfers between devices: 101 us -> none  [the longest x2 42.8 us: reduce_partial(): lax.psum_scatter(partial_value.astype(jnp.bfloat16), 'head', scatter_dime...]
    psum x1 -> x2, waiting for transfers between devices: 197 us -> 105 us  [the longest x1 62.9 us: shards(): dfg, dfu, dfd = lax.psum((dfg, dfu, dfd), 'seq')]
    dynamic_slice x130 -> x0, local copies, waits for them, and re-layouts: 71.7 us -> none  [the longest x128 70 us: core_forward(): lax.scan(forward_step, inc.T[None], (resets, decay_end, state_update))]
    all_gather x2 -> x0, blocking collectives: 54.7 us -> none  [carried_in(): lax.all_gather(a.astype(kind), axis)]
    another operation x3 -> x0, loops' own time: 44.3 us -> none  [the longest x1 22.2 us: core_forward(): lax.scan(forward_step, inc.T[None], (resets, decay_end, state_update))]
    dynamic_update_slice x64 -> x0, other arithmetic: 42.5 us -> none  [core_forward(): lax.scan(forward_step, inc.T[None], (resets, decay_end, state_update))]
  transfers between devices with their start and end apart: 10 -> 2, of which waited for: 5 -> 2; matrix products, arithmetic and copies ran while one was open for 27% -> 4% of each run, Pallas kernels for 0% -> 23%
where the time goes in v2:
time: 449 us
  Pallas kernels  239 us (53%)
  waiting for transfers between devices  105 us (23%)
  blocking collectives  48.7 us (11%)
  other arithmetic  24.7 us (6%)
  local copies, waits for them, and re-layouts  16.8 us (4%)
  between operations  14.3 us (3%)
    pallas_call x1, Pallas kernels, back(): pl.pallas_call(functools.partial(back_kernel, tiles, count), grid=(second...  105 us
    pallas_call x1, Pallas kernels, ffn(): pl.pallas_call(functools.partial(ffn_kernel, tiles), grid=(tiles + 7,), o...  74.6 us
    psum x1, waiting for transfers between devices, shards(): dfg, dfu, dfd = lax.psum((dfg, dfu, dfd), 'seq')  62.9 us
    pallas_call x1, Pallas kernels, front(): pl.pallas_call(functools.partial(front_kernel, tiles, count), grid=(2 * t...  58.8 us
    psum x1, waiting for transfers between devices, shards(): lax.psum((dq, dk, dv, dg, dwo, dr, dgg, dag.astype(BF16), dffg.astype(BF1...  42.3 us
    psum x1, blocking collectives, shards(): lax.psum((dq, dk, dv, dg, dwo, dr, dgg, dag.astype(BF16), dffg.astype(BF1...  37 us
    convert_element_type x13, other arithmetic, shards(): return (layer_out, grad_tokens) + tuple((g.astype(F32) for g in grads))  18.8 us
    unnamed x27, local copies, waits for them, and re-layouts  13 us
  transfers between devices with their start and end apart: 2, of which 2 were waited for; matrix products, arithmetic and copies ran while one was open for 4% of the time, Pallas kernels for 23%

profile of v2, /device:TPU:0, one launch (start us, length us, event | category | flops | bytes accessed | tf_op | source)
XLA Modules:
  0.0 448.6 jit_solution(4323541230212334805)
XLA Ops:
  8.1 1.2 convert_element_type.129.bias_ref
  9.3 1.2 convert_element_type.130.gg_ref
  10.6 1.3 convert_element_type.128.gain_ref
  11.9 1.3 convert_element_type.131.gain_ref
  14.1 1.3 pad.14.rup
  16.2 2.6 copy.45
  18.7 1.6 copy.46
  21.0 58.8 %front.1 = (bf16[2048,1024]{1,0:T(8,128)(2,1)}, bf16[2048,1024]{1,0:T(8,128)(2,1)}, f32[2048,128]{1,0:T(8,128)}, f32[2048,640]{1,0:T(8,128)}, bf16[2048,640]{1,0...) custom-call(bf16[2048,256]{1,0:T(8,128)(2,1)} %x_ref.5, ...), custom_call_target="tpu_custom_call" | custom-call | tf_op jit(solution)/shard_map/front/pallas_call | solution.py:290
  79.8 74.6 %ffn.1 = (bf16[2048,256]{1,0:T(8,128)(2,1)}, f32[2048,256]{1,0:T(8,128)}, bf16[32,256,128]{2,1,0:T(8,128)(2,1)}, f32[2048,256]{1,0:T(8,128)}, f32[2048,128]{1,0:...) custom-call(bf16[2048,256]{1,0:T(8,128)(2,1)} %x_ref.5, ...), custom_call_target="tpu_custom_call" | custom-call | tf_op jit(solution)/shard_map/ffn/pallas_call | solution.py:517
  154.7 105.3 %back.1 = (f32[2048,256]{1,0:T(8,128)}, bf16[2048,256]{1,0:T(8,128)(2,1)}, bf16[1024,128]{1,0:T(8,128)(2,1)}, bf16[1024,128]{1,0:T(8,128)(2,1)}, bf16[1024,256]{...) custom-call(bf16[2048,256]{1,0:T(8,128)(2,1)} %get-tuple-element.66., ...), custom_call_target="tpu_custom_call" | custom-call | tf_op jit(solution)/shard_map/back/pallas_call | solution.py:853
  260.0 62.9 %all-reduce.12.cloned.1.call-done = (bf16[1024,704]{1,0:T(8,128)(2,1)}, bf16[1024,704]{1,0:T(8,128)(2,1)}, bf16[704,1024]{1,0:T(8,128)(2,1)}) async-done(((bf16[1024,704]{1,0:T(8,128)(2,1)}, bf16[1024,704]{1,0:T(8,128)(2,1)}, bf16[704,1024]{1,0:T(8,128)(2,1)}), (bf16[1024,704]{1,0:T(8,128)(2,1)}, bf16[1024,704]{1,0:T(8,128)(2,1)}, bf16[704,1024]{1,0:T(8,128)(2,1)})) %all-reduce.12.cloned.1.call-update) | async-done | bytes 4325392 | tf_op jit(solution)/shard_map/psum | solution.py:941
  323.2 11.7 %all-reduce.6 = (bf16[128,128]{1,0:T(8,128)(2,1)S(1)}, bf16[1,256]{1,0:T(2,128)(2,1)S(1)}) all-reduce(bf16[128,128]{1,0:T(8,128)(2,1)S(1)} %convert_element_type.143, bf16[1,256]{1,0:T(2,128)(2,1)S(1)} %convert_element_type.152), channel_id=1, replica_groups=mesh['seq'=8,'head'=4] {'head'}, use_global_device_ids=true, to_apply=%region_9.10 | all-reduce | flops 16640 | bytes 66560 | tf_op jit(solution)/shard_map/psum | solution.py:951
  335.6 37.0 %all-reduce.3 = (bf16[1,256]{1,0:T(2,128)(2,1)S(1)}, bf16[1,1024,16]{1,2,0:T(8,128)(2,1)S(1)}, bf16[1,16,128]{2,1,0:T(8,128)(2,1)S(1)}, bf16[1,128]{1,0:T(2,128)...) all-reduce(bf16[1,256]{1,0:T(2,128)(2,1)S(1)} %convert_element_type, ...), channel_id=1, replica_groups=mesh['seq'=8,'head'=4] {'seq'}, use_global_device_ids=true, to_apply=%region_1.2 | all-reduce | flops 19328 | bytes 77312 | tf_op jit(solution)/shard_map/psum | solution.py:952
  376.1 4.1 bitcast_convert_fusion
  380.2 3.4 copy.49
  383.6 2.2 copy.48
  385.9 3.3 bitcast_convert_fusion.2
  389.2 42.3 %all-reduce.10.cloned.1.call-done = (bf16[1,1024,128]{2,1,0:T(8,128)(2,1)}, bf16[1,1024,128]{2,1,0:T(8,128)(2,1)}, bf16[1,1024,256]{2,1,0:T(8,128)(2,1)}, bf16[1...) async-done(((bf16[1,1024,128]{2,1,0:T(8,128)(2,1)}, bf16[1,1024,128]{2,1,0:T(8,128)(2,1)}, bf16[1,1024,256]{2,1,0:T(8,128)(2,1)}, bf16[1,1024,256]{2,1,0:T(8,128)(2,1)}, ...) | async-done | bytes 2097168 | tf_op jit(solution)/shard_map/psum | solution.py:952
  431.5 1.8 convert_element_type.135
  433.4 1.8 convert_element_type.137
  435.2 2.2 convert_element_type.139
  437.4 1.0 convert_element_type.141
  438.4 1.1 convert_element_type.155
  440.5 1.3 copy.61
  (49 shorter events, 9.0 us)
Async XLA Ops:
  7.2 11.6 %copy-start.1 = (bf16[1,1024,704]{1,2,0:T(8,128)(2,1)S(1)}, bf16[1,1024,704]{1,2,0:T(8,128)(2,1)}, u32[]{:S(2)}) copy-start(bf16[1,1024,704]{1,2,0:T(8,128)(2,1)} %param.31) | copy-start | bytes 4325380
  7.2 315.7 %all-reduce.12.cloned.1.call-start = ((), (), s32[]{:S(2)}) async-start(), calls=%async_computation.1 | async-start | bytes 9175040 | tf_op jit(solution)/shard_map/psum | solution.py:941
  154.4 277.1 %all-reduce.10.cloned.1.call-start = ((), (), s32[]{:S(2)}) async-start(), calls=%async_computation | async-start | bytes 4194304 | tf_op jit(solution)/shard_map/psum | solution.py:952
  260.0 63.0 %copy-start.9 = (f32[1,128]{1,0:T(1,128)S(1)}, f32[1,128]{1,0:T(1,128)}, u32[]{:S(2)}) copy-start(f32[1,128]{1,0:T(1,128)} %get-tuple-element.97) | copy-start | bytes 1540
  260.0 63.0 %copy-start.8 = (f32[1,256]{1,0:T(1,128)S(1)}, f32[1,256]{1,0:T(1,128)}, u32[]{:S(2)}) copy-start(f32[1,256]{1,0:T(1,128)} %get-tuple-element.82) | copy-start | bytes 3076
  260.0 63.0 %copy-start.7 = (f32[1,256]{1,0:T(1,128)S(1)}, f32[1,256]{1,0:T(1,128)}, u32[]{:S(2)}) copy-start(f32[1,256]{1,0:T(1,128)} %get-tuple-element.98) | copy-start | bytes 3076
  260.0 63.0 %copy-start.6 = (f32[1,256]{1,0:T(1,128)S(1)}, f32[1,256]{1,0:T(1,128)}, u32[]{:S(2)}) copy-start(f32[1,256]{1,0:T(1,128)} %get-tuple-element.100) | copy-start | bytes 3076
  260.0 63.0 %copy-start.5 = (f32[1024,128]{1,0:T(8,128)S(1)}, f32[1024,128]{1,0:T(8,128)}, u32[]{:S(2)}) copy-start(f32[1024,128]{1,0:T(8,128)} %get-tuple-element.95) | copy-start | bytes 1572868
  431.5 5.9 %copy-start.4 = (bf16[1,1024,256]{2,1,0:T(8,128)(2,1)S(1)}, bf16[1,1024,256]{2,1,0:T(8,128)(2,1)}, u32[]{:S(2)}) copy-start(bf16[1,1024,256]{2,1,0:T(8,128)(2,1)} %get-tuple-element.161) | copy-start | bytes 1572868
  433.4 5.1 %copy-start.3 = (bf16[1,256,1024]{2,1,0:T(8,128)(2,1)S(1)}, bf16[1,256,1024]{2,1,0:T(8,128)(2,1)}, u32[]{:S(2)}) copy-start(bf16[1,256,1024]{2,1,0:T(8,128)(2,1)} %get-tuple-element.162) | copy-start | bytes 1572868
  435.2 4.3 copy-start.2
  438.4 2.1 copy-start
Sparse Core Ops, SparseCore 0:
  154.6 168.3 all-reduce.11
  327.1 104.3 all-reduce.9

commit v3 on v2

--- a/solution.py
+++ b/solution.py
@@ -21,7 +21,7 @@
 F32 = jnp.float32
 BF16 = jnp.bfloat16
 MESH = pl.DeviceIdType.MESH
-VMEM_LIMIT = 60 * 1024 * 1024
+VMEM_LIMIT = 62 * 1024 * 1024
 
 
 def dot_nn(a, b):
@@ -137,7 +137,6 @@
         wcat[:, 128:256] = wk[...]
         wcat[:, 256:512] = wv[...]
         wcat[:, 512:768] = wg[...]
-        wcat[:, 768:896] = wr[...]
         causal, same = span_masks(TILE, TILE)
         tri[0:TILE, :] = jnp.where(causal, 1.0, 0.0).astype(BF16)
         tri[TILE : 2 * TILE, :] = jnp.where(same, 1.0, 0.0).astype(BF16)
@@ -171,14 +170,14 @@
         for j in range(4):
             cols = slice(j * BLOCK, (j + 1) * BLOCK)
             xj = grid_buf[m, j].astype(F32)
-            na_o[:, cols] = (xj * inv * gain_ref[:, cols]).astype(BF16)
+            na_o[:, cols] = (xj * inv * gain_ref[:, cols].astype(F32)).astype(BF16)
         proj = dot_nn(na_o[...], wcat[...])
         q = proj[:, 0:128]
         k = proj[:, 128:256]
         v = proj[:, 256:512].astype(BF16)
         o_o[:, 0:256] = proj[:, 512:768]
-        lr = proj[:, 768:896].astype(BF16)
-        z = dot_nn(lr, rup[...]) + bias_ref[...]
+        lr = dot_nt(na_o[...], wr[...]).astype(BF16)
+        z = dot_nn(lr, rup[...]) + bias_ref[...].astype(F32)
         g = (jnp.minimum(z, 0.0) - jnp.log1p(jnp.exp(-jnp.abs(z)))) / GATE_NORM
         sums = fold(dot_nn(tri[...], three(g)))
         b = sums[0:TILE]
@@ -198,7 +197,7 @@
         scores = jnp.where(causal, dot_nt(qd, kd), 0.0).astype(BF16)
         b_o[:, 0:256] = v
         b_o[:, 256:512] = scores
-        b_o[:, 512:640] = lr
+        b_o[:, 512 : 512 + RANK] = lr
         o_o[:, 256:512] = dot_nn(scores, v)
         for c in range(PER):
             rows = slice(c * SPAN, (c + 1) * SPAN)
@@ -295,7 +294,7 @@
         out_specs=[s for _, _, s in outs],
         scratch_shapes=[
             pltpu.VMEM((2 * tiles, 4, TILE, BLOCK), BF16),
-            pltpu.VMEM((MODEL_WIDTH, 896), BF16),
+            pltpu.VMEM((MODEL_WIDTH, 768), BF16),
             pltpu.VMEM((2 * TILE, TILE), BF16),
             pltpu.VMEM((HV, HK), F32),
             pltpu.VMEM((8, 128), F32),
@@ -323,17 +322,22 @@
     return pl.BlockSpec(shape, index)
 
 
+def up_to(n, step):
+    return (n + step - 1) // step * step
+
+
 def ffn_kernel(
     tiles,
     x_ref, keep_ref, in_ref, gg_ref, gain_ref, wout, wfg, wfu, wfd,
     f_ref, o_ref, u_ref, e_ref, cg_ref,
-    gated_o, oo_o, ws_o, h_o, inv_o, gsend_o, gown_o, psend_o, pown_o, stat_o, dg_o, du_o, dd_o,
-    state, pa, pp, pg, ma, mp, mg, sc, rc, own, hg, nf_s, ag, au, ad, st_s, st_r,
+    gated_o, oo_o, ws_o, h_o, inv_o, gsend_o, gown_o, psend_o, pown_o, stat_o, wide_o,
+    state, pa, pp, pg, ma, mp, mg, sc, rc, own, hg, nf_s, acc, st_s, st_r,
     asem, psem, gsem, csem, hsem, tsem,
 ):
     i = pl.program_id(0)
     me, mate, cross, far = peers()
     last = tiles - 1
+    hidden = wfg.shape[0]
 
     def pair(buf, got, sem, t, which):
         block = mate if which == 0 else far
@@ -358,9 +362,7 @@
     def _():
         greet_head()
         state[...] = in_ref[...]
-        ag[...] = jnp.zeros_like(ag)
-        au[...] = jnp.zeros_like(au)
-        ad[...] = jnp.zeros_like(ad)
+        acc[...] = jnp.zeros_like(acc)
         st_s[...] = jnp.zeros_like(st_s)
         pl.semaphore_wait(pltpu.get_barrier_semaphore(), 3)
 
@@ -403,7 +405,7 @@
         o = oo_o[...]
         gz = o_ref[:, 0:256]
         inv = lax.rsqrt(jnp.mean(o * o, axis=1, keepdims=True) + EPS)
-        gated = (o * inv * gg_ref[...] * (gz * jax.nn.sigmoid(gz))).astype(BF16)
+        gated = (o * inv * gg_ref[...].astype(F32) * (gz * jax.nn.sigmoid(gz))).astype(BF16)
         gated_o[...] = gated
         for j in range(4):
             pa[t, j] = dot_nn(gated, wout[:, j * BLOCK : (j + 1) * BLOCK]).astype(BF16)
@@ -434,10 +436,10 @@
         inv_o[...] = jnp.broadcast_to(inv, (TILE, 128))
         for j in range(4):
             cols = slice(j * BLOCK, (j + 1) * BLOCK)
-            nf_s[:, cols] = (hg[t, j].astype(F32) * inv * gain_ref[:, cols]).astype(BF16)
+            nf_s[:, cols] = (hg[t, j].astype(F32) * inv * gain_ref[:, cols].astype(F32)).astype(BF16)
         nf = nf_s[...]
-        fg = dot_nn(nf, wfg[...])
-        fu = dot_nn(nf, wfu[...])
+        fg = dot_nt(nf, wfg[...])
+        fu = dot_nt(nf, wfu[...])
         sig = jax.nn.sigmoid(fg)
         silu = fg * sig
         act = (silu * fu).astype(BF16)
@@ -452,15 +454,15 @@
         stat = jnp.zeros((TILE, 1), F32)
         for j in range(4):
             rows = slice(j * BLOCK, (j + 1) * BLOCK)
-            gj = dot_nt(gfg, wfg[rows, :]) + dot_nt(gfu, wfu[rows, :])
+            gj = dot_nn(gfg, wfg[:, rows]) + dot_nn(gfu, wfu[:, rows])
             stat = stat + jnp.sum(gj * nf_s[:, rows].astype(F32), axis=1, keepdims=True)
             pg[t, j] = gj.astype(BF16)
         for which in range(2):
             pair(pg, mg, gsem, t, which).start()
         st_s[pl.ds(t, 1), :] = jnp.broadcast_to(stat, (TILE, 128)).T[0:1, :]
-        ad[...] += dot_tn(act, cg)
-        ag[...] += dot_tn(nf, gfg)
-        au[...] += dot_tn(nf, gfu)
+        acc[0:hidden, :] += dot_tn(gfg, nf)
+        acc[hidden : 2 * hidden, :] += dot_tn(gfu, nf)
+        acc[2 * hidden : 3 * hidden, :] += dot_tn(act, cg)
 
     @pl.when(i == last + 6)
     def _():
@@ -469,9 +471,15 @@
 
     @pl.when(i == last + 7)
     def _():
-        dg_o[...] = ag[...].astype(BF16)
-        du_o[...] = au[...].astype(BF16)
-        dd_o[...] = ad[...].astype(BF16)
+        used = 3 * hidden // 16
+
+        def unit(r, carry):
+            wide_o[r] = acc[pl.ds(pl.multiple_of(r * 16, 16), 16), :].astype(BF16)
+            return carry
+
+        lax.fori_loop(0, used, unit, 0)
+        if wide_o.shape[0] > used:
+            wide_o[used:] = jnp.zeros((wide_o.shape[0] - used,) + wide_o.shape[1:], BF16)
         for n, other in enumerate((mate, cross, far)):
             stats(n, other).wait()
         stat_o[...] = (st_s[...] + st_r[0]) + (st_r[1] + st_r[2])
@@ -493,9 +501,10 @@
 def ffn(x, keep, inc, gg, gain, wout, wfg, wfu, wfd, f, o, u, e, cg):
     rows = x.shape[0]
     tiles = rows // TILE
-    hidden = wfg.shape[1]
-    width = wfg.shape[0]
-    assert tiles <= 8
+    hidden, width = wfg.shape
+    count = lax.axis_size("seq")
+    units = up_to(3 * hidden // 16, count)
+    assert tiles <= 8 and hidden % 16 == 0
     ts = functools.partial(tile_spec, tiles)
     ins = (x, keep, inc, gg, gain, wout, wfg, wfu, wfd)
     outs = [
@@ -509,9 +518,7 @@
         ((rows, BLOCK), BF16, ts((TILE, BLOCK), 7)),
         ((rows, BLOCK), F32, ts((TILE, BLOCK), 7)),
         ((8, TILE), F32, whole((8, TILE))),
-        ((width, hidden), BF16, whole((width, hidden))),
-        ((width, hidden), BF16, whole((width, hidden))),
-        ((hidden, width), BF16, whole((hidden, width))),
+        ((units, 16, width), BF16, whole((units, 16, width))),
     ]
     tiled = lambda n: pltpu.VMEM((tiles, n, TILE, BLOCK), BF16)
     return pl.pallas_call(
@@ -532,9 +539,7 @@
             pltpu.VMEM((4, TILE, BLOCK), F32),
             tiled(4),
             pltpu.VMEM((TILE, MODEL_WIDTH), BF16),
-            pltpu.VMEM((width, hidden), F32),
-            pltpu.VMEM((width, hidden), F32),
-            pltpu.VMEM((hidden, width), F32),
+            pltpu.VMEM((3 * hidden, width), F32),
             pltpu.VMEM((8, TILE), F32),
             pltpu.VMEM((3, 8, TILE), F32),
             pltpu.SemaphoreType.DMA((4, tiles)),
@@ -552,15 +557,196 @@
     )(*ins, f, o, u, e, cg)
 
 
+LAG = 2
+
+
+def levels(count):
+    bits = count.bit_length() - 1
+    assert 1 << bits == count
+    return bits
+
+
+class Sum:
+    def __init__(self, count, sources, dest, parts, first, gap, got, sems, lsem):
+        self.count = count
+        self.bits = levels(count)
+        self.sources = sources
+        self.dest = dest
+        self.parts = parts
+        self.first = first
+        self.gap = gap
+        self.got = got
+        self.sems = sems
+        self.lsem = lsem
+
+    def where(self, k, level):
+        place = lax.axis_index("seq")
+        turn = lax.div(lax.rem(k, 4), 3)
+        start = 0
+        for step in range(level + 1):
+            stride = 1 << step
+            if step < 2:
+                stride = stride + turn * (3 - 2 * stride)
+            bit = lax.rem(lax.div(place, stride), 2)
+            if step == level:
+                return bit, place + stride * (1 - 2 * bit), start
+            start = start + bit * (self.count >> (step + 1))
+
+    def own(self, k):
+        bit, _, _ = self.where(k, 0)
+        half = self.count >> 1
+        return pltpu.make_async_copy(
+            self.sources[0](k, bit * half, half), self.dest(k, bit * half, half), self.lsem.at[k]
+        )
+
+    def scatter(self, k, level, kind):
+        bit, partner, start = self.where(k, level)
+        half = self.count >> (level + 1)
+        if level == 0:
+            src = self.sources[kind](k, start + (1 - bit) * half, half)
+        else:
+            src = self.got[level - 1].at[k, pl.ds((1 - bit) * half, half)]
+        return to_seq(src, self.got[level].at[k], self.sems.at[0, level, k], self.sems.at[1, level, k], partner)
+
+    def gather(self, k, level):
+        bit, partner, start = self.where(k, level)
+        half = self.count >> (level + 1)
+        mine = start + bit * half
+        ref = self.dest(k, mine, half)
+        return to_seq(ref, ref, self.sems.at[2, level, k], self.sems.at[3, level, k], partner)
+
+    def gathered(self, k, level):
+        bit, partner, start = self.where(k, level)
+        half = self.count >> (level + 1)
+        ref = self.dest(k, start + (1 - bit) * half, half)
+        return to_seq(ref, ref, self.sems.at[2, level, k], self.sems.at[3, level, k], partner)
+
+    def begin(self, k, kind):
+        self.scatter(k, 0, kind).start()
+        if kind == 0:
+            self.own(k).start()
+
+    def add(self, k, kind, level):
+        bit, _, start = self.where(k, level)
+        half = self.count >> (level + 1)
+        self.scatter(k, level, kind).wait_recv()
+        if level == 0 and kind == 0:
+            self.own(k).wait()
+            mine = self.dest(k, bit * half, half)[...]
+        elif level == 0:
+            mine = self.sources[1](k, bit * half, half)[...]
+        else:
+            mine = self.got[level - 1][k, pl.ds(bit * half, half)]
+        total = (self.got[level][k].astype(F32) + mine.astype(F32)).astype(BF16)
+        if level + 1 < self.bits:
+            self.got[level][k] = total
+            self.scatter(k, level + 1, kind).start()
+        else:
+            self.dest(k, start + bit * half, half)[...] = total
+            self.gather(k, level).start()
+
+    def pass_on(self, k, kind, level):
+        self.gathered(k, level).wait_recv()
+        if level > 0:
+            self.gather(k, level - 1).start()
+
+    def at(self, j, body):
+        @pl.when((j >= 0) & (j < self.first))
+        def _():
+            body(j, 0)
+
+        @pl.when((j >= self.first + self.gap) & (j < self.parts + self.gap))
+        def _():
+            body(j - self.gap, 1)
+
+    def step(self, i):
+        stages = []
+        for level in range(self.bits):
+            stages.append(functools.partial(self.add, level=level))
+        for level in range(self.bits - 1, -1, -1):
+            stages.append(functools.partial(self.pass_on, level=level))
+        for s in range(len(stages) - 1, -1, -1):
+            self.at(i - LAG * (s + 1), stages[s])
+        self.at(i, self.begin)
+
+    def finish(self):
+        def one(kind, k, carry):
+            for level in range(self.bits):
+                self.scatter(k, level, kind).wait_send()
+                self.gather(k, level).wait_send()
+            return carry
+
+        lax.fori_loop(0, self.first, functools.partial(one, 0), 0)
+        lax.fori_loop(self.first, self.parts, functools.partial(one, 1), 0)
+
+    @staticmethod
+    def scratch(count, parts, first, unit):
+        bits = levels(count)
+        return [pltpu.VMEM((parts, count >> (level + 1)) + unit, BF16) for level in range(bits)] + [
+            pltpu.SemaphoreType.DMA((4, bits, parts)),
+            pltpu.SemaphoreType.DMA((first,)),
+        ]
+
+
+def finish_kernel(fg, fu, fd, mixed, tail, dfg, dfu, dfd, dq, dk, dv, dg, dwo, dr, dup, dag, dffg, db, dgg):
+    for src, dst in ((fg, dfg), (fu, dfu), (fd, dfd)):
+        dst[...] = src[...].reshape(dst.shape).astype(F32)
+    rows = mixed[...].reshape(-1, MODEL_WIDTH).astype(F32)
+    dq[...] = rows[:, 0:128]
+    dk[...] = rows[:, 128:256]
+    dv[...] = rows[:, 256:512]
+    dg[...] = rows[:, 512:768]
+    dwo[...] = rows[:, 768:1024].T
+    dr[...] = tail[0].astype(F32)
+    last = tail[1].astype(F32)
+    dup[...] = last[:, 0:128]
+    dag[...] = last[0:1, 128:384]
+    dffg[...] = last[1:2, 128:384]
+    db[...] = last[3:4, 128:256]
+    dgg[...] = last[2:3, 128:384]
+
+
+def finish(units, hidden, first):
+    width = units.shape[2]
+    steps = 4
+    per = hidden // 16 // steps
+    assert per * steps * 16 == hidden
+    rows = MODEL_WIDTH // steps
+    wide_spec = lambda n: pl.BlockSpec((per, 16, width), lambda i: (i + n * steps, 0, 0))
+    down = lambda r, c: ((r * steps, c), pl.BlockSpec((r, c), lambda i: (i, 0)))
+    full = lambda r, c: ((r, c), pl.BlockSpec((r, c), lambda i: (0, 0)))
+    outs = [
+        down(per * 16, width), down(per * 16, width), down(per * 16, width),
+        down(rows, 128), down(rows, 128), down(rows, 256), down(rows, 256),
+        ((256, MODEL_WIDTH), pl.BlockSpec((256, rows), lambda i: (0, i))),
+        full(RANK, MODEL_WIDTH), full(RANK, 128), full(1, 256), full(1, 256), full(1, 128), full(1, 256),
+    ]
+    return pl.pallas_call(
+        finish_kernel,
+        grid=(steps,),
+        out_shape=[jax.ShapeDtypeStruct(s, F32) for s, _ in outs],
+        in_specs=[
+            wide_spec(0), wide_spec(1), wide_spec(2),
+            pl.BlockSpec((pl.Element(rows // 16), pl.Element(16), pl.Element(width)), lambda i: (first + i * (rows // 16), 0, 0)),
+            pl.BlockSpec((pl.Element(2), pl.Element(16), pl.Element(width)), lambda i: (first + MODEL_WIDTH // 16, 0, 0)),
+        ],
+        out_specs=[s for _, s in outs],
+        compiler_params=pltpu.CompilerParams(
+            vmem_limit_bytes=VMEM_LIMIT, dimension_semantics=("arbitrary",)
+        ),
+        name="finish",
+    )(units, units, units, units, units)
+
+
 def back_kernel(
-    tiles, count,
-    gsend, psend, x_ref, c_ref, keep_ref, d_ref, stat_ref, gg_ref, again, fgain, wout, wq, wk, wv, wg, wr, rup,
-    gown, h1, invf, f1, gz_ref, oo_ref, gated, ws1, b1, e1,
-    f2, b2, ws2, e2, na, h2, pown, inva,
-    gt_o, lo_o, dq_o, dk_o, dv_o, dg_o, dr_o, dwo_o, dag_o, dfg_o, dgg_o, db_o, dup_o,
-    wcat, tri, rg, rp, gh, gb, gat, gzs, gw, gqd, gkd, gv, state, sbuf, rbuf,
-    gcat, pn, mn, sc, rc, own, st_s, st_r, dwa, dwo,
-    gsem, psem, hsem, nsem, csem, tsem, esend, erecv,
+    tiles, count, gap,
+    keep_ref, d_ref, stat_ref, gg_ref, again, fgain, wout, wq, wk, wv, wg, wr, rup,
+    wide_in, gsend, psend, x_ref, c_ref, gown, h1, invf, f1, gz_ref, oo_ref, gated, ws1, b1, e1,
+    na1, f2, b2, ws2, e2, na, h2, pown, inva,
+    gt_o, lo_o, units_o,
+    tri, rg, gh, gb, gzs, gw, gqd, gkd, gv, state, sbuf, rbuf,
+    gcat, mn, sc, rc, own, st_s, st_r, both, joint, small, held, wide_o, lot,
+    gsem, psem, hsem, nsem, csem, tsem, esend, erecv, wsem, jsem, *rest,
 ):
     i = pl.program_id(0)
     me, mate, cross, far = peers()
@@ -571,11 +757,14 @@
     def rows_of(t):
         return pl.ds(pl.multiple_of(t * TILE, TILE), TILE)
 
+    def own_cols(ref):
+        return ref[:, pl.ds(pl.multiple_of(me * BLOCK, BLOCK), BLOCK)].astype(F32)
+
     def grads(t):
         return to_head(gsend.at[rows_of(t)], rg.at[t], gsem.at[0, t], gsem.at[1, t], cross)
 
     def feeds(t):
-        return to_head(psend.at[rows_of(t)], rp.at[t], psem.at[0, t], psem.at[1, t], cross)
+        return to_head(psend.at[rows_of(t)], rg.at[t], psem.at[0, t], psem.at[1, t], cross)
 
     def own_mate(t):
         return to_head(gb.at[t, me], gb.at[t, me], hsem.at[0, t], hsem.at[1, t], mate)
@@ -588,13 +777,28 @@
 
     def pair(t, which):
         block = mate if which == 0 else far
-        return to_head(pn.at[t, block], mn.at[t, which], nsem.at[2 * which, t], nsem.at[2 * which + 1, t], mate)
+        return to_head(gb.at[t, block], mn.at[t, which], nsem.at[2 * which, t], nsem.at[2 * which + 1, t], mate)
 
     def over(t):
         return to_head(sc.at[t], rc.at[t], csem.at[0, t], csem.at[1, t], cross)
 
     def stats(t, n, other):
         return to_head(st_s.at[t], st_r.at[t, n], tsem.at[0, n, t], tsem.at[1, n, t], other)
+
+    first = wide_in.shape[0] // count
+    parts = wide_o.shape[0] // count
+    ready = second + tiles
+
+    def early(k, start, n):
+        return wide_in.at[pl.ds(k * count + start, n)]
+
+    def late(k, start, n):
+        return lot.at[pl.ds((k - first) * count + start, n)]
+
+    def some(k, start, n):
+        return wide_o.at[pl.ds(k * count + start, n)]
+
+    wide_sum = Sum(count, (early, late), some, parts, first, gap, rest[:-2], rest[-2], rest[-1])
 
     @pl.when(i == 0)
     def _():
@@ -603,26 +807,57 @@
         pl.semaphore_wait(pltpu.get_barrier_semaphore(), 3 + count - 1)
         for n in range(AHEAD):
             grads(last - n).start()
-        wcat[:, 0:128] = wq[...]
-        wcat[:, 128:256] = wk[...]
-        wcat[:, 256:512] = wv[...]
-        wcat[:, 512:768] = wg[...]
-        wcat[:, 768:896] = wr[...]
+        def weave(r, carry):
+            rows = pl.ds(pl.multiple_of(r * 16, 16), 16)
+            lot[r, :, 0:128] = wq[rows, :]
+            lot[r, :, 128:256] = wk[rows, :]
+            lot[r, :, 256:512] = wv[rows, :]
+            lot[r, :, 512:768] = wg[rows, :]
+            return carry
+
+        lax.fori_loop(0, MODEL_WIDTH // 16, weave, 0)
         r = lax.broadcasted_iota(jnp.int32, (TILE, TILE), 0)
         c = lax.broadcasted_iota(jnp.int32, (TILE, TILE), 1)
         tri[...] = jnp.where(((r >> 6) == (c >> 6)) & (r > c), 1.0, 0.0).astype(BF16)
         state[...] = jnp.zeros_like(state)
-        dwa[...] = jnp.zeros_like(dwa)
-        dwo[...] = jnp.zeros_like(dwo)
-        dag_o[...] = jnp.zeros_like(dag_o)
-        dfg_o[...] = jnp.zeros_like(dfg_o)
-        dgg_o[...] = jnp.zeros_like(dgg_o)
-        db_o[...] = jnp.zeros_like(db_o)
-        dup_o[...] = jnp.zeros_like(dup_o)
+        both[...] = jnp.zeros_like(both)
+        joint[...] = jnp.zeros_like(joint)
+        small[...] = jnp.zeros_like(small)
 
     @pl.when(i + AHEAD <= last)
     def _():
         grads(last - i - AHEAD).start()
+
+    def share(n, other):
+        return to_head(joint, held.at[me], jsem.at[0, n], jsem.at[1, n], other)
+
+    @pl.when(i == ready)
+    def _():
+        held[me] = joint[...]
+        for n, other in enumerate((mate, cross, far)):
+            share(n, other).start()
+
+        def copy(r, carry):
+            lot[r] = both[pl.ds(pl.multiple_of(r * 16, 16), 16), :].astype(BF16)
+            return carry
+
+        lax.fori_loop(0, MODEL_WIDTH // 16, copy, 0)
+        used = MODEL_WIDTH // 16 + 2
+        if lot.shape[0] > used:
+            lot[used:] = jnp.zeros((lot.shape[0] - used,) + lot.shape[1:], BF16)
+
+    @pl.when(i == ready + 3)
+    def _():
+        for n, other in enumerate((mate, cross, far)):
+            to_head(joint, held.at[other], jsem.at[0, n], jsem.at[1, n], other).wait()
+        base = MODEL_WIDTH // 16
+        sums = (held[0] + held[1]) + (held[2] + held[3])
+        lot[base] = sums[0:RANK].astype(BF16)
+        lot[base + 1] = jnp.zeros((16, MODEL_WIDTH), BF16)
+        small[2:3, 128:384] = sums[16:17, 0:256]
+        lot[base + 1, :, 0:512] = small[...].astype(BF16)
+
+    wide_sum.step(i)
 
     @pl.when((i >= 2) & (i - 2 <= last))
     def _():
@@ -639,8 +874,8 @@
         hn = h1[...].astype(BF16).astype(F32) * inv
         row = stat_ref[pl.ds(t, 1), :]
         stat = jnp.broadcast_to(row, (128, TILE)).T[:, 0:1]
-        grad = c_ref[rows_of(t), :].astype(F32) + inv * (fgain[me] * gnf - hn * (stat / MODEL_WIDTH))
-        dfg_o[...] += jnp.sum(gnf * hn, axis=0, keepdims=True)
+        grad = c_ref[...].astype(F32) + inv * (own_cols(fgain) * gnf - hn * (stat / MODEL_WIDTH))
+        small[1:2, 128:384] += jnp.sum(gnf * hn, axis=0, keepdims=True)
         gh[t] = grad
         gb[t, me] = grad.astype(BF16)
         own_cross(t).start()
@@ -660,20 +895,23 @@
         t = last - (i - 3)
         own_mate(t).wait_recv()
         onward(t).wait_recv()
+        gt = jnp.zeros((TILE, BLOCK), F32)
         for j in range(4):
-            gat[:, j * BLOCK : (j + 1) * BLOCK] = gb[t, j]
-        g = gat[...]
-        gt = dot_nt(g, wout[...])
-        dwo[...] += dot_tn(gated[...], g)
+            cols = slice(j * BLOCK, (j + 1) * BLOCK)
+            gt = gt + dot_nt(gb[t, j], wout[:, cols])
+            both[cols, 768:1024] += dot_tn(gb[t, j], gated[...])
         o = oo_ref[...]
         gz = gz_ref[...]
         inv = lax.rsqrt(jnp.mean(o * o, axis=1, keepdims=True) + EPS)
         on = o * inv
         sig = jax.nn.sigmoid(gz)
         gn = gt * (gz * sig)
-        dgg_o[...] += jnp.sum(gn * on, axis=0, keepdims=True)
-        gzs[t] = (gt * on * gg_ref[...] * (sig * (1.0 + gz * (1.0 - sig)))).astype(BF16)
-        p = gn * gg_ref[...]
+        joint[16:17, 0:256] += jnp.sum(gn * on, axis=0, keepdims=True)
+        gain = gg_ref[...].astype(F32)
+        ggz = (gt * on * gain * (sig * (1.0 + gz * (1.0 - sig)))).astype(BF16)
+        gzs[t] = ggz
+        both[:, 512:768] += dot_tn(na1[...], ggz)
+        p = gn * gain
         go = (inv * (p - on * jnp.mean(p * on, axis=1, keepdims=True))).astype(BF16)
         qd = f1[:, 0:128].astype(BF16)
         kd = f1[:, 128:256].astype(BF16)
@@ -709,6 +947,13 @@
 
     @pl.when(i == second)
     def _():
+        def free(t, carry):
+            own_cross(t).wait_send()
+            own_mate(t).wait_send()
+            onward(t).wait_send()
+            return carry
+
+        lax.fori_loop(0, tiles, free, 0)
         state[...] = jnp.zeros_like(state)
 
         def join(n, carry):
@@ -727,22 +972,22 @@
         over(t).wait_recv()
         for n, other in enumerate((mate, cross, far)):
             stats(t, n, other).wait_recv()
-        gna = own[lax.rem(t, 4)] + rc[t].astype(F32)
+        gna = own[lax.rem(t, 3)] + rc[t].astype(F32)
         inv = inva[...][:, 0:1]
-        xn = x_ref[rows_of(t), :].astype(F32) * inv
+        xn = x_ref[...].astype(F32) * inv
         row = (st_s[t] + st_r[t, 0]) + (st_r[t, 1] + st_r[t, 2])
         stat = jnp.broadcast_to(row[0:1], (128, TILE)).T[:, 0:1]
-        gt_o[...] = gh[t] + inv * (again[me] * gna - xn * (stat / MODEL_WIDTH))
-        dag_o[...] += jnp.sum(gna * xn, axis=0, keepdims=True)
+        gt_o[...] = gh[t] + inv * (own_cols(again) * gna - xn * (stat / MODEL_WIDTH))
+        small[0:1, 128:384] += jnp.sum(gna * xn, axis=0, keepdims=True)
 
     @pl.when((i >= second + 1) & (i - second - 1 <= last))
     def _():
         t = last - (i - second - 1)
         pair(t, 0).wait_recv()
         pair(t, 1).wait_recv()
-        sc[t] = (pn[t, cross].astype(F32) + mn[t, 1].astype(F32)).astype(BF16)
+        sc[t] = (gb[t, cross].astype(F32) + mn[t, 1].astype(F32)).astype(BF16)
         over(t).start()
-        own[lax.rem(t, 4)] = pn[t, me].astype(F32) + mn[t, 0].astype(F32)
+        own[lax.rem(t, 3)] = gb[t, me].astype(F32) + mn[t, 0].astype(F32)
 
     @pl.when((i >= second) & (i - second <= last))
     def _():
@@ -764,45 +1009,54 @@
         diff = gq * qf - gk * kf
         gg = jnp.concatenate(pieces, axis=0) - fold(dot_nn(tri[...], three(diff)))
         glogit = gg * f2[:, 512:640]
-        db_o[...] += jnp.sum(glogit, axis=0, keepdims=True)
+        small[3:4, 128:256] += jnp.sum(glogit, axis=0, keepdims=True)
         hi = glogit.astype(BF16)
         lo = (glogit - hi.astype(F32)).astype(BF16)
         glr = dot_nt(hi, rup[...]) + dot_nt(lo, rup[...])
-        lr = b2[:, 512:640]
-        dup_o[...] += dot_tn(lr, hi) + dot_tn(lr, lo)
+        lr = b2[:, 512 : 512 + RANK]
+        small[:, 0:128] += dot_tn(lr, hi) + dot_tn(lr, lo)
+        glr = glr.astype(BF16)
+        joint[0:RANK, :] += dot_tn(glr, na[...])
         gcat[:, 0:128] = (gq * f2[:, 256:384]).astype(BF16)
         gcat[:, 128:256] = (gk * f2[:, 384:512]).astype(BF16)
         gcat[:, 256:512] = gv[t].astype(BF16)
         gcat[:, 512:768] = gzs[t]
-        gcat[:, 768:896] = glr.astype(BF16)
         g = gcat[...]
         stat = jnp.zeros((TILE, 1), F32)
         for j in range(4):
             cols = slice(j * BLOCK, (j + 1) * BLOCK)
-            gj = dot_nt(g, wcat[cols, :])
+            gj = dot_nt(g, lot[16 * j : 16 * (j + 1), :, 0:768].reshape(BLOCK, 768)) + dot_nn(glr, wr[:, cols])
             stat = stat + jnp.sum(gj * na[:, cols].astype(F32), axis=1, keepdims=True)
-            pn[t, j] = gj.astype(BF16)
+            gb[t, j] = gj.astype(BF16)
         pair(t, 1).start()
         pair(t, 0).start()
         st_s[t] = jnp.broadcast_to(stat, (TILE, 128)).T[0:8, :]
         for n, other in enumerate((mate, cross, far)):
             stats(t, n, other).start()
-        dwa[...] += dot_tn(na[...], g)
+        both[:, 0:512] += dot_tn(na[...], g[:, 0:512])
 
     @pl.when((i >= second) & (i - second <= last))
     def _():
         t = last - (i - second)
         feeds(t).wait_recv()
-        lo_o[...] = (h2[...] + (pown[...] + rp[t].astype(F32))).astype(BF16)
-
-    @pl.when(i == second + last + 3)
-    def _():
-        dq_o[...] = dwa[:, 0:128].astype(BF16)
-        dk_o[...] = dwa[:, 128:256].astype(BF16)
-        dv_o[...] = dwa[:, 256:512].astype(BF16)
-        dg_o[...] = dwa[:, 512:768].astype(BF16)
-        dr_o[...] = dwa[:, 768:896]
-        dwo_o[...] = dwo[...].astype(BF16)
+        lo_o[...] = (h2[...] + (pown[...] + rg[t].astype(F32))).astype(BF16)
+
+    drained = first + 2 * levels(count) * LAG
+    head_units = pl.ds(0, first * count)
+    tail_units = pl.ds(first * count, (parts - first) * count)
+    head_copy = pltpu.make_async_copy(wide_o.at[head_units], units_o.at[head_units], wsem.at[0])
+    tail_copy = pltpu.make_async_copy(wide_o.at[tail_units], units_o.at[tail_units], wsem.at[1])
+
+    @pl.when(i == drained)
+    def _():
+        head_copy.start()
+
+    @pl.when(i == pl.num_programs(0) - 1)
+    def _():
+        tail_copy.start()
+        wide_sum.finish()
+        tail_copy.wait()
+        head_copy.wait()
 
         def sent(p, carry):
             to_seq(sbuf, rbuf.at[place], esend.at[p], erecv.at[place], p).wait_send()
@@ -813,9 +1067,6 @@
         def out(t, carry):
             grads(t).wait_send()
             feeds(t).wait_send()
-            own_cross(t).wait_send()
-            own_mate(t).wait_send()
-            onward(t).wait_send()
             pair(t, 0).wait_send()
             pair(t, 1).wait_send()
             over(t).wait_send()
@@ -826,63 +1077,64 @@
         lax.fori_loop(0, tiles, out, 0)
 
 
-def back(fixed, gown, h, invf, f, o, oo, gated, ws, b, e, na, pown, inva):
+def back(fixed, wide, gsend, psend, x, cot, gown, h, invf, f, o, oo, gated, ws, b, e, na, pown, inva):
     rows = h.shape[0]
     tiles = rows // TILE
     count = lax.axis_size("seq")
     second = tiles + 3
     width = MODEL_WIDTH
+    first = wide.shape[0] // count
+    extra = up_to(width // 16 + 2, count)
+    units = wide.shape[0] + extra
+    parts = units // count
+    gap = max(0, second + tiles - first, second + tiles + 3 - (first + extra // count - 1))
+    steps = parts + gap + 2 * levels(count) * LAG + 1
+    assert first + gap + extra // count - 1 >= second + tiles + 3
     ts = functools.partial(tile_spec, tiles, back=True)
     outs = [
         ((rows, BLOCK), F32, ts((TILE, BLOCK), second + 3)),
         ((rows, BLOCK), BF16, ts((TILE, BLOCK), second)),
-        ((width, 128), BF16, whole((width, 128))),
-        ((width, 128), BF16, whole((width, 128))),
-        ((width, 256), BF16, whole((width, 256))),
-        ((width, 256), BF16, whole((width, 256))),
-        ((width, 128), F32, whole((width, 128))),
-        ((256, width), BF16, whole((256, width))),
-        ((1, 256), F32, whole((1, 256))),
-        ((1, 256), F32, whole((1, 256))),
-        ((1, 256), F32, whole((1, 256))),
-        ((1, 128), F32, whole((1, 128))),
-        ((128, 128), F32, whole((128, 128))),
+        ((units, 16, width), BF16, pl.BlockSpec(memory_space=pl.ANY)),
     ]
     tiled = lambda n: pltpu.VMEM((tiles, n, TILE, BLOCK), BF16)
     flat = lambda n, d: pltpu.VMEM((tiles, TILE, n), d)
     return pl.pallas_call(
-        functools.partial(back_kernel, tiles, count),
-        grid=(second + tiles + 3,),
+        functools.partial(back_kernel, tiles, count, gap),
+        grid=(max(second + tiles + 3, steps),),
         out_shape=[jax.ShapeDtypeStruct(s, d) for s, d, _ in outs],
         in_specs=[whole(a.shape) for a in fixed]
         + [
+            pl.BlockSpec(memory_space=pl.ANY), pl.BlockSpec(memory_space=pl.ANY), pl.BlockSpec(memory_space=pl.ANY),
+            ts((TILE, BLOCK), second + 3), ts((TILE, BLOCK), 0),
             ts((TILE, BLOCK), 0), ts((TILE, BLOCK), 0), ts((TILE, 128), 0),
             ts((TILE, 256), 3), ts((TILE, 256), 3), ts((TILE, 256), 3), ts((TILE, 256), 3),
-            ts((PER, HV, HK), 3), ts((TILE, 640), 3), ts((1, 8, 128), 3),
+            ts((PER, HV, HK), 3), ts((TILE, 640), 3), ts((1, 8, 128), 3), ts((TILE, width), 3),
             ts((TILE, 640), second), ts((TILE, 640), second), ts((PER, HV, HK), second), ts((1, 8, 128), second),
             ts((TILE, width), second), ts((TILE, BLOCK), second), ts((TILE, BLOCK), second),
             ts((TILE, 128), second + 3),
         ],
         out_specs=[s for _, _, s in outs],
         scratch_shapes=[
-            pltpu.VMEM((width, 896), BF16),
             pltpu.VMEM((TILE, TILE), BF16),
-            flat(BLOCK, BF16), flat(BLOCK, BF16), flat(BLOCK, F32),
+            flat(BLOCK, BF16), flat(BLOCK, F32),
             tiled(4),
-            pltpu.VMEM((TILE, width), BF16),
             flat(BLOCK, BF16),
             pltpu.VMEM((rows // SPAN, HV, HK), F32),
             flat(HK, F32), flat(HK, F32), flat(HV, F32),
             pltpu.VMEM((HV, HK), F32),
             pltpu.VMEM((HV + 16, HK), BF16),
             pltpu.VMEM((count, HV + 16, HK), BF16),
-            pltpu.VMEM((TILE, 896), BF16),
-            tiled(4), tiled(2), flat(BLOCK, BF16), flat(BLOCK, BF16),
-            pltpu.VMEM((4, TILE, BLOCK), F32),
+            pltpu.VMEM((TILE, 768), BF16),
+            tiled(2), flat(BLOCK, BF16), flat(BLOCK, BF16),
+            pltpu.VMEM((3, TILE, BLOCK), F32),
             pltpu.VMEM((tiles, 8, TILE), F32),
             pltpu.VMEM((tiles, 3, 8, TILE), F32),
-            pltpu.VMEM((width, 896), F32),
-            pltpu.VMEM((256, width), F32),
+            pltpu.VMEM((width, width), F32),
+            pltpu.VMEM((24, width), F32),
+            pltpu.VMEM((16, 512), F32),
+            pltpu.VMEM((4, 24, width), F32),
+            pltpu.VMEM((units, 16, width), BF16),
+            pltpu.VMEM((extra, 16, width), BF16),
             pltpu.SemaphoreType.DMA((2, tiles)),
             pltpu.SemaphoreType.DMA((2, tiles)),
             pltpu.SemaphoreType.DMA((6, tiles)),
@@ -891,13 +1143,16 @@
             pltpu.SemaphoreType.DMA((2, 3, tiles)),
             pltpu.SemaphoreType.DMA((count,)),
             pltpu.SemaphoreType.DMA((count,)),
-        ],
+            pltpu.SemaphoreType.DMA((2,)),
+            pltpu.SemaphoreType.DMA((2, 3)),
+        ]
+        + Sum.scratch(count, parts, first, wide.shape[1:]),
         compiler_params=pltpu.CompilerParams(
             collective_id=3, has_side_effects=True, vmem_limit_bytes=VMEM_LIMIT,
             dimension_semantics=("arbitrary",),
         ),
         name="back",
-    )(*fixed, gown, h, invf, f, o, oo, gated, ws, b, e, f, b, ws, e, na, h, pown, inva)
+    )(*fixed, wide, gsend, psend, x, cot, gown, h, invf, f, o, oo, gated, ws, b, e, na, f, b, ws, e, na, h, pown, inva)
 
 
 def shards(
@@ -926,36 +1181,22 @@
     resets = jnp.any((row_starts // SPAN)[None, :] == span_ids[:, None], axis=1).astype(F32)
     keep = jnp.pad((1.0 - resets).reshape(tiles, PER, 1), ((0, 0), (0, 8 - PER), (0, 0)))
     keep = jnp.broadcast_to(keep, (tiles, 8, 128))
-    wide = jnp.pad(rank_down[0], ((0, 0), (0, 128 - RANK)))
-    tall = jnp.pad(rank_up[0], ((0, 128 - RANK), (0, 0)))
-    weights = (query_weight[0], key_weight[0], value_weight[0], gate_weight[0], wide, tall)
-    again = attn_gain.astype(F32)
-    fgain = feed_gain.astype(F32)
-    ggain = group_gain.astype(F32)
-    na, cg, inva, f, b, o, u, e, inc, dec = front(
-        tokens, cotangent, keep, again, *weights, rank_bias.astype(F32)
+    weights = (
+        query_weight[0], key_weight[0], value_weight[0], gate_weight[0], jnp.swapaxes(rank_down[0], 0, 1), rank_up[0]
     )
-    gated, oo, ws, h, invf, gsend, gown, psend, pown, stat, dfg, dfu, dfd = ffn(
-        tokens, keep, inc, ggain, fgain, out_weight[0], feed_gate[0], feed_up[0], feed_down[0], f, o, u, e, cg
+    na, cg, inva, f, b, o, u, e, inc, dec = front(tokens, cotangent, keep, attn_gain, *weights, rank_bias)
+    gated, oo, ws, h, invf, gsend, gown, psend, pown, stat, wide = ffn(
+        tokens, keep, inc, group_gain, feed_gain, out_weight[0], jnp.swapaxes(feed_gate[0], 0, 1),
+        jnp.swapaxes(feed_up[0], 0, 1), feed_down[0], f, o, u, e, cg,
     )
-    dfg, dfu, dfd = lax.psum((dfg, dfu, dfd), "seq")
     fixed = (
-        gsend, psend, tokens, cotangent, keep, dec, stat, ggain, again.reshape(4, 1, BLOCK), fgain.reshape(4, 1, BLOCK),
-        out_weight[0],
+        keep, dec, stat, group_gain, attn_gain, feed_gain, out_weight[0],
     ) + weights
-    grad_tokens, layer_out, dq, dk, dv, dg, dr, dwo, dag, dffg, dgg, db, dup = back(
-        fixed, gown, h, invf, f, o, oo, gated, ws, b, e, na, pown, inva
-    )
-    dq, dk, dv, dg, dwo, dfg, dfu, dfd = lax.optimization_barrier((dq, dk, dv, dg, dwo, dfg, dfu, dfd))
-    dr = dr[:, 0:RANK].T.reshape(128, 128)
-    dr, dgg = lax.psum((dr.astype(BF16), dgg.astype(BF16)), "head")
-    dq, dk, dv, dg, dwo, dr, dgg, dag, dffg, db, dup = lax.psum(
-        (dq, dk, dv, dg, dwo, dr, dgg, dag.astype(BF16), dffg.astype(BF16), db.astype(BF16), dup[0:RANK].astype(BF16)),
-        "seq",
-    )
-    dr = dr.reshape(RANK, MODEL_WIDTH).T
+    grad_tokens, layer_out, units = back(fixed, wide, gsend, psend, tokens, cotangent, gown, h, invf, f, o, oo, gated, ws, b, e, na, pown, inva)
+    dfg, dfu, dfd, dq, dk, dv, dg, dwo, dr, dup, dag, dffg, db, dgg = finish(units, feed_gate.shape[2], wide.shape[0])
+    dfg, dfu, dr = (jnp.swapaxes(a, 0, 1) for a in (dfg, dfu, dr))
     grads = (dag, dq[None], dk[None], dv[None], dg[None], dr[None], dup[None], db, dgg, dwo[None], dffg, dfg[None], dfu[None], dfd[None])
-    return (layer_out, grad_tokens) + tuple(g.astype(F32) for g in grads)
+    return (layer_out, grad_tokens) + grads
 
 
 def solution(mesh):

time: 449 us -> 334 us (0.74)
  waiting for transfers between devices: 105 us -> 0 us
  Pallas kernels: 239 us -> 329 us
  blocking collectives: 48.7 us -> 0 us
  other arithmetic: 24.7 us -> 0.77 us
  between operations: 14.3 us -> 0.72 us
  local copies, waits for them, and re-layouts: 16.8 us -> 4.06 us
    psum x2 -> x0, waiting for transfers between devices: 105 us -> none  [the longest x1 62.9 us: shards(): dfg, dfu, dfd = lax.psum((dfg, dfu, dfd), 'seq')]
    pallas_call x1 -> x2, Pallas kernels: 105 us -> 196 us  [the longest x1 188 us: back(): pl.pallas_call(functools.partial(back_kernel, tiles, count, gap), grid=(m...]
    psum x2 -> x0, blocking collectives: 48.7 us -> none  [the longest x1 37 us: shards(): lax.psum((dq, dk, dv, dg, dwo, dr, dgg, dag.astype(BF16), dffg.astype(BF1...]
    convert_element_type x21 -> x0, other arithmetic: 23.8 us -> none  [the longest x13 18.8 us: shards(): return (layer_out, grad_tokens) + tuple((g.astype(F32) for g in grads))]
    unnamed x27 -> x6, local copies, waits for them, and re-layouts: 13 us -> 3.27 us
  transfers between devices with their start and end apart: 2 -> 0, of which waited for: 2 -> 0; matrix products, arithmetic and copies ran while one was open for 4% -> 0% of each run, Pallas kernels for 23% -> 0%
where the time goes in v3:
time: 334 us
  Pallas kernels  329 us (99%)
  local copies, waits for them, and re-layouts  4.06 us (1%)
    pallas_call x1, Pallas kernels, back(): pl.pallas_call(functools.partial(back_kernel, tiles, count, gap), grid=(m...  188 us
    pallas_call x1, Pallas kernels, ffn(): pl.pallas_call(functools.partial(ffn_kernel, tiles), grid=(tiles + 7,), o...  74.1 us
    pallas_call x1, Pallas kernels, front(): pl.pallas_call(functools.partial(front_kernel, tiles, count), grid=(2 * t...  58.7 us
    pallas_call x1, Pallas kernels, finish(): pl.pallas_call(finish_kernel, grid=(steps,), out_shape=[jax.ShapeDtypeStr...  7.82 us

profile of v3, /device:TPU:0, one launch (start us, length us, event | category | flops | bytes accessed | tf_op | source)
XLA Modules:
  0.0 334.1 jit_solution(6091149191785374955)
XLA Ops:
  0.7 0.7 and_select_fusion
  1.3 0.1 compare_reduce_fusion
  1.4 0.1 sub.23
  1.5 0.7 broadcast_in_dim.40.keep_ref
  2.2 58.7 %front.1 = (bf16[2048,1024]{1,0:T(8,128)(2,1)}, bf16[2048,1024]{1,0:T(8,128)(2,1)}, f32[2048,128]{1,0:T(8,128)}, f32[2048,640]{1,0:T(8,128)}, bf16[2048,640]{1,0...) custom-call(bf16[2048,256]{1,0:T(8,128)(2,1)} %x_ref.5, ...), custom_call_target="tpu_custom_call" | custom-call | tf_op jit(solution)/shard_map/front/pallas_call | solution.py:289
  60.9 74.1 %ffn.1 = (bf16[2048,256]{1,0:T(8,128)(2,1)}, f32[2048,256]{1,0:T(8,128)}, bf16[32,256,128]{2,1,0:T(8,128)(2,1)}, f32[2048,256]{1,0:T(8,128)}, f32[2048,128]{1,0:...) custom-call(bf16[2048,256]{1,0:T(8,128)(2,1)} %x_ref.5, ...), custom_call_target="tpu_custom_call" | custom-call | tf_op jit(solution)/shard_map/ffn/pallas_call | solution.py:524
  135.0 188.0 %back.1 = (f32[2048,256]{1,0:T(8,128)}, bf16[2048,256]{1,0:T(8,128)(2,1)}, bf16[208,16,1024]{2,1,0:T(8,128)(2,1)}) custom-call(f32[8,8,128]{2,1,0:T(8,128)} %broadcast_in_dim.40.keep_ref, f32[8,128]{1,0:T(8,128)} %get-tuple-element.54.d_ref, f32[8,256]{1,0:T(8,128)} %get-tuple-element.61.stat_ref, bf16[1,256]{1,0:T(2,128)(2,1)} %gg_ref.3, ...), custom_call_target="tpu_custom_call" | custom-call | tf_op jit(solution)/shard_map/back/pallas_call | solution.py:1101
  323.0 0.0 copy-start.1
  323.0 7.8 %finish.1 = (f32[704,1024]{1,0:T(8,128)}, f32[704,1024]{1,0:T(8,128)}, f32[704,1024]{1,0:T(8,128)}, f32[1024,128]{1,0:T(8,128)}, f32[1024,128]{1,0:T(8,128)}, /*...) custom-call(bf16[208,16,1024]{2,1,0:T(8,128)(2,1)} %get-tuple-elemen, ...), custom_call_target="tpu_custom_call" | custom-call | tf_op jit(solution)/shard_map/finish/pallas_call | solution.py:724
  330.9 0.0 copy-start
  330.9 0.0 copy-done.1
  330.9 1.0 copy.35
  331.9 1.0 copy-done
  332.8 1.3 copy.36
  (3 shorter events, 0.0 us)
Async XLA Ops:
  323.0 7.9 %copy-start.1 = (bf16[2048,256]{1,0:T(8,128)(2,1)S(1)}, bf16[2048,256]{1,0:T(8,128)(2,1)}, u32[]{:S(2)}) copy-start(bf16[2048,256]{1,0:T(8,128)(2,1)} %get-tuple-element.108) | copy-start | bytes 3145732
  330.9 2.0 copy-start

commit v4 on v3

--- a/solution.py
+++ b/solution.py
@@ -478,8 +478,6 @@
             return carry
 
         lax.fori_loop(0, used, unit, 0)
-        if wide_o.shape[0] > used:
-            wide_o[used:] = jnp.zeros((wide_o.shape[0] - used,) + wide_o.shape[1:], BF16)
         for n, other in enumerate((mate, cross, far)):
             stats(n, other).wait()
         stat_o[...] = (st_s[...] + st_r[0]) + (st_r[1] + st_r[2])
@@ -502,8 +500,7 @@
     rows = x.shape[0]
     tiles = rows // TILE
     hidden, width = wfg.shape
-    count = lax.axis_size("seq")
-    units = up_to(3 * hidden // 16, count)
+    units = 3 * hidden // 16
     assert tiles <= 8 and hidden % 16 == 0
     ts = functools.partial(tile_spec, tiles)
     ins = (x, keep, inc, gg, gain, wout, wfg, wfu, wfd)
@@ -557,7 +554,7 @@
     )(*ins, f, o, u, e, cg)
 
 
-LAG = 2
+LAGS = (2, 2, 2)
 
 
 def levels(count):
@@ -566,22 +563,31 @@
     return bits
 
 
+def folds(count):
+    return count == 8
+
+
 class Sum:
-    def __init__(self, count, sources, dest, parts, first, gap, got, sems, lsem):
+    def __init__(self, count, sources, dest, segments, scratch):
         self.count = count
         self.bits = levels(count)
+        self.folds = folds(count)
         self.sources = sources
         self.dest = dest
-        self.parts = parts
-        self.first = first
-        self.gap = gap
-        self.got = got
-        self.sems = sems
-        self.lsem = lsem
+        self.segments = segments
+        self.got = scratch[: self.bits]
+        self.ring, self.side_sum, self.line_sum = scratch[self.bits : self.bits + 3]
+        self.sems, self.lsem = scratch[self.bits + 3 :]
+
+    def slot(self, k):
+        if not self.folds:
+            return k
+        odd = lax.rem(lax.rem(k, 5), 2)
+        return (3 - odd) * lax.div(k, 5) + lax.div(lax.rem(k, 5), 2)
 
     def where(self, k, level):
         place = lax.axis_index("seq")
-        turn = lax.div(lax.rem(k, 4), 3)
+        turn = 1 if self.folds else lax.div(lax.rem(k, 4), 3)
         start = 0
         for step in range(level + 1):
             stride = 1 << step
@@ -605,8 +611,8 @@
         if level == 0:
             src = self.sources[kind](k, start + (1 - bit) * half, half)
         else:
-            src = self.got[level - 1].at[k, pl.ds((1 - bit) * half, half)]
-        return to_seq(src, self.got[level].at[k], self.sems.at[0, level, k], self.sems.at[1, level, k], partner)
+            src = self.got[level - 1].at[self.slot(k), pl.ds((1 - bit) * half, half)]
+        return to_seq(src, self.got[level].at[self.slot(k)], self.sems.at[0, level, k], self.sems.at[1, level, k], partner)
 
     def gather(self, k, level):
         bit, partner, start = self.where(k, level)
@@ -634,12 +640,12 @@
             self.own(k).wait()
             mine = self.dest(k, bit * half, half)[...]
         elif level == 0:
-            mine = self.sources[1](k, bit * half, half)[...]
+            mine = self.sources[kind](k, bit * half, half)[...]
         else:
-            mine = self.got[level - 1][k, pl.ds(bit * half, half)]
-        total = (self.got[level][k].astype(F32) + mine.astype(F32)).astype(BF16)
+            mine = self.got[level - 1][self.slot(k), pl.ds(bit * half, half)]
+        total = (self.got[level][self.slot(k)].astype(F32) + mine.astype(F32)).astype(BF16)
         if level + 1 < self.bits:
-            self.got[level][k] = total
+            self.got[level][self.slot(k)] = total
             self.scatter(k, level + 1, kind).start()
         else:
             self.dest(k, start + bit * half, half)[...] = total
@@ -650,14 +656,132 @@
         if level > 0:
             self.gather(k, level - 1).start()
 
-    def at(self, j, body):
-        @pl.when((j >= 0) & (j < self.first))
+    def spot(self):
+        place = lax.axis_index("seq")
+        side = lax.rem(place, 2)
+        z = lax.div(place, 2)
+        low = lax.rem(z, 2)
+        end = low == lax.div(z, 2)
+        return side, place + 1 - 2 * side, place + 2 * (1 - 2 * low), 2 * (3 - z) + side, end
+
+    def half_of(self, k, which):
+        half = self.count >> 1
+        return self.dest(k, which * half, half)
+
+    def fold_own(self, k):
+        half = self.count >> 1
+        return pltpu.make_async_copy(
+            self.sources[0](k, self.spot()[0] * half, half), self.ring.at[lax.rem(k, 4)], self.lsem.at[k]
+        )
+
+    def fold_side(self, k, kind):
+        side, twin, _, _, _ = self.spot()
+        half = self.count >> 1
+        src = self.sources[kind](k, (1 - side) * half, half)
+        return to_seq(src, self.side_sum.at[self.slot(k)], self.sems.at[0, 0, k], self.sems.at[1, 0, k], twin)
+
+    def fold_in(self, k):
+        n = self.slot(k)
+        return to_seq(
+            self.side_sum.at[n], self.line_sum.at[n], self.sems.at[0, 1, k], self.sems.at[1, 1, k], self.spot()[2]
+        )
+
+    def fold_cross(self, k):
+        side, _, _, other, _ = self.spot()
+        return to_seq(
+            self.line_sum.at[self.slot(k)], self.half_of(k, side), self.sems.at[0, 2, k], self.sems.at[1, 2, k], other
+        )
+
+    def fold_out(self, k):
+        side, _, across, _, _ = self.spot()
+        ref = self.half_of(k, side)
+        return to_seq(ref, ref, self.sems.at[2, 1, k], self.sems.at[3, 1, k], across)
+
+    def fold_back(self, k, mine):
+        side, twin, _, _, _ = self.spot()
+        ref = self.half_of(k, side if mine else 1 - side)
+        return to_seq(ref, ref, self.sems.at[2, 0, k], self.sems.at[3, 0, k], twin)
+
+    def fold_begin(self, k, kind):
+        self.fold_side(k, kind).start()
+        if kind == 0:
+            self.fold_own(k).start()
+
+    def fold_1(self, k, kind):
+        side, _, _, _, end = self.spot()
+        half = self.count >> 1
+        n = self.slot(k)
+        self.fold_side(k, kind).wait_recv()
+        if kind == 0:
+            self.fold_own(k).wait()
+            mine = self.ring[lax.rem(k, 4)]
+        else:
+            mine = self.sources[kind](k, side * half, half)[...]
+        self.side_sum[n] = (self.side_sum[n].astype(F32) + mine.astype(F32)).astype(BF16)
+
+        @pl.when(end)
         def _():
-            body(j, 0)
-
-        @pl.when((j >= self.first + self.gap) & (j < self.parts + self.gap))
+            self.fold_in(k).start()
+
+    def fold_2(self, k, kind):
+        n = self.slot(k)
+
+        @pl.when(jnp.logical_not(self.spot()[4]))
         def _():
-            body(j - self.gap, 1)
+            self.fold_in(k).wait_recv()
+            self.line_sum[n] = (self.line_sum[n].astype(F32) + self.side_sum[n].astype(F32)).astype(BF16)
+            self.fold_cross(k).start()
+
+    def fold_3(self, k, kind):
+        side, _, _, _, end = self.spot()
+
+        @pl.when(jnp.logical_not(end))
+        def _():
+            self.fold_cross(k).wait_recv()
+            ref = self.half_of(k, side)
+            ref[...] = (ref[...].astype(F32) + self.line_sum[self.slot(k)].astype(F32)).astype(BF16)
+            self.fold_out(k).start()
+            self.fold_back(k, True).start()
+
+    def fold_4(self, k, kind):
+        end = self.spot()[4]
+
+        @pl.when(end)
+        def _():
+            self.fold_out(k).wait_recv()
+            self.fold_back(k, True).start()
+
+        @pl.when(jnp.logical_not(end))
+        def _():
+            self.fold_back(k, False).wait_recv()
+
+    def fold_5(self, k, kind):
+        @pl.when(self.spot()[4])
+        def _():
+            self.fold_back(k, False).wait_recv()
+
+    def at(self, i, stage, body, fold):
+        for kind, (low, high, gap) in enumerate(self.segments):
+            k = i - gap - LAGS[kind] * stage
+            here = (k >= low) & (k < high)
+            if not self.folds:
+
+                @pl.when(here)
+                def _(kind=kind, k=k):
+                    body(k, kind)
+
+                continue
+            odd = lax.rem(lax.rem(jnp.maximum(k, 0), 5), 2) == 1
+
+            @pl.when(here & odd)
+            def _(kind=kind, k=k):
+                body(k, kind)
+
+            if fold is not None:
+
+                @pl.when(here & jnp.logical_not(odd))
+                def _(kind=kind, k=k):
+                    fold(k, kind)
 
     def step(self, i):
         stages = []
@@ -665,38 +789,97 @@
             stages.append(functools.partial(self.add, level=level))
         for level in range(self.bits - 1, -1, -1):
             stages.append(functools.partial(self.pass_on, level=level))
+        folded = [self.fold_1, self.fold_2, self.fold_3, self.fold_4, self.fold_5]
+        folded = folded + [None] * (len(stages) - len(folded))
         for s in range(len(stages) - 1, -1, -1):
-            self.at(i - LAG * (s + 1), stages[s])
-        self.at(i, self.begin)
+            self.at(i, s + 1, stages[s], folded[s])
+        self.at(i, 0, self.begin, self.fold_begin)
 
     def finish(self):
-        def one(kind, k, carry):
+        def halving(k, kind):
             for level in range(self.bits):
                 self.scatter(k, level, kind).wait_send()
                 self.gather(k, level).wait_send()
+
+        def folding(k, kind):
+            end = self.spot()[4]
+            self.fold_side(k, kind).wait_send()
+            self.fold_back(k, True).wait_send()
+
+            @pl.when(end)
+            def _():
+                self.fold_in(k).wait_send()
+
+            @pl.when(jnp.logical_not(end))
+            def _():
+                self.fold_cross(k).wait_send()
+                self.fold_out(k).wait_send()
+
+        def one(kind, k, carry):
+            if not self.folds:
+                halving(k, kind)
+                return carry
+            odd = lax.rem(lax.rem(k, 5), 2) == 1
+
+            @pl.when(odd)
+            def _():
+                halving(k, kind)
+
+            @pl.when(jnp.logical_not(odd))
+            def _():
+                folding(k, kind)
+
             return carry
 
-        lax.fori_loop(0, self.first, functools.partial(one, 0), 0)
-        lax.fori_loop(self.first, self.parts, functools.partial(one, 1), 0)
+        for kind, (low, high, _) in enumerate(self.segments):
+            lax.fori_loop(low, high, functools.partial(one, kind), 0)
 
     @staticmethod
     def scratch(count, parts, first, unit):
         bits = levels(count)
-        return [pltpu.VMEM((parts, count >> (level + 1)) + unit, BF16) for level in range(bits)] + [
+        odd = parts
+        even = 1
+        half = 16
+        if folds(count):
+            odd = sum(1 for k in range(parts) if k % 5 % 2 == 1)
+            even = parts - odd
+            half = count // 2
+        one = (1,) + unit if not folds(count) else (half,) + unit
+        return [pltpu.VMEM((odd, count >> (level + 1)) + unit, BF16) for level in range(bits)] + [
+            pltpu.VMEM((4 if folds(count) else 1,) + one, BF16),
+            pltpu.VMEM((even,) + one, BF16),
+            pltpu.VMEM((even,) + one, BF16),
             pltpu.SemaphoreType.DMA((4, bits, parts)),
             pltpu.SemaphoreType.DMA((first,)),
         ]
 
 
-def finish_kernel(fg, fu, fd, mixed, tail, dfg, dfu, dfd, dq, dk, dv, dg, dwo, dr, dup, dag, dffg, db, dgg):
+def plan(count, wide, tiles):
+    second = tiles + 3
+    a = wide // count
+    b = a + 32 // count
+    c = b + up_to(34 + wide % count, count) // count
+    gap = max(0, second - a)
+    late = max(gap, second + tiles - b, second + tiles + 3 - (c - 1))
+    return (0, a, 0), (a, b, gap), (b, c, late)
+
+
+def finish_kernel(fg, fu, fd, first, second, tail, extra, dfg, dfu, dfd, dq, dk, dv, dg, dwo, dr, dup, dag, dffg, db, dgg):
     for src, dst in ((fg, dfg), (fu, dfu), (fd, dfd)):
         dst[...] = src[...].reshape(dst.shape).astype(F32)
-    rows = mixed[...].reshape(-1, MODEL_WIDTH).astype(F32)
+
+    @pl.when(pl.program_id(0) == pl.num_programs(0) - 1)
+    def _():
+        tail_rows = extra.shape[0] * 16
+        dfd[dfd.shape[0] - tail_rows :, :] = extra[...].reshape(tail_rows, -1).astype(F32)
+
+    rows = first[...].reshape(-1, 512).astype(F32)
+    dg[...] = rows[:, 0:256]
+    dwo[...] = rows[:, 256:512].T
+    rows = second[...].reshape(-1, 512).astype(F32)
     dq[...] = rows[:, 0:128]
     dk[...] = rows[:, 128:256]
     dv[...] = rows[:, 256:512]
-    dg[...] = rows[:, 512:768]
-    dwo[...] = rows[:, 768:1024].T
     dr[...] = tail[0].astype(F32)
     last = tail[1].astype(F32)
     dup[...] = last[:, 0:128]
@@ -706,13 +889,19 @@
     dgg[...] = last[2:3, 128:384]
 
 
-def finish(units, hidden, first):
+def finish(units, hidden, wide, count):
+    first = wide // count * count
+    rest = wide % count
     width = units.shape[2]
     steps = 4
     per = hidden // 16 // steps
-    assert per * steps * 16 == hidden
+    assert per * steps * 16 == hidden and 0 < rest <= per
     rows = MODEL_WIDTH // steps
     wide_spec = lambda n: pl.BlockSpec((per, 16, width), lambda i: (i + n * steps, 0, 0))
+    half_spec = lambda n: pl.BlockSpec(
+        (pl.Element(rows // 16), pl.Element(16), pl.Element(512)),
+        lambda i: (first + n + (i % 2) * (rows // 16), 0, (i // 2) * 512),
+    )
     down = lambda r, c: ((r * steps, c), pl.BlockSpec((r, c), lambda i: (i, 0)))
     full = lambda r, c: ((r, c), pl.BlockSpec((r, c), lambda i: (0, 0)))
     outs = [
@@ -727,25 +916,26 @@
         out_shape=[jax.ShapeDtypeStruct(s, F32) for s, _ in outs],
         in_specs=[
             wide_spec(0), wide_spec(1), wide_spec(2),
-            pl.BlockSpec((pl.Element(rows // 16), pl.Element(16), pl.Element(width)), lambda i: (first + i * (rows // 16), 0, 0)),
-            pl.BlockSpec((pl.Element(2), pl.Element(16), pl.Element(width)), lambda i: (first + MODEL_WIDTH // 16, 0, 0)),
+            half_spec(0), half_spec(32),
+            pl.BlockSpec((pl.Element(2), pl.Element(16), pl.Element(width)), lambda i: (first + 64, 0, 0)),
+            pl.BlockSpec((pl.Element(rest), pl.Element(16), pl.Element(width)), lambda i: (first + 66, 0, 0)),
         ],
         out_specs=[s for _, s in outs],
         compiler_params=pltpu.CompilerParams(
             vmem_limit_bytes=VMEM_LIMIT, dimension_semantics=("arbitrary",)
         ),
         name="finish",
-    )(units, units, units, units, units)
+    )(units, units, units, units, units, units, units)
 
 
 def back_kernel(
-    tiles, count, gap,
+    tiles, count, segments,
     keep_ref, d_ref, stat_ref, gg_ref, again, fgain, wout, wq, wk, wv, wg, wr, rup,
     wide_in, gsend, psend, x_ref, c_ref, gown, h1, invf, f1, gz_ref, oo_ref, gated, ws1, b1, e1,
     na1, f2, b2, ws2, e2, na, h2, pown, inva,
     gt_o, lo_o, units_o,
     tri, rg, gh, gb, gzs, gw, gqd, gkd, gv, state, sbuf, rbuf,
-    gcat, mn, sc, rc, own, st_s, st_r, both, joint, small, held, wide_o, lot,
+    gcat, mn, sc, rc, own, st_s, st_r, both, joint, small, held, wide_o, few, lot,
     gsem, psem, hsem, nsem, csem, tsem, esend, erecv, wsem, jsem, *rest,
 ):
     i = pl.program_id(0)
@@ -786,19 +976,24 @@
         return to_head(st_s.at[t], st_r.at[t, n], tsem.at[0, n, t], tsem.at[1, n, t], other)
 
     first = wide_in.shape[0] // count
+    spare = wide_in.shape[0] - first * count
     parts = wide_o.shape[0] // count
     ready = second + tiles
+    feed = ready + 4
 
     def early(k, start, n):
         return wide_in.at[pl.ds(k * count + start, n)]
 
+    def middle(k, start, n):
+        return few.at[pl.ds((k - segments[1][0]) * count + start, n)]
+
     def late(k, start, n):
-        return lot.at[pl.ds((k - first) * count + start, n)]
+        return lot.at[pl.ds((k - segments[2][0]) * count + start, n)]
 
     def some(k, start, n):
         return wide_o.at[pl.ds(k * count + start, n)]
 
-    wide_sum = Sum(count, (early, late), some, parts, first, gap, rest[:-2], rest[-2], rest[-1])
+    wide_sum = Sum(count, (early, middle, late), some, segments, rest)
 
     @pl.when(i == 0)
     def _():
@@ -831,26 +1026,38 @@
     def share(n, other):
         return to_head(joint, held.at[me], jsem.at[0, n], jsem.at[1, n], other)
 
+    spare_copy = pltpu.make_async_copy(
+        wide_in.at[pl.ds(first * count, spare)], lot.at[pl.ds(34, spare)], wsem.at[2]
+    )
+
+    def lay(dst, col):
+        def copy(r, carry):
+            for side in range(2):
+                rows = pl.ds(pl.multiple_of(side * (MODEL_WIDTH // 2) + r * 16, 16), 16)
+                dst[r, :, side * 512 : (side + 1) * 512] = both[rows, col : col + 512].astype(BF16)
+            return carry
+
+        lax.fori_loop(0, 32, copy, 0)
+
+    @pl.when(i == second)
+    def _():
+        lay(few, 512)
+
     @pl.when(i == ready)
     def _():
         held[me] = joint[...]
         for n, other in enumerate((mate, cross, far)):
             share(n, other).start()
-
-        def copy(r, carry):
-            lot[r] = both[pl.ds(pl.multiple_of(r * 16, 16), 16), :].astype(BF16)
-            return carry
-
-        lax.fori_loop(0, MODEL_WIDTH // 16, copy, 0)
-        used = MODEL_WIDTH // 16 + 2
-        if lot.shape[0] > used:
-            lot[used:] = jnp.zeros((lot.shape[0] - used,) + lot.shape[1:], BF16)
+        lay(lot, 0)
+        lot[32:] = jnp.zeros((lot.shape[0] - 32,) + lot.shape[1:], BF16)
+        spare_copy.start()
 
     @pl.when(i == ready + 3)
     def _():
+        spare_copy.wait()
         for n, other in enumerate((mate, cross, far)):
             to_head(joint, held.at[other], jsem.at[0, n], jsem.at[1, n], other).wait()
-        base = MODEL_WIDTH // 16
+        base = 32
         sums = (held[0] + held[1]) + (held[2] + held[3])
         lot[base] = sums[0:RANK].astype(BF16)
         lot[base + 1] = jnp.zeros((16, MODEL_WIDTH), BF16)
@@ -881,14 +1088,20 @@
         own_cross(t).start()
         own_mate(t).start()
 
-    @pl.when((i >= last) & (i - last <= (tiles - 1) // 2))
-    def _():
-        n = 2 * (i - last)
-        feeds(last - n).start()
-
-        @pl.when(n + 1 <= last)
+    half = tiles // 2
+
+    def some_feeds(low, high, at):
+        @pl.when((i >= at) & (low + 2 * (i - at) < high))
         def _():
-            feeds(last - n - 1).start()
+            n = low + 2 * (i - at)
+            feeds(last - n).start()
+
+            @pl.when(n + 1 < high)
+            def _():
+                feeds(last - n - 1).start()
+
+    some_feeds(0, half, last + 2)
+    some_feeds(half, tiles, ready)
 
     @pl.when((i >= 3) & (i - 3 <= last))
     def _():
@@ -1035,13 +1248,13 @@
             stats(t, n, other).start()
         both[:, 0:512] += dot_tn(na[...], g[:, 0:512])
 
-    @pl.when((i >= second) & (i - second <= last))
-    def _():
-        t = last - (i - second)
+    @pl.when((i >= feed) & (i - feed <= last))
+    def _():
+        t = last - (i - feed)
         feeds(t).wait_recv()
         lo_o[...] = (h2[...] + (pown[...] + rg[t].astype(F32))).astype(BF16)
 
-    drained = first + 2 * levels(count) * LAG
+    drained = first + 2 * levels(count) * LAGS[0]
     head_units = pl.ds(0, first * count)
     tail_units = pl.ds(first * count, (parts - first) * count)
     head_copy = pltpu.make_async_copy(wide_o.at[head_units], units_o.at[head_units], wsem.at[0])
@@ -1083,24 +1296,24 @@
     count = lax.axis_size("seq")
     second = tiles + 3
     width = MODEL_WIDTH
-    first = wide.shape[0] // count
-    extra = up_to(width // 16 + 2, count)
-    units = wide.shape[0] + extra
-    parts = units // count
-    gap = max(0, second + tiles - first, second + tiles + 3 - (first + extra // count - 1))
-    steps = parts + gap + 2 * levels(count) * LAG + 1
-    assert first + gap + extra // count - 1 >= second + tiles + 3
+    segments = plan(count, wide.shape[0], tiles)
+    first = segments[0][1]
+    parts = segments[2][1]
+    units = parts * count
+    feed = second + tiles + 4
+    stages = 2 * levels(count)
+    steps = max([feed + tiles] + [end + gap + stages * lag + 1 for (_, end, gap), lag in zip(segments, LAGS)])
     ts = functools.partial(tile_spec, tiles, back=True)
     outs = [
         ((rows, BLOCK), F32, ts((TILE, BLOCK), second + 3)),
-        ((rows, BLOCK), BF16, ts((TILE, BLOCK), second)),
+        ((rows, BLOCK), BF16, ts((TILE, BLOCK), feed)),
         ((units, 16, width), BF16, pl.BlockSpec(memory_space=pl.ANY)),
     ]
     tiled = lambda n: pltpu.VMEM((tiles, n, TILE, BLOCK), BF16)
     flat = lambda n, d: pltpu.VMEM((tiles, TILE, n), d)
     return pl.pallas_call(
-        functools.partial(back_kernel, tiles, count, gap),
-        grid=(max(second + tiles + 3, steps),),
+        functools.partial(back_kernel, tiles, count, segments),
+        grid=(steps,),
         out_shape=[jax.ShapeDtypeStruct(s, d) for s, d, _ in outs],
         in_specs=[whole(a.shape) for a in fixed]
         + [
@@ -1110,7 +1323,7 @@
             ts((TILE, 256), 3), ts((TILE, 256), 3), ts((TILE, 256), 3), ts((TILE, 256), 3),
             ts((PER, HV, HK), 3), ts((TILE, 640), 3), ts((1, 8, 128), 3), ts((TILE, width), 3),
             ts((TILE, 640), second), ts((TILE, 640), second), ts((PER, HV, HK), second), ts((1, 8, 128), second),
-            ts((TILE, width), second), ts((TILE, BLOCK), second), ts((TILE, BLOCK), second),
+            ts((TILE, width), second), ts((TILE, BLOCK), feed), ts((TILE, BLOCK), feed),
             ts((TILE, 128), second + 3),
         ],
         out_specs=[s for _, _, s in outs],
@@ -1134,7 +1347,8 @@
             pltpu.VMEM((16, 512), F32),
             pltpu.VMEM((4, 24, width), F32),
             pltpu.VMEM((units, 16, width), BF16),
-            pltpu.VMEM((extra, 16, width), BF16),
+            pltpu.VMEM((32, 16, width), BF16),
+            pltpu.VMEM((max(width // 16, (parts - segments[2][0]) * count), 16, width), BF16),
             pltpu.SemaphoreType.DMA((2, tiles)),
             pltpu.SemaphoreType.DMA((2, tiles)),
             pltpu.SemaphoreType.DMA((6, tiles)),
@@ -1143,7 +1357,7 @@
             pltpu.SemaphoreType.DMA((2, 3, tiles)),
             pltpu.SemaphoreType.DMA((count,)),
             pltpu.SemaphoreType.DMA((count,)),
-            pltpu.SemaphoreType.DMA((2,)),
+            pltpu.SemaphoreType.DMA((3,)),
             pltpu.SemaphoreType.DMA((2, 3)),
         ]
         + Sum.scratch(count, parts, first, wide.shape[1:]),
@@ -1193,7 +1407,9 @@
         keep, dec, stat, group_gain, attn_gain, feed_gain, out_weight[0],
     ) + weights
     grad_tokens, layer_out, units = back(fixed, wide, gsend, psend, tokens, cotangent, gown, h, invf, f, o, oo, gated, ws, b, e, na, pown, inva)
-    dfg, dfu, dfd, dq, dk, dv, dg, dwo, dr, dup, dag, dffg, db, dgg = finish(units, feed_gate.shape[2], wide.shape[0])
+    dfg, dfu, dfd, dq, dk, dv, dg, dwo, dr, dup, dag, dffg, db, dgg = finish(
+        units, feed_gate.shape[2], wide.shape[0], lax.axis_size("seq")
+    )
     dfg, dfu, dr = (jnp.swapaxes(a, 0, 1) for a in (dfg, dfu, dr))
     grads = (dag, dq[None], dk[None], dv[None], dg[None], dr[None], dup[None], db, dgg, dwo[None], dffg, dfg[None], dfu[None], dfd[None])
     return (layer_out, grad_tokens) + grads

time: 334 us -> 315 us (0.943)
  Pallas kernels: 329 us -> 309 us
    pallas_call x1, Pallas kernels: 188 us -> 168 us  [back(): pl.pallas_call(functools.partial(back_kernel, tiles, count, segments), gr...]
where the time goes in v4:
time: 315 us; the launch traced here: 314 us
  Pallas kernels  309 us (98%)
  local copies, waits for them, and re-layouts  4.06 us (1%)
    pallas_call x1, Pallas kernels, back(): pl.pallas_call(functools.partial(back_kernel, tiles, count, segments), gr...  168 us
    pallas_call x1, Pallas kernels, ffn(): pl.pallas_call(functools.partial(ffn_kernel, tiles), grid=(tiles + 7,), o...  74.1 us
    pallas_call x1, Pallas kernels, front(): pl.pallas_call(functools.partial(front_kernel, tiles, count), grid=(2 * t...  58.7 us
    pallas_call x1, Pallas kernels, finish(): pl.pallas_call(finish_kernel, grid=(steps,), out_shape=[jax.ShapeDtypeStr...  8.06 us

profile of v4, /device:TPU:0, one launch (start us, length us, event | category | flops | bytes accessed | tf_op | source)
XLA Modules:
  0.0 314.2 jit_solution(5751409452120206126)
XLA Ops:
  0.7 0.7 and_select_fusion
  1.3 0.1 compare_reduce_fusion
  1.4 0.1 sub.23
  1.5 0.7 broadcast_in_dim.40.keep_ref
  2.2 58.7 %front.1 = (bf16[2048,1024]{1,0:T(8,128)(2,1)}, bf16[2048,1024]{1,0:T(8,128)(2,1)}, f32[2048,128]{1,0:T(8,128)}, f32[2048,640]{1,0:T(8,128)}, bf16[2048,640]{1,0...) custom-call(bf16[2048,256]{1,0:T(8,128)(2,1)} %x_ref.5, ...), custom_call_target="tpu_custom_call" | custom-call | tf_op jit(solution)/shard_map/front/pallas_call | solution.py:289
  60.9 74.1 %ffn.1 = (bf16[2048,256]{1,0:T(8,128)(2,1)}, f32[2048,256]{1,0:T(8,128)}, bf16[32,256,128]{2,1,0:T(8,128)(2,1)}, f32[2048,256]{1,0:T(8,128)}, f32[2048,128]{1,0:...) custom-call(bf16[2048,256]{1,0:T(8,128)(2,1)} %x_ref.5, ...), custom_call_target="tpu_custom_call" | custom-call | tf_op jit(solution)/shard_map/ffn/pallas_call | solution.py:521
  135.0 167.8 %back.1 = (f32[2048,256]{1,0:T(8,128)}, bf16[2048,256]{1,0:T(8,128)(2,1)}, bf16[200,16,1024]{2,1,0:T(8,128)(2,1)}) custom-call(f32[8,8,128]{2,1,0:T(8,128)} %broadcast_in_dim.40.keep_ref, f32[8,128]{1,0:T(8,128)} %get-tuple-element.54.d_ref, f32[8,256]{1,0:T(8,128)} %get-tuple-element.61.stat_ref, bf16[1,256]{1,0:T(2,128)(2,1)} %gg_ref.3, ...), custom_call_target="tpu_custom_call" | custom-call | tf_op jit(solution)/shard_map/back/pallas_call | solution.py:1314
  302.9 0.0 copy-start.1
  302.9 8.1 %finish.1 = (f32[704,1024]{1,0:T(8,128)}, f32[704,1024]{1,0:T(8,128)}, f32[704,1024]{1,0:T(8,128)}, f32[1024,128]{1,0:T(8,128)}, f32[1024,128]{1,0:T(8,128)}, /*...) custom-call(bf16[200,16,1024]{2,1,0:T(8,128)(2,1)} %get-tuple-elemen, ...), custom_call_target="tpu_custom_call" | custom-call | tf_op jit(solution)/shard_map/finish/pallas_call | solution.py:913
  311.0 0.0 copy-start
  311.0 0.0 copy-done.1
  311.0 1.0 copy.35
  311.9 1.0 copy-done
  312.9 1.3 copy.36
  (3 shorter events, 0.0 us)
Async XLA Ops:
  302.9 8.1 %copy-start.1 = (bf16[2048,256]{1,0:T(8,128)(2,1)S(1)}, bf16[2048,256]{1,0:T(8,128)(2,1)}, u32[]{:S(2)}) copy-start(bf16[2048,256]{1,0:T(8,128)(2,1)} %get-tuple-element.108) | copy-start | bytes 3145732
  311.0 2.0 copy-start

commit v5 on v4

--- a/solution.py
+++ b/solution.py
@@ -328,11 +328,11 @@
 
 def ffn_kernel(
     tiles,
-    x_ref, keep_ref, in_ref, gg_ref, gain_ref, wout, wfg, wfu, wfd,
+    x_ref, keep_ref, in_ref, gg_ref, gain_ref, wout, wfg_in, wfu_in, wfd_in,
     f_ref, o_ref, u_ref, e_ref, cg_ref,
-    gated_o, oo_o, ws_o, h_o, inv_o, gsend_o, gown_o, psend_o, pown_o, stat_o, wide_o,
-    state, pa, pp, pg, ma, mp, mg, sc, rc, own, hg, nf_s, acc, st_s, st_r,
-    asem, psem, gsem, csem, hsem, tsem,
+    gated_o, oo_o, ws_o, h_o, inv_o, gsend_o, gown_o, psend_o, pown_o, stat_o, wide_o, gx_o,
+    state, pa, pp, pg, ma, mp, mg, sc, rc, own, hg, nf_s, acc, wfg, wfu, wfd, st_s, st_r, gxs, gxr,
+    asem, psem, gsem, csem, hsem, tsem, wsem, xsem,
 ):
     i = pl.program_id(0)
     me, mate, cross, far = peers()
@@ -355,73 +355,33 @@
     def onward(t):
         return to_head(hg.at[t, cross], hg.at[t, cross], hsem.at[4, t], hsem.at[5, t], mate)
 
+    some = gxs.shape[0]
+
+    def early(t):
+        return to_head(gxs.at[t], gxr.at[t], xsem.at[0, t], xsem.at[1, t], cross)
+
     def stats(n, other):
         return to_head(st_s, st_r.at[n], tsem.at[0, n], tsem.at[1, n], other)
 
+    fetches = [
+        pltpu.make_async_copy(src, dst, wsem.at[n])
+        for n, (src, dst) in enumerate(((wfg_in, wfg), (wfu_in, wfu), (wfd_in, wfd)))
+    ]
+
+    @pl.when(i == 4)
+    def _():
+        for fetch in fetches:
+            fetch.wait()
+
     @pl.when(i == 0)
     def _():
+        for fetch in fetches:
+            fetch.start()
         greet_head()
         state[...] = in_ref[...]
         acc[...] = jnp.zeros_like(acc)
         st_s[...] = jnp.zeros_like(st_s)
         pl.semaphore_wait(pltpu.get_barrier_semaphore(), 3)
-
-    @pl.when((i >= 5) & (i - 5 <= last))
-    def _():
-        t = i - 5
-        own_cross(t).wait_recv()
-        onward(t).start()
-
-    @pl.when((i >= 3) & (i - 3 <= last))
-    def _():
-        t = i - 3
-        over(t).wait_recv()
-        rows = pl.ds(pl.multiple_of(t * TILE, TILE), TILE)
-        h = x_ref[rows, :].astype(F32) + (own[lax.rem(t, 4)] + rc[t].astype(F32))
-        h_o[...] = h
-        hg[t, me] = h.astype(BF16)
-        own_cross(t).start()
-        own_mate(t).start()
-
-    @pl.when((i >= 1) & (i - 1 <= last))
-    def _():
-        t = i - 1
-        pair(pa, ma, asem, t, 0).wait_recv()
-        pair(pa, ma, asem, t, 1).wait_recv()
-        sc[t] = (pa[t, cross].astype(F32) + ma[t, 1].astype(F32)).astype(BF16)
-        over(t).start()
-        own[lax.rem(t, 4)] = pa[t, me].astype(F32) + ma[t, 0].astype(F32)
-
-    @pl.when(i <= last)
-    def _():
-        t = i
-        for c in range(PER):
-            rows = slice(c * SPAN, (c + 1) * SPAN)
-            scaled = (keep_ref[t, c : c + 1, :] * e_ref[0, c : c + 1, :]) * state[...]
-            low = scaled.astype(BF16)
-            ws_o[c] = low
-            state[...] = scaled + u_ref[c]
-            oo_o[rows, :] = o_ref[rows, 256:512] + dot_nt(f_ref[rows, :].astype(BF16), low)
-        o = oo_o[...]
-        gz = o_ref[:, 0:256]
-        inv = lax.rsqrt(jnp.mean(o * o, axis=1, keepdims=True) + EPS)
-        gated = (o * inv * gg_ref[...].astype(F32) * (gz * jax.nn.sigmoid(gz))).astype(BF16)
-        gated_o[...] = gated
-        for j in range(4):
-            pa[t, j] = dot_nn(gated, wout[:, j * BLOCK : (j + 1) * BLOCK]).astype(BF16)
-        pair(pa, ma, asem, t, 1).start()
-        pair(pa, ma, asem, t, 0).start()
-
-    @pl.when((i >= 7) & (i - 7 <= last))
-    def _():
-        t = i - 7
-        for which in range(2):
-            pair(pp, mp, psem, t, which).wait_recv()
-            pair(pg, mg, gsem, t, which).wait_recv()
-        psend_o[...] = (pp[t, cross].astype(F32) + mp[t, 1].astype(F32)).astype(BF16)
-        pown_o[...] = pp[t, me].astype(F32) + mp[t, 0].astype(F32)
-        gsend_o[...] = (pg[t, cross].astype(F32) + mg[t, 1].astype(F32)).astype(BF16)
-        gown_o[...] = pg[t, me].astype(F32) + mg[t, 0].astype(F32)
 
     @pl.when((i >= 6) & (i - 6 <= last))
     def _():
@@ -464,6 +424,74 @@
         acc[hidden : 2 * hidden, :] += dot_tn(gfu, nf)
         acc[2 * hidden : 3 * hidden, :] += dot_tn(act, cg)
 
+    @pl.when((i >= 5) & (i - 5 <= last))
+    def _():
+        t = i - 5
+        own_cross(t).wait_recv()
+        onward(t).start()
+
+    @pl.when((i >= 3) & (i - 3 <= last))
+    def _():
+        t = i - 3
+        over(t).wait_recv()
+        rows = pl.ds(pl.multiple_of(t * TILE, TILE), TILE)
+        h = x_ref[rows, :].astype(F32) + (own[lax.rem(t, 4)] + rc[t].astype(F32))
+        h_o[...] = h
+        hg[t, me] = h.astype(BF16)
+        own_cross(t).start()
+        own_mate(t).start()
+
+    @pl.when((i >= 1) & (i - 1 <= last))
+    def _():
+        t = i - 1
+        pair(pa, ma, asem, t, 0).wait_recv()
+        pair(pa, ma, asem, t, 1).wait_recv()
+        sc[t] = (pa[t, cross].astype(F32) + ma[t, 1].astype(F32)).astype(BF16)
+        over(t).start()
+        own[lax.rem(t, 4)] = pa[t, me].astype(F32) + ma[t, 0].astype(F32)
+
+    @pl.when(i <= last)
+    def _():
+        t = i
+        for c in range(PER):
+            rows = slice(c * SPAN, (c + 1) * SPAN)
+            scaled = (keep_ref[t, c : c + 1, :] * e_ref[0, c : c + 1, :]) * state[...]
+            low = scaled.astype(BF16)
+            ws_o[c] = low
+            state[...] = scaled + u_ref[c]
+            oo_o[rows, :] = o_ref[rows, 256:512] + dot_nt(f_ref[rows, :].astype(BF16), low)
+        o = oo_o[...]
+        gz = o_ref[:, 0:256]
+        inv = lax.rsqrt(jnp.mean(o * o, axis=1, keepdims=True) + EPS)
+        gated = (o * inv * gg_ref[...].astype(F32) * (gz * jax.nn.sigmoid(gz))).astype(BF16)
+        gated_o[...] = gated
+        for j in range(4):
+            pa[t, j] = dot_nn(gated, wout[:, j * BLOCK : (j + 1) * BLOCK]).astype(BF16)
+        pair(pa, ma, asem, t, 1).start()
+        pair(pa, ma, asem, t, 0).start()
+
+    @pl.when((i >= 7) & (i - 7 <= last))
+    def _():
+        t = i - 7
+        for which in range(2):
+            pair(pp, mp, psem, t, which).wait_recv()
+            pair(pg, mg, gsem, t, which).wait_recv()
+        psend_o[...] = (pp[t, cross].astype(F32) + mp[t, 1].astype(F32)).astype(BF16)
+        pown_o[...] = pp[t, me].astype(F32) + mp[t, 0].astype(F32)
+        gs = (pg[t, cross].astype(F32) + mg[t, 1].astype(F32)).astype(BF16)
+        gsend_o[...] = gs
+
+        @pl.when(t < some)
+        def _():
+            gxs[t] = gs
+
+        gown_o[...] = pg[t, me].astype(F32) + mg[t, 0].astype(F32)
+
+    @pl.when(i == some + 6)
+    def _():
+        for t in range(some):
+            early(t).start()
+
     @pl.when(i == last + 6)
     def _():
         for n, other in enumerate((mate, cross, far)):
@@ -480,6 +508,9 @@
         lax.fori_loop(0, used, unit, 0)
         for n, other in enumerate((mate, cross, far)):
             stats(n, other).wait()
+        for t in range(some):
+            early(t).wait()
+            gx_o[t * TILE : (t + 1) * TILE, :] = gxr[t]
         stat_o[...] = (st_s[...] + st_r[0]) + (st_r[1] + st_r[2])
 
         def out(t, carry):
@@ -501,9 +532,10 @@
     tiles = rows // TILE
     hidden, width = wfg.shape
     units = 3 * hidden // 16
-    assert tiles <= 8 and hidden % 16 == 0
+    some = tiles - 3
+    assert 3 < tiles <= 8 and hidden % 16 == 0
     ts = functools.partial(tile_spec, tiles)
-    ins = (x, keep, inc, gg, gain, wout, wfg, wfu, wfd)
+    ins = (x, keep, inc, gg, gain, wout)
     outs = [
         ((rows, BLOCK), BF16, ts((TILE, BLOCK), 0)),
         ((rows, HV), F32, ts((TILE, HV), 0)),
@@ -516,6 +548,7 @@
         ((rows, BLOCK), F32, ts((TILE, BLOCK), 7)),
         ((8, TILE), F32, whole((8, TILE))),
         ((units, 16, width), BF16, whole((units, 16, width))),
+        ((some * TILE, BLOCK), BF16, whole((some * TILE, BLOCK))),
     ]
     tiled = lambda n: pltpu.VMEM((tiles, n, TILE, BLOCK), BF16)
     return pl.pallas_call(
@@ -523,6 +556,7 @@
         grid=(tiles + 7,),
         out_shape=[jax.ShapeDtypeStruct(s, d) for s, d, _ in outs],
         in_specs=[whole(a.shape) for a in ins]
+        + [pl.BlockSpec(memory_space=pl.ANY)] * 3
         + [
             ts((TILE, 128), 0), ts((TILE, 512), 0), ts((PER, HV, HK), 0), ts((1, 8, 128), 0),
             ts((TILE, MODEL_WIDTH), 6),
@@ -537,24 +571,33 @@
             tiled(4),
             pltpu.VMEM((TILE, MODEL_WIDTH), BF16),
             pltpu.VMEM((3 * hidden, width), F32),
+            pltpu.VMEM((hidden, width), BF16),
+            pltpu.VMEM((hidden, width), BF16),
+            pltpu.VMEM((hidden, width), BF16),
             pltpu.VMEM((8, TILE), F32),
             pltpu.VMEM((3, 8, TILE), F32),
+            pltpu.VMEM((some, TILE, BLOCK), BF16),
+            pltpu.VMEM((some, TILE, BLOCK), BF16),
             pltpu.SemaphoreType.DMA((4, tiles)),
             pltpu.SemaphoreType.DMA((4, tiles)),
             pltpu.SemaphoreType.DMA((4, tiles)),
             pltpu.SemaphoreType.DMA((2, tiles)),
             pltpu.SemaphoreType.DMA((6, tiles)),
             pltpu.SemaphoreType.DMA((2, 3)),
+            pltpu.SemaphoreType.DMA((3,)),
+            pltpu.SemaphoreType.DMA((2, some)),
         ],
         compiler_params=pltpu.CompilerParams(
             collective_id=2, has_side_effects=True, vmem_limit_bytes=VMEM_LIMIT,
             dimension_semantics=("arbitrary",),
         ),
         name="ffn",
-    )(*ins, f, o, u, e, cg)
+    )(*ins, wfg, wfu, wfd, f, o, u, e, cg)
 
 
 LAGS = (2, 2, 2)
+CYCLE = 5
+WAIT = 0
 
 
 def levels(count):
@@ -582,8 +625,8 @@
     def slot(self, k):
         if not self.folds:
             return k
-        odd = lax.rem(lax.rem(k, 5), 2)
-        return (3 - odd) * lax.div(k, 5) + lax.div(lax.rem(k, 5), 2)
+        odd = lax.rem(lax.rem(k, CYCLE), 2)
+        return ((CYCLE + 1) // 2 - odd) * lax.div(k, CYCLE) + lax.div(lax.rem(k, CYCLE), 2)
 
     def where(self, k, level):
         place = lax.axis_index("seq")
@@ -771,7 +814,7 @@
                     body(k, kind)
 
                 continue
-            odd = lax.rem(lax.rem(jnp.maximum(k, 0), 5), 2) == 1
+            odd = lax.rem(lax.rem(jnp.maximum(k, 0), CYCLE), 2) == 1
 
             @pl.when(here & odd)
             def _(kind=kind, k=k):
@@ -819,7 +862,7 @@
             if not self.folds:
                 halving(k, kind)
                 return carry
-            odd = lax.rem(lax.rem(k, 5), 2) == 1
+            odd = lax.rem(lax.rem(k, CYCLE), 2) == 1
 
             @pl.when(odd)
             def _():
@@ -841,7 +884,7 @@
         even = 1
         half = 16
         if folds(count):
-            odd = sum(1 for k in range(parts) if k % 5 % 2 == 1)
+            odd = sum(1 for k in range(parts) if k % CYCLE % 2 == 1)
             even = parts - odd
             half = count // 2
         one = (1,) + unit if not folds(count) else (half,) + unit
@@ -855,13 +898,22 @@
 
 
 def plan(count, wide, tiles):
-    second = tiles + 3
+    second = tiles + 3 + WAIT
     a = wide // count
     b = a + 32 // count
     c = b + up_to(34 + wide % count, count) // count
     gap = max(0, second - a)
     late = max(gap, second + tiles - b, second + tiles + 3 - (c - 1))
     return (0, a, 0), (a, b, gap), (b, c, late)
+
+
+def last_step(count, segments):
+    latest = 0
+    for kind, (low, high, gap) in enumerate(segments):
+        for k in range(low, high):
+            stages = 2 * levels(count) - (1 if folds(count) and k % CYCLE % 2 == 0 else 0)
+            latest = max(latest, k + gap + stages * LAGS[kind])
+    return latest
 
 
 def finish_kernel(fg, fu, fd, first, second, tail, extra, dfg, dfu, dfd, dq, dk, dv, dg, dwo, dr, dup, dag, dffg, db, dgg):
@@ -931,7 +983,7 @@
 def back_kernel(
     tiles, count, segments,
     keep_ref, d_ref, stat_ref, gg_ref, again, fgain, wout, wq, wk, wv, wg, wr, rup,
-    wide_in, gsend, psend, x_ref, c_ref, gown, h1, invf, f1, gz_ref, oo_ref, gated, ws1, b1, e1,
+    wide_in, gsend, psend, x_ref, c_ref, gx, gown, h1, invf, f1, gz_ref, oo_ref, gated, ws1, b1, e1,
     na1, f2, b2, ws2, e2, na, h2, pown, inva,
     gt_o, lo_o, units_o,
     tri, rg, gh, gb, gzs, gw, gqd, gkd, gv, state, sbuf, rbuf,
@@ -942,7 +994,9 @@
     me, mate, cross, far = peers()
     place = lax.axis_index("seq")
     last = tiles - 1
-    second = tiles + 3
+    second = tiles + 3 + WAIT
+
+    some = tiles - 3
 
     def rows_of(t):
         return pl.ds(pl.multiple_of(t * TILE, TILE), TILE)
@@ -990,27 +1044,18 @@
     def late(k, start, n):
         return lot.at[pl.ds((k - segments[2][0]) * count + start, n)]
 
-    def some(k, start, n):
+    def place_of(k, start, n):
         return wide_o.at[pl.ds(k * count + start, n)]
 
-    wide_sum = Sum(count, (early, middle, late), some, segments, rest)
+    wide_sum = Sum(count, (early, middle, late), place_of, segments, rest)
 
     @pl.when(i == 0)
     def _():
         greet_head()
         greet_seq(count)
         pl.semaphore_wait(pltpu.get_barrier_semaphore(), 3 + count - 1)
-        for n in range(AHEAD):
+        for n in range(tiles - some):
             grads(last - n).start()
-        def weave(r, carry):
-            rows = pl.ds(pl.multiple_of(r * 16, 16), 16)
-            lot[r, :, 0:128] = wq[rows, :]
-            lot[r, :, 128:256] = wk[rows, :]
-            lot[r, :, 256:512] = wv[rows, :]
-            lot[r, :, 512:768] = wg[rows, :]
-            return carry
-
-        lax.fori_loop(0, MODEL_WIDTH // 16, weave, 0)
         r = lax.broadcasted_iota(jnp.int32, (TILE, TILE), 0)
         c = lax.broadcasted_iota(jnp.int32, (TILE, TILE), 1)
         tri[...] = jnp.where(((r >> 6) == (c >> 6)) & (r > c), 1.0, 0.0).astype(BF16)
@@ -1018,10 +1063,6 @@
         both[...] = jnp.zeros_like(both)
         joint[...] = jnp.zeros_like(joint)
         small[...] = jnp.zeros_like(small)
-
-    @pl.when(i + AHEAD <= last)
-    def _():
-        grads(last - i - AHEAD).start()
 
     def share(n, other):
         return to_head(joint, held.at[me], jsem.at[0, n], jsem.at[1, n], other)
@@ -1066,6 +1107,18 @@
 
     wide_sum.step(i)
 
+    @pl.when(i == 1)
+    def _():
+        def weave(r, carry):
+            rows = pl.ds(pl.multiple_of(r * 16, 16), 16)
+            lot[r, :, 0:128] = wq[rows, :]
+            lot[r, :, 128:256] = wk[rows, :]
+            lot[r, :, 256:512] = wv[rows, :]
+            lot[r, :, 512:768] = wg[rows, :]
+            return carry
+
+        lax.fori_loop(0, MODEL_WIDTH // 16, weave, 0)
+
     @pl.when((i >= 2) & (i - 2 <= last))
     def _():
         t = last - (i - 2)
@@ -1075,7 +1128,15 @@
     @pl.when(i <= last)
     def _():
         t = last - i
-        grads(t).wait_recv()
+
+        @pl.when(t >= some)
+        def _():
+            grads(t).wait_recv()
+
+        @pl.when(t < some)
+        def _():
+            rg[t] = gx[...]
+
         gnf = gown[...] + rg[t].astype(F32)
         inv = invf[...][:, 0:1]
         hn = h1[...].astype(BF16).astype(F32) * inv
@@ -1278,7 +1339,10 @@
         lax.fori_loop(0, place, sent, 0)
 
         def out(t, carry):
-            grads(t).wait_send()
+            @pl.when(t >= some)
+            def _():
+                grads(t).wait_send()
+
             feeds(t).wait_send()
             pair(t, 0).wait_send()
             pair(t, 1).wait_send()
@@ -1290,19 +1354,18 @@
         lax.fori_loop(0, tiles, out, 0)
 
 
-def back(fixed, wide, gsend, psend, x, cot, gown, h, invf, f, o, oo, gated, ws, b, e, na, pown, inva):
+def back(fixed, wide, gsend, psend, x, cot, gx, gown, h, invf, f, o, oo, gated, ws, b, e, na, pown, inva):
     rows = h.shape[0]
     tiles = rows // TILE
     count = lax.axis_size("seq")
-    second = tiles + 3
+    second = tiles + 3 + WAIT
     width = MODEL_WIDTH
     segments = plan(count, wide.shape[0], tiles)
     first = segments[0][1]
     parts = segments[2][1]
     units = parts * count
     feed = second + tiles + 4
-    stages = 2 * levels(count)
-    steps = max([feed + tiles] + [end + gap + stages * lag + 1 for (_, end, gap), lag in zip(segments, LAGS)])
+    steps = max(feed + tiles, last_step(count, segments) + 1)
     ts = functools.partial(tile_spec, tiles, back=True)
     outs = [
         ((rows, BLOCK), F32, ts((TILE, BLOCK), second + 3)),
@@ -1319,6 +1382,7 @@
         + [
             pl.BlockSpec(memory_space=pl.ANY), pl.BlockSpec(memory_space=pl.ANY), pl.BlockSpec(memory_space=pl.ANY),
             ts((TILE, BLOCK), second + 3), ts((TILE, BLOCK), 0),
+            pl.BlockSpec((TILE, BLOCK), lambda i: (jnp.clip(tiles - 1 - i, 0, tiles - 4), 0)),
             ts((TILE, BLOCK), 0), ts((TILE, BLOCK), 0), ts((TILE, 128), 0),
             ts((TILE, 256), 3), ts((TILE, 256), 3), ts((TILE, 256), 3), ts((TILE, 256), 3),
             ts((PER, HV, HK), 3), ts((TILE, 640), 3), ts((1, 8, 128), 3), ts((TILE, width), 3),
@@ -1366,7 +1430,7 @@
             dimension_semantics=("arbitrary",),
         ),
         name="back",
-    )(*fixed, wide, gsend, psend, x, cot, gown, h, invf, f, o, oo, gated, ws, b, e, na, f, b, ws, e, na, h, pown, inva)
+    )(*fixed, wide, gsend, psend, x, cot, gx, gown, h, invf, f, o, oo, gated, ws, b, e, na, f, b, ws, e, na, h, pown, inva)
 
 
 def shards(
@@ -1399,14 +1463,14 @@
         query_weight[0], key_weight[0], value_weight[0], gate_weight[0], jnp.swapaxes(rank_down[0], 0, 1), rank_up[0]
     )
     na, cg, inva, f, b, o, u, e, inc, dec = front(tokens, cotangent, keep, attn_gain, *weights, rank_bias)
-    gated, oo, ws, h, invf, gsend, gown, psend, pown, stat, wide = ffn(
+    gated, oo, ws, h, invf, gsend, gown, psend, pown, stat, wide, gx = ffn(
         tokens, keep, inc, group_gain, feed_gain, out_weight[0], jnp.swapaxes(feed_gate[0], 0, 1),
         jnp.swapaxes(feed_up[0], 0, 1), feed_down[0], f, o, u, e, cg,
     )
     fixed = (
         keep, dec, stat, group_gain, attn_gain, feed_gain, out_weight[0],
     ) + weights
-    grad_tokens, layer_out, units = back(fixed, wide, gsend, psend, tokens, cotangent, gown, h, invf, f, o, oo, gated, ws, b, e, na, pown, inva)
+    grad_tokens, layer_out, units = back(fixed, wide, gsend, psend, tokens, cotangent, gx, gown, h, invf, f, o, oo, gated, ws, b, e, na, pown, inva)
     dfg, dfu, dfd, dq, dk, dv, dg, dwo, dr, dup, dag, dffg, db, dgg = finish(
         units, feed_gate.shape[2], wide.shape[0], lax.axis_size("seq")
     )

time: 315 us -> 302 us (0.959)
  Pallas kernels: 309 us -> 297 us
    pallas_call x1, Pallas kernels: 168 us -> 157 us  [back(): pl.pallas_call(functools.partial(back_kernel, tiles, count, segments), gr...]
where the time goes in v5:
time: 302 us
  Pallas kernels  297 us (98%)
  local copies, waits for them, and re-layouts  4.06 us (1%)
    pallas_call x1, Pallas kernels, back(): pl.pallas_call(functools.partial(back_kernel, tiles, count, segments), gr...  157 us
    pallas_call x1, Pallas kernels, ffn(): pl.pallas_call(functools.partial(ffn_kernel, tiles), grid=(tiles + 7,), o...  73.3 us
    pallas_call x1, Pallas kernels, front(): pl.pallas_call(functools.partial(front_kernel, tiles, count), grid=(2 * t...  58.7 us
    pallas_call x1, Pallas kernels, finish(): pl.pallas_call(finish_kernel, grid=(steps,), out_shape=[jax.ShapeDtypeStr...  8.06 us

profile of v5, /device:TPU:0, one launch (start us, length us, event | category | flops | bytes accessed | tf_op | source)
XLA Modules:
  0.0 302.1 jit_solution(14800887896437971359)
XLA Ops:
  0.7 0.7 and_select_fusion
  1.3 0.1 compare_reduce_fusion
  1.4 0.1 sub.23
  1.5 0.7 broadcast_in_dim.40.keep_ref
  2.2 58.7 %front.1 = (bf16[2048,1024]{1,0:T(8,128)(2,1)}, bf16[2048,1024]{1,0:T(8,128)(2,1)}, f32[2048,128]{1,0:T(8,128)}, f32[2048,640]{1,0:T(8,128)}, bf16[2048,640]{1,0...) custom-call(bf16[2048,256]{1,0:T(8,128)(2,1)} %x_ref.5, ...), custom_call_target="tpu_custom_call" | custom-call | tf_op jit(solution)/shard_map/front/pallas_call | solution.py:289
  60.9 73.3 %ffn.1 = (bf16[2048,256]{1,0:T(8,128)(2,1)}, f32[2048,256]{1,0:T(8,128)}, bf16[32,256,128]{2,1,0:T(8,128)(2,1)}, f32[2048,256]{1,0:T(8,128)}, f32[2048,128]{1,0:...) custom-call(bf16[2048,256]{1,0:T(8,128)(2,1)} %x_ref.5, ...), custom_call_target="tpu_custom_call" | custom-call | tf_op jit(solution)/shard_map/ffn/pallas_call | solution.py:554
  134.2 156.5 %back.1 = (f32[2048,256]{1,0:T(8,128)}, bf16[2048,256]{1,0:T(8,128)(2,1)}, bf16[200,16,1024]{2,1,0:T(8,128)(2,1)}) custom-call(f32[8,8,128]{2,1,0:T(8,128)} %broadcast_in_dim.40.keep_ref, f32[8,128]{1,0:T(8,128)} %get-tuple-element.55.d_ref, f32[8,256]{1,0:T(8,128)} %get-tuple-element.62.stat_ref, bf16[1,256]{1,0:T(2,128)(2,1)} %gg_ref.3, ...), custom_call_target="tpu_custom_call" | custom-call | tf_op jit(solution)/shard_map/back/pallas_call | solution.py:1377
  290.8 0.0 copy-start.1
  290.8 8.1 %finish.1 = (f32[704,1024]{1,0:T(8,128)}, f32[704,1024]{1,0:T(8,128)}, f32[704,1024]{1,0:T(8,128)}, f32[1024,128]{1,0:T(8,128)}, f32[1024,128]{1,0:T(8,128)}, /*...) custom-call(bf16[200,16,1024]{2,1,0:T(8,128)(2,1)} %get-tuple-elemen, ...), custom_call_target="tpu_custom_call" | custom-call | tf_op jit(solution)/shard_map/finish/pallas_call | solution.py:965
  298.8 0.0 copy-start
  298.8 0.0 copy-done.1
  298.9 1.0 copy.35
  299.8 1.0 copy-done
  300.8 1.3 copy.36
  (3 shorter events, 0.0 us)
Async XLA Ops:
  290.8 8.1 %copy-start.1 = (bf16[2048,256]{1,0:T(8,128)(2,1)S(1)}, bf16[2048,256]{1,0:T(8,128)(2,1)}, u32[]{:S(2)}) copy-start(bf16[2048,256]{1,0:T(8,128)(2,1)} %get-tuple-element.110) | copy-start | bytes 3145732
  298.8 2.0 copy-start

commit v6 on v5

--- a/solution.py
+++ b/solution.py
@@ -597,7 +597,7 @@
 
 LAGS = (2, 2, 2)
 CYCLE = 5
-WAIT = 0
+WAIT = 2
 
 
 def levels(count):
@@ -916,7 +916,7 @@
     return latest
 
 
-def finish_kernel(fg, fu, fd, first, second, tail, extra, dfg, dfu, dfd, dq, dk, dv, dg, dwo, dr, dup, dag, dffg, db, dgg):
+def finish_kernel(fg, fu, fd, first, second, tail, extra, gt_in, lo_in, dfg, dfu, dfd, dq, dk, dv, dg, dwo, dr, dup, dag, dffg, db, dgg, gt, lo):
     for src, dst in ((fg, dfg), (fu, dfu), (fd, dfd)):
         dst[...] = src[...].reshape(dst.shape).astype(F32)
 
@@ -925,6 +925,8 @@
         tail_rows = extra.shape[0] * 16
         dfd[dfd.shape[0] - tail_rows :, :] = extra[...].reshape(tail_rows, -1).astype(F32)
 
+    gt[...] = gt_in[...]
+    lo[...] = lo_in[...]
     rows = first[...].reshape(-1, 512).astype(F32)
     dg[...] = rows[:, 0:256]
     dwo[...] = rows[:, 256:512].T
@@ -941,7 +943,7 @@
     dgg[...] = last[2:3, 128:384]
 
 
-def finish(units, hidden, wide, count):
+def finish(units, gt, lo, hidden, wide, count):
     first = wide // count * count
     rest = wide % count
     width = units.shape[2]
@@ -962,22 +964,25 @@
         ((256, MODEL_WIDTH), pl.BlockSpec((256, rows), lambda i: (0, i))),
         full(RANK, MODEL_WIDTH), full(RANK, 128), full(1, 256), full(1, 256), full(1, 128), full(1, 256),
     ]
+    same = pl.BlockSpec((gt.shape[0] // steps, gt.shape[1]), lambda i: (i, 0))
     return pl.pallas_call(
         finish_kernel,
         grid=(steps,),
-        out_shape=[jax.ShapeDtypeStruct(s, F32) for s, _ in outs],
+        out_shape=[jax.ShapeDtypeStruct(s, F32) for s, _ in outs]
+        + [jax.ShapeDtypeStruct(gt.shape, F32), jax.ShapeDtypeStruct(lo.shape, BF16)],
         in_specs=[
             wide_spec(0), wide_spec(1), wide_spec(2),
             half_spec(0), half_spec(32),
             pl.BlockSpec((pl.Element(2), pl.Element(16), pl.Element(width)), lambda i: (first + 64, 0, 0)),
             pl.BlockSpec((pl.Element(rest), pl.Element(16), pl.Element(width)), lambda i: (first + 66, 0, 0)),
+            same, same,
         ],
-        out_specs=[s for _, s in outs],
+        out_specs=[s for _, s in outs] + [same, same],
         compiler_params=pltpu.CompilerParams(
             vmem_limit_bytes=VMEM_LIMIT, dimension_semantics=("arbitrary",)
         ),
         name="finish",
-    )(units, units, units, units, units, units, units)
+    )(units, units, units, units, units, units, units, gt, lo)
 
 
 def back_kernel(
@@ -986,9 +991,9 @@
     wide_in, gsend, psend, x_ref, c_ref, gx, gown, h1, invf, f1, gz_ref, oo_ref, gated, ws1, b1, e1,
     na1, f2, b2, ws2, e2, na, h2, pown, inva,
     gt_o, lo_o, units_o,
-    tri, rg, gh, gb, gzs, gw, gqd, gkd, gv, state, sbuf, rbuf,
+    tri, rg, gh, gb, gzs, gw, gqd, gkd, gv, state, sbuf, tbuf, hbuf, xbuf, ybuf, rbuf,
     gcat, mn, sc, rc, own, st_s, st_r, both, joint, small, held, wide_o, few, lot,
-    gsem, psem, hsem, nsem, csem, tsem, esend, erecv, wsem, jsem, *rest,
+    gsem, psem, hsem, nsem, csem, tsem, esend, erecv, xsem, wsem, jsem, *rest,
 ):
     i = pl.program_id(0)
     me, mate, cross, far = peers()
@@ -1203,21 +1208,80 @@
             through = keep_ref[t, c : c + 1, :] * e1[0, c : c + 1, :]
             state[...] = through * (fresh + state[...])
 
+    length = count // 2
+    side = lax.rem(place, 2)
+    line = lax.div(place, 2)
+    twin = place + 1 - 2 * side
+    half_rows = HV // 2
+    mine = pl.ds(pl.multiple_of(side * half_rows, half_rows), half_rows)
+    other = pl.ds(pl.multiple_of((1 - side) * half_rows, half_rows), half_rows)
+
+    def to_twin():
+        return to_seq(sbuf, tbuf, xsem.at[0], xsem.at[1], twin)
+
+    def to_twin_half():
+        return to_seq(xbuf, ybuf, xsem.at[2], xsem.at[3], twin)
+
+    def to_line(p):
+        return to_seq(hbuf, rbuf.at[line], esend.at[p], erecv.at[line], 2 * p + side)
+
+    def from_line(p):
+        return to_seq(hbuf, rbuf.at[p], esend.at[p], erecv.at[p], 2 * p + side)
+
+    def two_terms(d):
+        hi = d.astype(BF16).astype(F32)
+        first_rows = lax.broadcasted_iota(jnp.int32, (16, HK), 0) < 8
+        hi = jnp.broadcast_to(hi, (16, HK))
+        return jnp.where(first_rows, hi, jnp.broadcast_to(d, (16, HK)) - hi).astype(BF16)
+
+    def decay_of(rows):
+        rows = rows.astype(F32)
+        return rows[0:1] + rows[8:9]
+
     @pl.when(i == last + 3)
     def _():
-        sbuf[...] = jnp.zeros_like(sbuf)
         sbuf[0:HV, :] = state[...].astype(BF16)
-        d = d_ref[...]
-        hi = d.astype(BF16).astype(F32)
-        first = lax.broadcasted_iota(jnp.int32, (16, 128), 0) < 8
-        both = jnp.where(first, jnp.concatenate([hi, hi], axis=0), jnp.concatenate([d - hi, d - hi], axis=0))
-        sbuf[HV : HV + 16, :] = both.astype(BF16)
+        sbuf[HV : HV + 16, :] = two_terms(d_ref[0:1, :])
+        to_twin().start()
+
+    @pl.when(i == last + 4)
+    def _():
+        to_twin().wait_recv()
+        d_mine = decay_of(sbuf[HV : HV + 16, :])
+        d_twin = decay_of(tbuf[HV : HV + 16, :])
+        s_mine = sbuf[mine, :].astype(F32)
+        s_twin = tbuf[mine, :].astype(F32)
+
+        @pl.when(side == 0)
+        def _():
+            hbuf[0:half_rows, :] = (s_mine + d_mine * s_twin).astype(BF16)
+
+        @pl.when(side == 1)
+        def _():
+            hbuf[0:half_rows, :] = (s_twin + d_twin * s_mine).astype(BF16)
+
+        hbuf[half_rows : half_rows + 16, :] = two_terms(d_mine * d_twin)
 
         def send(p, carry):
-            to_seq(sbuf, rbuf.at[place], esend.at[p], erecv.at[place], p).start()
+            to_line(p).start()
             return carry
 
-        lax.fori_loop(0, place, send, 0)
+        lax.fori_loop(0, line, send, 0)
+
+    @pl.when(i == last + 5)
+    def _():
+        state[mine, :] = jnp.zeros((half_rows, HK), F32)
+
+        def join(n, carry):
+            p = length - 1 - n
+            from_line(p).wait_recv()
+            d = decay_of(rbuf[p, half_rows : half_rows + 16, :])
+            state[mine, :] = rbuf[p, 0:half_rows, :].astype(F32) + d * state[mine, :]
+            return carry
+
+        lax.fori_loop(0, length - 1 - line, join, 0)
+        xbuf[...] = state[mine, :].astype(BF16)
+        to_twin_half().start()
 
     @pl.when(i == second)
     def _():
@@ -1228,17 +1292,12 @@
             return carry
 
         lax.fori_loop(0, tiles, free, 0)
-        state[...] = jnp.zeros_like(state)
-
-        def join(n, carry):
-            p = count - 1 - n
-            to_seq(sbuf, rbuf.at[p], esend.at[p], erecv.at[p], place).wait_recv()
-            got = rbuf[p].astype(F32)
-            d = got[HV : HV + 1] + got[HV + 8 : HV + 9]
-            state[...] = got[0:HV] + d * state[...]
-            return carry
-
-        lax.fori_loop(0, count - 1 - place, join, 0)
+        to_twin_half().wait_recv()
+        state[other, :] = ybuf[...].astype(F32)
+
+        @pl.when(side == 0)
+        def _():
+            state[...] = tbuf[0:HV, :].astype(F32) + decay_of(tbuf[HV : HV + 16, :]) * state[...]
 
     @pl.when((i >= second + 3) & (i - second - 3 <= last))
     def _():
@@ -1332,11 +1391,14 @@
         tail_copy.wait()
         head_copy.wait()
 
+        to_twin().wait_send()
+        to_twin_half().wait_send()
+
         def sent(p, carry):
-            to_seq(sbuf, rbuf.at[place], esend.at[p], erecv.at[place], p).wait_send()
+            to_line(p).wait_send()
             return carry
 
-        lax.fori_loop(0, place, sent, 0)
+        lax.fori_loop(0, line, sent, 0)
 
         def out(t, carry):
             @pl.when(t >= some)
@@ -1400,7 +1462,11 @@
             flat(HK, F32), flat(HK, F32), flat(HV, F32),
             pltpu.VMEM((HV, HK), F32),
             pltpu.VMEM((HV + 16, HK), BF16),
-            pltpu.VMEM((count, HV + 16, HK), BF16),
+            pltpu.VMEM((HV + 16, HK), BF16),
+            pltpu.VMEM((HV // 2 + 16, HK), BF16),
+            pltpu.VMEM((HV // 2, HK), BF16),
+            pltpu.VMEM((HV // 2, HK), BF16),
+            pltpu.VMEM((count // 2, HV // 2 + 16, HK), BF16),
             pltpu.VMEM((TILE, 768), BF16),
             tiled(2), flat(BLOCK, BF16), flat(BLOCK, BF16),
             pltpu.VMEM((3, TILE, BLOCK), F32),
@@ -1419,8 +1485,9 @@
             pltpu.SemaphoreType.DMA((4, tiles)),
             pltpu.SemaphoreType.DMA((2, tiles)),
             pltpu.SemaphoreType.DMA((2, 3, tiles)),
-            pltpu.SemaphoreType.DMA((count,)),
-            pltpu.SemaphoreType.DMA((count,)),
+            pltpu.SemaphoreType.DMA((count // 2,)),
+            pltpu.SemaphoreType.DMA((count // 2,)),
+            pltpu.SemaphoreType.DMA((4,)),
             pltpu.SemaphoreType.DMA((3,)),
             pltpu.SemaphoreType.DMA((2, 3)),
         ]
@@ -1471,8 +1538,8 @@
         keep, dec, stat, group_gain, attn_gain, feed_gain, out_weight[0],
     ) + weights
     grad_tokens, layer_out, units = back(fixed, wide, gsend, psend, tokens, cotangent, gx, gown, h, invf, f, o, oo, gated, ws, b, e, na, pown, inva)
-    dfg, dfu, dfd, dq, dk, dv, dg, dwo, dr, dup, dag, dffg, db, dgg = finish(
-        units, feed_gate.shape[2], wide.shape[0], lax.axis_size("seq")
+    dfg, dfu, dfd, dq, dk, dv, dg, dwo, dr, dup, dag, dffg, db, dgg, grad_tokens, layer_out = finish(
+        units, grad_tokens, layer_out, feed_gate.shape[2], wide.shape[0], lax.axis_size("seq")
     )
     dfg, dfu, dr = (jnp.swapaxes(a, 0, 1) for a in (dfg, dfu, dr))
     grads = (dag, dq[None], dk[None], dv[None], dg[None], dr[None], dup[None], db, dgg, dwo[None], dffg, dfg[None], dfu[None], dfd[None])

time: 302 us -> 296 us (0.980)
  local copies, waits for them, and re-layouts: 4.06 us -> 0.78 us
    pallas_call x1, Pallas kernels: 157 us -> 151 us  [back(): pl.pallas_call(functools.partial(back_kernel, tiles, count, segments), gr...]
    unnamed x6 -> x0, local copies, waits for them, and re-layouts: 3.27 us -> none
where the time goes in v6:
time: 296 us
  Pallas kernels  294 us (99%)
    pallas_call x1, Pallas kernels, back(): pl.pallas_call(functools.partial(back_kernel, tiles, count, segments), gr...  151 us
    pallas_call x1, Pallas kernels, ffn(): pl.pallas_call(functools.partial(ffn_kernel, tiles), grid=(tiles + 7,), o...  73.3 us
    pallas_call x1, Pallas kernels, front(): pl.pallas_call(functools.partial(front_kernel, tiles, count), grid=(2 * t...  58.7 us
    pallas_call x1, Pallas kernels, finish(): pl.pallas_call(finish_kernel, grid=(steps,), out_shape=[jax.ShapeDtypeStr...  10.1 us

profile of v6, /device:TPU:0, one launch (start us, length us, event | category | flops | bytes accessed | tf_op | source)
XLA Modules:
  0.0 296.1 jit_solution(5641804384073190112)
XLA Ops:
  0.7 0.7 and_select_fusion
  1.3 0.1 compare_reduce_fusion
  1.4 0.1 sub.23
  1.5 0.7 broadcast_in_dim.40.keep_ref
  2.2 58.7 %front.1 = (bf16[2048,1024]{1,0:T(8,128)(2,1)}, bf16[2048,1024]{1,0:T(8,128)(2,1)}, f32[2048,128]{1,0:T(8,128)}, f32[2048,640]{1,0:T(8,128)}, bf16[2048,640]{1,0...) custom-call(bf16[2048,256]{1,0:T(8,128)(2,1)} %x_ref.5, ...), custom_call_target="tpu_custom_call" | custom-call | tf_op jit(solution)/shard_map/front/pallas_call | solution.py:289
  61.0 73.3 %ffn.1 = (bf16[2048,256]{1,0:T(8,128)(2,1)}, f32[2048,256]{1,0:T(8,128)}, bf16[32,256,128]{2,1,0:T(8,128)(2,1)}, f32[2048,256]{1,0:T(8,128)}, f32[2048,128]{1,0:...) custom-call(bf16[2048,256]{1,0:T(8,128)(2,1)} %x_ref.5, ...), custom_call_target="tpu_custom_call" | custom-call | tf_op jit(solution)/shard_map/ffn/pallas_call | solution.py:554
  134.3 151.5 %back.1 = (f32[2048,256]{1,0:T(8,128)}, bf16[2048,256]{1,0:T(8,128)(2,1)}, bf16[200,16,1024]{2,1,0:T(8,128)(2,1)}) custom-call(f32[8,8,128]{2,1,0:T(8,128)} %broadcast_in_dim.40.keep_ref, f32[8,128]{1,0:T(8,128)} %get-tuple-element.57.d_ref, f32[8,256]{1,0:T(8,128)} %get-tuple-element.64.stat_ref, bf16[1,256]{1,0:T(2,128)(2,1)} %gg_ref.3, ...), custom_call_target="tpu_custom_call" | custom-call | tf_op jit(solution)/shard_map/back/pallas_call | solution.py:1439
  285.8 10.1 %finish.1 = (f32[704,1024]{1,0:T(8,128)}, f32[704,1024]{1,0:T(8,128)}, f32[704,1024]{1,0:T(8,128)}, f32[1024,128]{1,0:T(8,128)}, f32[1024,128]{1,0:T(8,128)}, /*...) custom-call(bf16[200,16,1024]{2,1,0:T(8,128)(2,1)} %get-tuple-elemen, ...), custom_call_target="tpu_custom_call" | custom-call | tf_op jit(solution)/shard_map/finish/pallas_call | solution.py:968
  (3 shorter events, 0.0 us)

commit v7 on v6

--- a/solution.py
+++ b/solution.py
@@ -101,13 +101,17 @@
     tiles, count,
     x_ref, c_ref, keep_ref, gain_ref, wq, wk, wv, wg, wr, rup, bias_ref,
     na_o, cg_o, inv_o, f_o, b_o, o_o, u_o, e_o, in_o, d_o,
-    grid_buf, wcat, tri, state, decay, sbuf, rbuf, sems, esend, erecv,
+    grid_buf, wcat, tri, state, decay, sbuf, rbuf, sems, esend, erecv, fsem,
 ):
     i = pl.program_id(0)
     me, mate, cross, far = peers()
     place = lax.axis_index("seq")
     total = 2 * tiles
 
+    def fetch(m, ref, n):
+        rows = pl.ds(pl.multiple_of(n * TILE, TILE), TILE)
+        return pltpu.make_async_copy(ref.at[rows], grid_buf.at[m, me], fsem.at[m])
+
     def own_mate(m):
         return to_head(grid_buf.at[m, me], grid_buf.at[m, me], sems.at[0, m], sems.at[1, m], mate)
 
@@ -119,18 +123,21 @@
 
     @pl.when(i == 0)
     def _():
+        def own(m, carry):
+            fetch(m, x_ref, m).start()
+            return carry
+
+        def own_too(m, carry):
+            fetch(m + tiles, c_ref, m).start()
+            return carry
+
+        lax.fori_loop(0, tiles, own, 0)
+        lax.fori_loop(0, tiles, own_too, 0)
         greet_head()
         greet_seq(count)
-
-        def own(m, carry):
-            rows = pl.ds(pl.multiple_of(m * TILE, TILE), TILE)
-            grid_buf[m, me] = x_ref[rows, :]
-            grid_buf[m + tiles, me] = c_ref[rows, :]
-            return carry
-
-        lax.fori_loop(0, tiles, own, 0)
         pl.semaphore_wait(pltpu.get_barrier_semaphore(), 3 + count - 1)
         for m in range(AHEAD):
+            fetch(m, x_ref, m).wait()
             own_cross(m).start()
             own_mate(m).start()
         wcat[:, 0:128] = wq[...]
@@ -150,6 +157,7 @@
 
     @pl.when(i + AHEAD < total)
     def _():
+        fetch(i + AHEAD, x_ref, 0).wait()
         own_cross(i + AHEAD).start()
         own_mate(i + AHEAD).start()
 
@@ -290,7 +298,7 @@
         functools.partial(front_kernel, tiles, count),
         grid=(2 * tiles + 1,),
         out_shape=[jax.ShapeDtypeStruct(s, d) for s, d, _ in outs],
-        in_specs=[whole(a.shape) for a in ins],
+        in_specs=[pl.BlockSpec(memory_space=pl.ANY)] * 2 + [whole(a.shape) for a in ins[2:]],
         out_specs=[s for _, _, s in outs],
         scratch_shapes=[
             pltpu.VMEM((2 * tiles, 4, TILE, BLOCK), BF16),
@@ -303,6 +311,7 @@
             pltpu.SemaphoreType.DMA((6, 2 * tiles)),
             pltpu.SemaphoreType.DMA((count,)),
             pltpu.SemaphoreType.DMA((count,)),
+            pltpu.SemaphoreType.DMA((2 * tiles,)),
         ],
         compiler_params=pltpu.CompilerParams(
             collective_id=1, has_side_effects=True, vmem_limit_bytes=VMEM_LIMIT,
@@ -1522,10 +1531,11 @@
     rows = tokens.shape[0]
     tiles = rows // TILE
     spans = rows // SPAN
-    span_ids = lax.axis_index("seq") * spans + jnp.arange(spans, dtype=jnp.int32)
-    resets = jnp.any((row_starts // SPAN)[None, :] == span_ids[:, None], axis=1).astype(F32)
-    keep = jnp.pad((1.0 - resets).reshape(tiles, PER, 1), ((0, 0), (0, 8 - PER), (0, 0)))
-    keep = jnp.broadcast_to(keep, (tiles, 8, 128))
+    shape = (tiles, 8, 128)
+    span = lax.axis_index("seq") * spans + PER * lax.broadcasted_iota(jnp.int32, shape, 0)
+    span = span + lax.broadcasted_iota(jnp.int32, shape, 1)
+    hits = (row_starts // SPAN)[:, None, None, None] == span[None]
+    keep = 1.0 - jnp.any(hits, axis=0).astype(F32)
     weights = (
         query_weight[0], key_weight[0], value_weight[0], gate_weight[0], jnp.swapaxes(rank_down[0], 0, 1), rank_up[0]
     )

time: 296 us -> 296 us (level)
  no operation moved by 1% of the time
where the time goes in v7:
time: 296 us
  Pallas kernels  293 us (99%)
    pallas_call x1, Pallas kernels, back(): pl.pallas_call(functools.partial(back_kernel, tiles, count, segments), gr...  151 us
    pallas_call x1, Pallas kernels, ffn(): pl.pallas_call(functools.partial(ffn_kernel, tiles), grid=(tiles + 7,), o...  73.3 us
    pallas_call x1, Pallas kernels, front(): pl.pallas_call(functools.partial(front_kernel, tiles, count), grid=(2 * t...  58.3 us
    pallas_call x1, Pallas kernels, finish(): pl.pallas_call(finish_kernel, grid=(steps,), out_shape=[jax.ShapeDtypeStr...  10.1 us

profile of v7, /device:TPU:0, one launch (start us, length us, event | category | flops | bytes accessed | tf_op | source)
XLA Modules:
  0.0 295.6 jit_solution(5378165301366510467)
XLA Ops:
  0.7 0.7 and_select_fusion
  1.3 0.1 iota_add_fusion
  1.4 0.1 compare_reduce_fusion
  1.5 0.6 convert_subtract_fusion.keep_ref
  2.1 58.3 %front.1 = (bf16[2048,1024]{1,0:T(8,128)(2,1)}, bf16[2048,1024]{1,0:T(8,128)(2,1)}, f32[2048,128]{1,0:T(8,128)}, f32[2048,640]{1,0:T(8,128)}, bf16[2048,640]{1,0...) custom-call(bf16[2048,256]{1,0:T(8,128)(2,1)} %x_ref.5, ...), custom_call_target="tpu_custom_call" | custom-call | tf_op jit(solution)/shard_map/front/pallas_call | solution.py:297
  60.4 73.3 %ffn.1 = (bf16[2048,256]{1,0:T(8,128)(2,1)}, f32[2048,256]{1,0:T(8,128)}, bf16[32,256,128]{2,1,0:T(8,128)(2,1)}, f32[2048,256]{1,0:T(8,128)}, f32[2048,128]{1,0:...) custom-call(bf16[2048,256]{1,0:T(8,128)(2,1)} %x_ref.5, ...), custom_call_target="tpu_custom_call" | custom-call | tf_op jit(solution)/shard_map/ffn/pallas_call | solution.py:563
  133.8 151.5 %back.1 = (f32[2048,256]{1,0:T(8,128)}, bf16[2048,256]{1,0:T(8,128)(2,1)}, bf16[200,16,1024]{2,1,0:T(8,128)(2,1)}) custom-call(f32[8,8,128]{2,1,0:T(8,128)} %convert_subtract_fusion.keep_ref, f32[8,128]{1,0:T(8,128)} %get-tuple-element.57.d_ref, f32[8,256]{1,0:T(8,128)} %get-tuple-element.64.stat_ref, bf16[1,256]{1,0:T(2,128)(2,1)} %gg_ref.3, ...), custom_call_target="tpu_custom_call" | custom-call | tf_op jit(solution)/shard_map/back/pallas_call | solution.py:1448
  285.3 10.1 %finish.1 = (f32[704,1024]{1,0:T(8,128)}, f32[704,1024]{1,0:T(8,128)}, f32[704,1024]{1,0:T(8,128)}, f32[1024,128]{1,0:T(8,128)}, f32[1024,128]{1,0:T(8,128)}, /*...) custom-call(bf16[200,16,1024]{2,1,0:T(8,128)(2,1)} %get-tuple-elemen, ...), custom_call_target="tpu_custom_call" | custom-call | tf_op jit(solution)/shard_map/finish/pallas_call | solution.py:977
  (1 shorter events, 0.0 us)
